TPU v7x, 32 devices: a whole 2x2x4 slice. The times are simulated.
32 devices in a mesh: dp: 4 (over y, x), fsdp: 8 (over z, core).
Axes of the slice: x: 2, y: 2, z: 4, core: 2. Of those that a mesh axis runs over, the one named last changes fastest.
Arguments:
- tokens: bfloat16 [2, 8192, 1024], P(None, ('dp', 'fsdp')), may hold values from -6 to 6
- lengths: int32 [2, 32, 4], P(None, ('dp', 'fsdp')), may hold values from 0 to 256, as said below
- mix_weight: bfloat16 [1024, 3072], P(('dp', 'fsdp')), may hold values from -0.1875 to 0.1875
- out_weight: bfloat16 [1024, 1024], P(('dp', 'fsdp')), may hold values from -0.5 to 0.5
- up_weight: bfloat16 [1024, 4096], P(('dp', 'fsdp')), may hold values from -0.1875 to 0.1875
- down_weight: bfloat16 [4096, 1024], P(('dp', 'fsdp')), may hold values from -0.09375 to 0.09375
- attn_gain: bfloat16 [1024], P(('dp', 'fsdp')), may hold values from 0.099609375 to 1.8984375
- attn_bias: bfloat16 [1024], P(('dp', 'fsdp')), may hold values from -3 to 3
- feed_gain: bfloat16 [1024], P(('dp', 'fsdp')), may hold values from 0.099609375 to 1.8984375
- feed_bias: bfloat16 [1024], P(('dp', 'fsdp')), may hold values from -3 to 3
- feature_freq: float32 [64, 64], replicated, may hold values from -4 to 4
- feature_scale: float32 [64], replicated, may hold values from 0.5 to 2
- cotangent: bfloat16 [2, 8192, 1024], P(None, ('dp', 'fsdp')), may hold values from -6 to 6
Outputs:
- out: bfloat16 [2, 8192, 1024], P(None, ('dp', 'fsdp'))
- grad_tokens: float32 [2, 8192, 1024], P(None, ('dp', 'fsdp'))
- grad_mix: float32 [1024, 3072], P(('dp', 'fsdp'))
- grad_out: float32 [1024, 1024], P(('dp', 'fsdp'))
- grad_up: float32 [1024, 4096], P(('dp', 'fsdp'))
- grad_down: float32 [4096, 1024], P(('dp', 'fsdp'))
- grad_attn_gain: float32 [1024], P(('dp', 'fsdp'))
- grad_attn_bias: float32 [1024], P(('dp', 'fsdp'))
- grad_feed_gain: float32 [1024], P(('dp', 'fsdp'))
- grad_feed_bias: float32 [1024], P(('dp', 'fsdp'))
Inputs may be any that keep to these rules, and one draw needn't show every extreme that they name: A slot's lengths are those of its packed sequences in order, 0 for unused places; they sum to at least 192 and at most 256, the rest of the slot being padding; the first slot of each micro-batch holds one sequence of 256 tokens.
All inputs are finite; a program needn't handle non-finite values.
Results may differ from a plain program's by a relative error of at most 0.012.
The roundings to bfloat16 on the way count: a program that leaves them out, or rounds other values in their place, can miss the bound.
Values may be sent and summed in bfloat16 or wider, within the bound.
A program may use at most 256 MiB of HBM per device.

v0:
```python
from functools import partial
import math

import jax
import jax.numpy as jnp
from jax import lax
from jax.sharding import PartitionSpec as P

D = 1024
HEAD = 64
ROT = 16


epsilon = 1e-05
exact_precision = lax.Precision.HIGHEST


def dct_matrix(width):
    order = jnp.arange(width, dtype=jnp.float32)[:, None]
    sample = jnp.arange(width, dtype=jnp.float32)[None, :]
    factor = jnp.where(order == 0, jnp.sqrt(1.0 / width), jnp.sqrt(2.0 / width))
    return factor * jnp.cos(math.pi * (2.0 * sample + 1.0) * order / (2.0 * width))


def feature_table(feature_freq):
    table = jnp.dot(dct_matrix(HEAD).T, feature_freq.T, precision=exact_precision) / math.sqrt(HEAD)
    return table.astype(jnp.bfloat16)


def slot_layout(span_table, slot_len):
    seg_ends = jnp.cumsum(span_table, axis=-1)
    seg_starts = seg_ends - span_table
    places = jnp.arange(slot_len, dtype=jnp.int32)
    segment = jnp.sum((places[:, None] >= seg_ends[..., None, :]).astype(jnp.int32), axis=-1)
    numbers = jnp.arange(span_table.shape[-1], dtype=jnp.int32)
    matched = segment[..., None] == numbers
    begin_at = jnp.sum(jnp.where(matched, seg_starts[..., None, :], 0), axis=-1)
    begin_at = begin_at + jnp.where(segment == span_table.shape[-1], seg_ends[..., -1:], 0)
    position = (places - begin_at).astype(jnp.float32)
    valid = (segment < span_table.shape[-1]).astype(jnp.float32)
    return (segment, position, valid)


def rotate(raw_heads, position):
    half_rot = ROT // 2
    inverse = 10000.0 ** (-2.0 * jnp.arange(half_rot, dtype=jnp.float32) / ROT)
    angle = position[..., None] * inverse
    cosine_wave = jnp.cos(angle)[..., None, :]
    sine = jnp.sin(angle)[..., None, :]
    first = raw_heads[..., :half_rot]
    second = raw_heads[..., half_rot:ROT]
    return jnp.concatenate(
        [
            first * cosine_wave - second * sine,
            second * cosine_wave + first * sine,
            raw_heads[..., ROT:],
        ],
        axis=-1,
    )


def feature_map(raw_heads, position, table, feature_scale):
    rotated_rows = rotate(raw_heads, position).astype(jnp.bfloat16)
    pre = jnp.einsum("shd,df->shf", rotated_rows, table, preferred_element_type=jnp.float32)
    return feature_scale * jnp.exp(pre)


def feature_back(raw_heads, grad_phi, position, table, feature_scale):
    phi = feature_map(raw_heads, position, table, feature_scale)
    grad_pre = (grad_phi * phi).astype(jnp.bfloat16)
    grad_turned = jnp.einsum("shf,df->shd", grad_pre, table, preferred_element_type=jnp.float32)
    _, turn_pull = jax.vjp(lambda values: rotate(values, position), raw_heads)
    return turn_pull(grad_turned)[0]


def norm_apply(inputs, gain, shift):
    center = inputs - jnp.mean(inputs, axis=-1, keepdims=True)
    spread = jnp.mean(center * center, axis=-1, keepdims=True)
    return center * lax.rsqrt(spread + epsilon) * gain + shift


def head_major(values):
    return jnp.swapaxes(values, 0, 1)


def attend_head(allowed, pieces):
    mapped_query, mapped_key, value_rows = pieces
    score_matrix = jnp.einsum(
        "qf,kf->qk", mapped_query, mapped_key, preferred_element_type=jnp.float32
    )
    score_matrix = jnp.where(allowed, score_matrix, 0.0)
    totals = jnp.sum(score_matrix, axis=1)
    numerator = jnp.dot(
        score_matrix.astype(jnp.bfloat16), value_rows, preferred_element_type=jnp.float32
    )
    return numerator / totals[:, None]


def attend_back(allowed, pieces):
    mapped_query, mapped_key, value_rows, grad_heads = pieces
    score_matrix = jnp.einsum(
        "qf,kf->qk", mapped_query, mapped_key, preferred_element_type=jnp.float32
    )
    score_matrix = jnp.where(allowed, score_matrix, 0.0)
    totals = jnp.sum(score_matrix, axis=1)
    scores_low = score_matrix.astype(jnp.bfloat16)
    numerator = jnp.dot(scores_low, value_rows, preferred_element_type=jnp.float32)
    grad_numer = (grad_heads / totals[:, None]).astype(jnp.bfloat16)
    grad_totals = -jnp.sum(grad_heads * numerator, axis=1) / (totals * totals)
    grad_scores = jnp.einsum(
        "qd,kd->qk", grad_numer, value_rows, preferred_element_type=jnp.float32
    )
    grad_scores = jnp.where(allowed, grad_scores + grad_totals[:, None], 0.0).astype(jnp.bfloat16)
    grad_query = jnp.dot(grad_scores, mapped_key, preferred_element_type=jnp.float32)
    grad_key = jnp.einsum(
        "qk,qf->kf", grad_scores, mapped_query, preferred_element_type=jnp.float32
    )
    grad_value = jnp.einsum("qk,qd->kd", scores_low, grad_numer, preferred_element_type=jnp.float32)
    return (grad_query, grad_key, grad_value)


def fetch_attention(shards):
    return (
        lax.all_gather(shards[0], ("dp", "fsdp"), axis=0, tiled=True),
        lax.all_gather(shards[1], ("dp", "fsdp"), axis=0, tiled=True),
        lax.all_gather(shards[2], ("dp", "fsdp"), axis=0, tiled=True),
        lax.all_gather(shards[3], ("dp", "fsdp"), axis=0, tiled=True),
    )


def fetch_feed(shards):
    return (
        lax.all_gather(shards[0], ("dp", "fsdp"), axis=0, tiled=True),
        lax.all_gather(shards[1], ("dp", "fsdp"), axis=0, tiled=True),
        lax.all_gather(shards[2], ("dp", "fsdp"), axis=0, tiled=True),
        lax.all_gather(shards[3], ("dp", "fsdp"), axis=0, tiled=True),
    )


def reduce_attention(grads):
    return (
        lax.psum_scatter(grads[0], ("dp", "fsdp"), scatter_dimension=0, tiled=True),
        lax.psum_scatter(grads[1], ("dp", "fsdp"), scatter_dimension=0, tiled=True),
        lax.psum_scatter(grads[2], ("dp", "fsdp"), scatter_dimension=0, tiled=True),
        lax.psum_scatter(grads[3], ("dp", "fsdp"), scatter_dimension=0, tiled=True),
    )


def reduce_feed(grads):
    return (
        lax.psum_scatter(grads[0], ("dp", "fsdp"), scatter_dimension=0, tiled=True),
        lax.psum_scatter(grads[1], ("dp", "fsdp"), scatter_dimension=0, tiled=True),
        lax.psum_scatter(grads[2], ("dp", "fsdp"), scatter_dimension=0, tiled=True),
        lax.psum_scatter(grads[3], ("dp", "fsdp"), scatter_dimension=0, tiled=True),
    )


def add_tuples(running, update):
    if running is None:
        return tuple(update)
    return tuple(jax.tree.map(jnp.add, tuple(running), tuple(update)))


def per_device(
    tokens,
    lengths,
    mix_weight,
    out_weight,
    up_weight,
    down_weight,
    attn_gain,
    attn_bias,
    feed_gain,
    feed_bias,
    feature_freq,
    feature_scale,
    cotangent,
):
    table = feature_table(feature_freq)
    slot_len = tokens.shape[1]
    head_count = D // HEAD
    attn_shards = (mix_weight, out_weight, attn_gain, attn_bias)
    feed_shards = (up_weight, down_weight, feed_gain, feed_bias)
    places = jnp.arange(slot_len, dtype=jnp.int32)
    output_rows = []
    grad_inputs = []
    attn_total = None
    feed_total = None
    for micro_index in range(tokens.shape[0]):
        attn_full = fetch_attention(attn_shards)
        feed_full = fetch_feed(feed_shards)
        mix_full, out_full, gain_one, bias_one = attn_full
        up_full, down_full, gain_two, bias_two = feed_full
        gain_attn = gain_one.astype(jnp.float32)
        shift_attn = bias_one.astype(jnp.float32)
        gain_feed = gain_two.astype(jnp.float32)
        shift_feed = bias_two.astype(jnp.float32)
        inputs = tokens[micro_index].astype(jnp.float32)
        segment, position, valid = slot_layout(lengths[micro_index, 0], slot_len)
        allowed = (segment[:, None] == segment[None, :]) & (places[None, :] <= places[:, None])
        normed_attn = norm_apply(inputs, gain_attn, shift_attn).astype(jnp.bfloat16)
        normed_feed = norm_apply(inputs, gain_feed, shift_feed).astype(jnp.bfloat16)
        mixed = jnp.dot(normed_attn, mix_full, preferred_element_type=jnp.float32)
        mixed = mixed.reshape(slot_len, 3, head_count, HEAD)
        query_raw = mixed[:, 0]
        key_raw = mixed[:, 1]
        value_rows = mixed[:, 2].astype(jnp.bfloat16)
        mapped_query = feature_map(query_raw, position, table, feature_scale).astype(jnp.bfloat16)
        mapped_key = feature_map(key_raw, position, table, feature_scale).astype(jnp.bfloat16)
        attended = lax.map(
            partial(attend_head, allowed),
            (head_major(mapped_query), head_major(mapped_key), head_major(value_rows)),
        )
        attended = head_major(attended).reshape(slot_len, D).astype(jnp.bfloat16)
        attn_rows = jnp.dot(attended, out_full, preferred_element_type=jnp.float32)
        hidden = jnp.dot(normed_feed, up_full, preferred_element_type=jnp.float32)
        active = jax.nn.gelu(hidden, approximate=False).astype(jnp.bfloat16)
        feed_rows = jnp.dot(active, down_full, preferred_element_type=jnp.float32)
        result = inputs + valid[:, None] * (attn_rows + feed_rows)
        output_rows.append(result.astype(jnp.bfloat16))
        attn_full = fetch_attention(attn_shards)
        feed_full = fetch_feed(feed_shards)
        mix_full, out_full, gain_one, bias_one = attn_full
        up_full, down_full, gain_two, bias_two = feed_full
        grad_rows = cotangent[micro_index]
        grad_branch = jnp.where(valid[:, None] > 0.0, grad_rows, jnp.zeros_like(grad_rows))
        grad_down = jnp.einsum("sf,sd->fd", active, grad_branch, preferred_element_type=jnp.float32)
        grad_out = jnp.einsum(
            "sd,se->de", attended, grad_branch, preferred_element_type=jnp.float32
        )
        grad_active = jnp.einsum(
            "sd,fd->sf", grad_branch, down_full, preferred_element_type=jnp.float32
        )
        _, gelu_pull = jax.vjp(partial(jax.nn.gelu, approximate=False), hidden)
        grad_hidden = gelu_pull(grad_active)[0].astype(jnp.bfloat16)
        grad_up = jnp.einsum(
            "sd,sf->df", normed_feed, grad_hidden, preferred_element_type=jnp.float32
        )
        grad_normed_feed = jnp.einsum(
            "sf,df->sd", grad_hidden, up_full, preferred_element_type=jnp.float32
        )
        grad_attended = jnp.einsum(
            "sd,ed->se", grad_branch, out_full, preferred_element_type=jnp.float32
        )
        grad_attended = grad_attended.reshape(slot_len, head_count, HEAD)
        grad_phi_q, grad_phi_k, grad_value = lax.map(
            partial(attend_back, allowed),
            (
                head_major(mapped_query),
                head_major(mapped_key),
                head_major(value_rows),
                head_major(grad_attended),
            ),
        )
        grad_query = feature_back(query_raw, head_major(grad_phi_q), position, table, feature_scale)
        grad_key = feature_back(key_raw, head_major(grad_phi_k), position, table, feature_scale)
        grad_mixed = jnp.stack([grad_query, grad_key, head_major(grad_value)], axis=1)
        grad_mixed = grad_mixed.reshape(slot_len, 3 * D).astype(jnp.bfloat16)
        grad_mix = jnp.einsum(
            "sd,se->de", normed_attn, grad_mixed, preferred_element_type=jnp.float32
        )
        grad_normed_attn = jnp.einsum(
            "se,de->sd", grad_mixed, mix_full, preferred_element_type=jnp.float32
        )
        _, attn_norm_pull = jax.vjp(norm_apply, inputs, gain_attn, shift_attn)
        grad_in_one, grad_gain_one, grad_bias_one = attn_norm_pull(grad_normed_attn)
        _, feed_norm_pull = jax.vjp(norm_apply, inputs, gain_feed, shift_feed)
        grad_in_two, grad_gain_two, grad_bias_two = feed_norm_pull(grad_normed_feed)
        grad_inputs.append(grad_rows.astype(jnp.float32) + grad_in_one + grad_in_two)
        attn_grads = (grad_mix, grad_out, grad_gain_one, grad_bias_one)
        feed_grads = (grad_up, grad_down, grad_gain_two, grad_bias_two)
        attn_grads = reduce_attention(attn_grads)
        feed_grads = reduce_feed(feed_grads)
        attn_total = add_tuples(attn_total, attn_grads)
        feed_total = add_tuples(feed_total, feed_grads)
    return (
        jnp.stack(output_rows),
        jnp.stack(grad_inputs),
        attn_total[0],
        attn_total[1],
        feed_total[0],
        feed_total[1],
        attn_total[2],
        attn_total[3],
        feed_total[2],
        feed_total[3],
    )


def solution(mesh):
    placed = (
        P(None, ("dp", "fsdp"), None),
        P(None, ("dp", "fsdp"), None),
        P(("dp", "fsdp"), None),
        P(("dp", "fsdp"), None),
        P(("dp", "fsdp"), None),
        P(("dp", "fsdp"), None),
        P(("dp", "fsdp")),
        P(("dp", "fsdp")),
        P(("dp", "fsdp")),
        P(("dp", "fsdp")),
        P(),
        P(),
        P(None, ("dp", "fsdp"), None),
    )
    return jax.shard_map(
        per_device,
        mesh=mesh,
        in_specs=placed,
        out_specs=(
            P(None, ("dp", "fsdp"), None),
            P(None, ("dp", "fsdp"), None),
            P(("dp", "fsdp"), None),
            P(("dp", "fsdp"), None),
            P(("dp", "fsdp"), None),
            P(("dp", "fsdp"), None),
            P(("dp", "fsdp")),
            P(("dp", "fsdp")),
            P(("dp", "fsdp")),
            P(("dp", "fsdp")),
        ),
        check_vma=False,
    )
```

profile of v0, /device:TPU:0, one launch (start us, length us, event | category | flops | bytes accessed | tf_op | source)
XLA Modules:
  0.0 1062.4 jit_solution(8287746859617565368)
XLA Ops:
  17.7 42.3 %all-reduce.21 = (bf16[1024]{0:T(1024)(128)(2,1)S(1)}, bf16[1024]{0:T(1024)(128)(2,1)S(1)}, bf16[1024]{0:T(1024)(128)(2,1)S(1)}, bf16[1024]{0:T(1024)(128)(2,1)S(1)}) all-reduce(bf16[1024]{0:T(1024)(128)(2,1)S(1)} %dynamic-update-slice.3, bf16[1024]{0:T(1024)(128)(2,1)S(1)} %dynamic-update-slice.2, ...), channel_id=1, replica_groups=mesh['dp'=4,'fsdp'=8] {'dp','fsdp'}, use_global_device_ids=true, to_apply=%add.15 | all-reduce | flops 4096 | bytes 16384
  61.9 8.7 all-gather.7.cloned.1.call-done
  70.7 3.6 convolution_bitcast_fusion.7
  74.2 1.8 convolution_bitcast_fusion.6
  76.1 65.8 %all-gather.5.cloned.1.call-done = bf16[1024,3072]{1,0:T(8,128)(2,1)} async-done(((bf16[32,3072]{1,0:T(8,128)(2,1)}), bf16[1024,3072]{1,0:T(8,128)(2,1)}) %all-gather.5.cloned.1.call-update) | async-done | bytes 6291472 | tf_op jit(solution)/shard_map/all_gather | solution.py:124
  141.9 8.6 copy.63
  150.5 5.2 fusion.198
  156.1 2.0 fusion.196
  167.5 2.3 copy.73
  177.3 34.7 %while.52 = (s32[]{:T(128)}, bf16[16,256,64]{1,2,0:T(8,128)(2,1)S(1)}, bf16[16,256,64]{2,1,0:T(8,128)(2,1)}, bf16[16,256,64]{2,1,0:T(8,128)(2,1)}, bf16[16,256,6...) while((s32[]{:T(128)}, bf16[16,256,64]{1,2,0:T(8,128)(2,1)S(1)}, ...), condition=%wide.region_7.8_spmd.clone, body=%wide.region_5.7_spmd.clone.sunk | while | flops 17186560 | bytes 530517 | solution.py:210
  214.8 34.8 %while.53 = (s32[]{:T(128)}, bf16[16,256,64]{1,2,0:T(8,128)(2,1)S(1)}, bf16[16,256,64]{2,1,0:T(8,128)(2,1)}, bf16[16,256,64]{2,1,0:T(8,128)(2,1)}, bf16[16,256,6...) while((s32[]{:T(128)}, bf16[16,256,64]{1,2,0:T(8,128)(2,1)S(1)}, ...), condition=%wide.region_15.16_spmd.clone, body=%wide.region_13.15_spmd.clone.sunk | while | flops 17186560 | bytes 530517 | solution.py:210
  249.6 2.0 fusion.203
  251.7 2.9 convolution_add_fusion.5
  255.7 122.2 %while.54 = (s32[]{:T(128)}, f32[16,256,64]{1,2,0:T(8,128)S(1)}, f32[16,256,64]{1,2,0:T(8,128)}, bf16[16,256,64]{1,2,0:T(8,128)(2,1)}, f32[16,256,64]{1,2,0:T(8,...) while((s32[]{:T(128)}, f32[16,256,64]{1,2,0:T(8,128)S(1)}, ...), condition=%wide.region_19.20_spmd.clone, body=%wide.region_16.19_spmd.clone.sunk | while | flops 51216640 | bytes 1591405 | solution.py:246
  380.3 122.3 %while.55 = (s32[]{:T(128)}, f32[16,256,64]{1,2,0:T(8,128)}, f32[16,256,64]{1,2,0:T(8,128)}, bf16[16,256,64]{1,2,0:T(8,128)(2,1)S(1)}, f32[16,256,64]{1,2,0:T(8,...) while((s32[]{:T(128)}, f32[16,256,64]{1,2,0:T(8,128)}, ...), condition=%wide.region_27.28_spmd.clone, body=%wide.region_24.27_spmd.clone.sunk | while | flops 51216640 | bytes 1591405 | solution.py:246
  392.3 1.7 fusion.395
  399.9 1.7 fusion.395
  407.6 1.7 fusion.395
  415.2 1.7 fusion.395
  422.8 1.7 fusion.395
  430.5 1.7 fusion.395
  438.1 1.7 fusion.395
  445.8 1.7 fusion.395
  453.4 1.7 fusion.395
  461.0 1.7 fusion.395
  468.7 1.7 fusion.395
  476.3 1.7 fusion.395
  491.6 1.7 fusion.395
  499.2 1.7 fusion.395
  508.4 2.1 fusion.206
  510.5 6.5 convolution_add_fusion.4
  517.1 16.3 %multiply_convert_fusion.1 = (bf16[256,4096]{1,0:T(8,128)(2,1)}, f32[256,4096]{1,0:T(8,128)}, f32[256,4096]{1,0:T(8,128)}) fusion(bf16[1024,4096]{1,0:T(8,128)(2,1)} %all-gather.9.cloned.1.call-done, f32[1024]{0:T(1024)S(1)} %convert_element_type.276, f32[1024]{0:T(1024)S(1)} %convert_element_type.275, f32[256]{0:T(256)S(1)} %fusion.225, ...), kind=kOutput, calls=%fused_computation.136 | convolution fusion | flops 2217213952 | bytes 19408896 | tf_op jit(solution)/shard_map/dot_general | solution.py:216
  533.5 12.0 %add_convert_fusion.1 = bf16[256,4096]{1,0:T(8,128)(2,1)S(1)} fusion(f32[256,4096]{1,0:T(8,128)} %get-tuple-element.443, f32[256,4096]{1,0:T(8,128)} %get-tuple-element.501, bf16[4096,1024]{1,0:T(8,128)(2,1)} %all-gather.11.cloned.1.call-done, pred[256]{0:T(512)(128)(4,1)S(1)} %get-tuple-element.492, bf16[2,256,1024]{2,1,0:T(8,128)(2,1)S(1)} %copy-done.12), kind=kOutput, calls=%fused_computation.122 | convolution fusion | flops 2162425856 | bytes 19399168 | tf_op jit(solution)/shard_map/sd,fd->sf/dot_general | solution.py:231
  545.5 11.1 %fusion.244 = f32[1024,4096]{1,0:T(8,128)} fusion(bf16[256,4096]{1,0:T(8,128)(2,1)S(1)} %add_convert_fusion.1, f32[1024]{0:T(1024)S(1)} %convert_element_type.276, f32[1024]{0:T(1024)S(1)} %convert_element_type.275, f32[256]{0:T(256)S(1)} %fusion.225, f32[256]{0:T(256)S(1)} %get-tuple-element.505, bf16[2,256,1024]{2,1,0:T(8,128)(2,1)S(1)} %copy-done.2), kind=kOutput, calls=%fused_computation.388 | convolution fusion | flops 2149056512 | bytes 19408896 | tf_op jit(solution)/shard_map/sd,sf->df/dot_general | solution.py:236
  556.6 16.3 %multiply_convert_fusion = (bf16[256,4096]{1,0:T(8,128)(2,1)}, f32[256,4096]{1,0:T(8,128)}, f32[256,4096]{1,0:T(8,128)}) fusion(bf16[1024,4096]{1,0:T(8,128)(2,1)S(1)} %copy-done.53, f32[256]{0:T(256)S(1)} %fusion.226, f32[256]{0:T(256)S(1)} %get-tuple-element.504, f32[1024]{0:T(1024)S(1)} %convert_element_type.276, f32[1024]{0:T(1024)S(1)} %convert_element_type.275, ...), kind=kOutput, calls=%fused_computation.123 | convolution fusion | flops 2217213952 | bytes 19408896 | tf_op jit(solution)/shard_map/dot_general | solution.py:216
  572.9 8.9 add_convert_fusion
  583.2 14.2 %convolution_add_fusion.3 = f32[1024,4096]{1,0:T(8,128)} fusion(f32[1024,4096]{1,0:T(8,128)} %fusion.244, bf16[256,4096]{1,0:T(8,128)(2,1)S(1)} %add_convert_fusion, f32[256]{0:T(256)S(1)} %fusion.226, f32[256]{0:T(256)S(1)} %get-tuple-element.504, f32[1024]{0:T(1024)S(1)} %convert_element_type.276, f32[1024]{0:T(1024)S(1)} %convert_element_type.275, ...), kind=kOutput, calls=%fused_computation.115 | convolution fusion | flops 2153250816 | bytes 36186112 | tf_op jit(solution)/shard_map/sd,sf->df/dot_general | solution.py:236
  597.7 4.0 fusion.208
  601.7 10.3 convolution_add_fusion.2
  612.0 5.5 fusion.264
  617.5 5.4 fusion.152
  623.1 2.6 fusion.265
  625.8 3.8 fusion.153
  630.7 40.1 %all-reduce.20 = (f32[1024]{0:T(1024)S(1)}, f32[1024]{0:T(1024)S(1)}, f32[1024]{0:T(1024)S(1)}, f32[1024]{0:T(1024)S(1)}) all-reduce(f32[1024]{0:T(1024)S(1)} %add.271, f32[1024]{0:T(1024)S(1)} %add.272, f32[1024]{0:T(1024)S(1)} %add.273, f32[1024]{0:T(1024)S(1)} %add.274), channel_id=14, replica_groups=mesh['dp'=4,'fsdp'=8] {'dp','fsdp'}, use_global_device_ids=true, to_apply=%region_41.42.clone | all-reduce | flops 4096 | bytes 32768
  673.1 6.6 fusion.263
  681.3 5.8 fusion.262
  692.2 175.8 %reduce-scatter.9.cloned.1.call-done = f32[32,4096]{1,0:T(8,128)} async-done(((f32[1024,4096]{1,0:T(8,128)}), f32[32,4096]{1,0:T(8,128)}) %reduce-scatter.9.cloned.1.call-update) | async-done | bytes 524304 | tf_op jit(solution)/shard_map/reduce_scatter | solution.py:151
  868.0 187.3 %reduce-scatter.11.cloned.1.call-done = f32[128,1024]{1,0:T(8,128)} async-done(((f32[4096,1024]{1,0:T(8,128)}), f32[128,1024]{1,0:T(8,128)}) %reduce-scatter.11.cloned.1.call-update) | async-done | bytes 524304 | tf_op jit(solution)/shard_map/reduce_scatter | solution.py:152
  (525 shorter events, 341.2 us)
Async XLA Ops:
  7.2 54.2 %copy-start = (f32[64,64]{1,0:T(8,128)S(1)}, f32[64,64]{1,0:T(8,128)}, u32[]{:S(2)}) copy-start(f32[64,64]{1,0:T(8,128)} %param.31) | copy-start | bytes 49156
  7.2 8.9 copy-start.2
  7.2 9.5 copy-start.54
  7.2 9.8 copy-start.55
  7.2 10.0 copy-start.56
  7.2 10.2 copy-start.57
  7.2 63.4 %copy-start.10 = (bf16[2,256,1024]{2,1,0:T(8,128)(2,1)S(1)}, bf16[2,256,1024]{2,1,0:T(8,128)(2,1)}, u32[]{:S(2)}) copy-start(bf16[2,256,1024]{2,1,0:T(8,128)(2,1)} %param.33) | copy-start | bytes 3145732
  7.3 63.4 %all-gather.7.cloned.1.call-start = ((), (), s32[]{:S(2)}) async-start(), calls=%async_computation.5 | async-start | bytes 2162688 | tf_op jit(solution)/shard_map/all_gather | solution.py:125
  8.0 133.9 %all-gather.5.cloned.1.call-start = ((), (), s32[]{:S(2)}) async-start(), calls=%async_computation.4 | async-start | bytes 6488064 | tf_op jit(solution)/shard_map/all_gather | solution.py:124
  8.7 508.4 %all-gather.9.cloned.1.call-start = ((), (), s32[]{:S(2)}) async-start(), calls=%async_computation.6 | async-start | bytes 8650752 | tf_op jit(solution)/shard_map/all_gather | solution.py:133
  9.5 524.0 %all-gather.11.cloned.1.call-start = ((), (), s32[]{:S(2)}) async-start(), calls=%async_computation.7 | async-start | bytes 8650752 | tf_op jit(solution)/shard_map/all_gather | solution.py:134
  10.1 682.1 %reduce-scatter.7.cloned.1.call-start = ((), (), s32[]{:S(2)}) async-start(), calls=%async_computation.9 | async-start | bytes 4325376 | tf_op jit(solution)/shard_map/reduce_scatter | solution.py:143
  13.1 61.2 %copy-start.3 = (bf16[16,256,64]{1,2,0:T(8,128)(2,1)}, bf16[16,256,64]{1,2,0:T(8,128)(2,1)S(1)}, u32[]{:S(2)}) copy-start(bf16[16,256,64]{1,2,0:T(8,128)(2,1)S(1)} %fusion.261) | copy-start | bytes 1572868
  16.7 59.4 %copy-start.49 = (f32[256]{0:T(256)}, f32[256]{0:T(256)S(1)}, u32[]{:S(2)}) copy-start(f32[256]{0:T(256)S(1)} %get-tuple-element.367) | copy-start | bytes 3076
  16.7 59.4 %copy-start.51 = (f32[256]{0:T(256)}, f32[256]{0:T(256)S(1)}, u32[]{:S(2)}) copy-start(f32[256]{0:T(256)S(1)} %get-tuple-element.366) | copy-start | bytes 3076
  70.7 3.6 copy-start.13
  150.5 5.5 copy-start.15
  156.1 4.0 copy-start.36
  156.1 4.8 copy-start.35
  158.9 4.5 copy-start.58
  172.2 5.1 copy-start.9
  177.3 37.4 %copy-start.4 = (bf16[16,256,64]{1,2,0:T(8,128)(2,1)S(1)}, bf16[16,256,64]{1,2,0:T(8,128)(2,1)}, u32[]{:S(2)}) copy-start(bf16[16,256,64]{1,2,0:T(8,128)(2,1)} %copy-done.3) | copy-start | bytes 1572868
  212.0 37.6 %copy-start.7 = (bf16[16,256,64]{1,2,0:T(8,128)(2,1)}, bf16[16,256,64]{1,2,0:T(8,128)(2,1)S(1)}, u32[]{:S(2)}) copy-start(bf16[16,256,64]{1,2,0:T(8,128)(2,1)S(1)} %get-tuple-element.172) | copy-start | bytes 1572868
  378.0 314.2 %reduce-scatter.5.cloned.1.call-start = ((), (), s32[]{:S(2)}) async-start(), calls=%async_computation.8 | async-start | bytes 12976128 | tf_op jit(solution)/shard_map/reduce_scatter | solution.py:142
  380.3 122.3 %copy-start.20 = (f32[256,16,64]{0,2,1:T(8,128)S(1)}, f32[256,16,64]{0,2,1:T(8,128)}, u32[]{:S(2)}) copy-start(f32[256,16,64]{0,2,1:T(8,128)} %copy-done.19) | copy-start | bytes 3145732
  517.0 351.0 %reduce-scatter.9.cloned.1.call-start = ((), (), s32[]{:S(2)}) async-start(), calls=%async_computation.10 | async-start | bytes 17301504 | tf_op jit(solution)/shard_map/reduce_scatter | solution.py:151
  517.1 16.4 %copy-start.12 = (bf16[2,256,1024]{2,1,0:T(8,128)(2,1)S(1)}, bf16[2,256,1024]{2,1,0:T(8,128)(2,1)}, u32[]{:S(2)}) copy-start(bf16[2,256,1024]{2,1,0:T(8,128)(2,1)} %param.33) | copy-start | bytes 3145732
  545.4 11.1 %copy-start.41 = (bf16[256,4096]{1,0:T(8,128)(2,1)}, bf16[256,4096]{1,0:T(8,128)(2,1)S(1)}, u32[]{:S(2)}) copy-start(bf16[256,4096]{1,0:T(8,128)(2,1)S(1)} %add_convert_fusion.1) | copy-start | bytes 6291460
  545.4 11.1 %copy-start.53 = (bf16[1024,4096]{1,0:T(8,128)(2,1)S(1)}, bf16[1024,4096]{1,0:T(8,128)(2,1)}, u32[]{:S(2)}) copy-start(bf16[1024,4096]{1,0:T(8,128)(2,1)} %all-gather.9.cloned.1.call-done) | copy-start | bytes 25165828
  545.4 27.5 %slice-start = ((s8[8388608]{0:T(1024)(128)(4,1)}), s8[4194304]{0:T(1024)(128)(4,1)S(1)}, s32[]{:S(2)}) async-start(s8[8388608]{0:T(1024)(128)(4,1)} %bitcast.526), calls=%async_computation.12 | async-start | bytes 8388608
  556.6 16.4 %slice-start.1 = ((s8[8388608]{0:T(1024)(128)(4,1)}), s8[4194304]{0:T(1024)(128)(4,1)S(1)}, s32[]{:S(2)}) async-start(s8[8388608]{0:T(1024)(128)(4,1)} %bitcast.526), calls=%async_computation.13 | async-start | bytes 8388608
  597.4 457.9 %reduce-scatter.11.cloned.1.call-start = ((), (), s32[]{:S(2)}) async-start(), calls=%async_computation.11 | async-start | bytes 17301504 | tf_op jit(solution)/shard_map/reduce_scatter | solution.py:152
  612.0 5.5 copy-start.17
  612.0 11.1 %slice-start.2 = ((s8[8388608]{0:T(1024)(128)(4,1)}), s8[4194304]{0:T(1024)(128)(4,1)S(1)}, s32[]{:S(2)}) async-start(s8[8388608]{0:T(1024)(128)(4,1)} %bitcast.528), calls=%async_computation.14 | async-start | bytes 8388608
  617.5 8.2 copy-start.43
  617.5 5.5 copy-start.52
  617.5 5.5 copy-start.50
  617.5 5.5 copy-start.38
  617.5 5.5 slice-start.3
  623.0 2.7 copy-start.45
  623.1 2.7 copy-start.42
  625.7 3.9 copy-start.27
  673.1 6.6 copy-start.6
  673.1 6.6 copy-start.14
  673.1 6.6 copy-start.48
  681.3 5.9 copy-start.8
  681.3 5.9 copy-start.47
  689.1 366.3 %copy-start.1 = (f32[64,64]{1,0:T(8,128)S(1)}, f32[64,64]{1,0:T(8,128)}, u32[]{:S(2)}) copy-start(f32[64,64]{1,0:T(8,128)} %param.31) | copy-start | bytes 49156
  (23 other events, 40.6 us)
Sparse Core Ops, SparseCore 0:
  11.1 59.5 all-gather.6
  73.7 68.1 all-gather.4
  144.9 75.8 all-gather.8
  223.6 76.2 all-gather.10
  378.1 141.1 reduce-scatter.6
  525.7 153.9 reduce-scatter.4
  682.6 185.3 reduce-scatter.8
  871.0 184.3 reduce-scatter.10
where the time goes:
time: 1080 us; the launch traced here: 1060 us
  matrix products  468 us (43%)
  waiting for transfers between devices  440 us (41%)
  blocking collectives  82.4 us (8%)
  local copies, waits for them, and re-layouts  40.1 us (4%)
  between operations  15.6 us (1%)
  other arithmetic  14 us (1%)
    reduce_scatter x1, waiting for transfers between devices, reduce_feed(): lax.psum_scatter(grads[1], ('dp', 'fsdp'), scatter_dimension=0, tiled=True)  187 us
    reduce_scatter x1, waiting for transfers between devices, reduce_feed(): lax.psum_scatter(grads[0], ('dp', 'fsdp'), scatter_dimension=0, tiled=True)  176 us
    unnamed x2, blocking collectives  82.4 us
    all_gather x1, waiting for transfers between devices, fetch_attention(): lax.all_gather(shards[0], ('dp', 'fsdp'), axis=0, tiled=True)  65.8 us
    dot_general x32, matrix products, attend_back(): jnp.einsum('qk,qf->kf', grad_scores, mapped_query, preferred_element_type...  53.9 us
    dot_general x32, matrix products, attend_back(): jnp.dot(grad_scores, mapped_key, preferred_element_type=jnp.float32)  43.2 us
    dot_general x32, matrix products, attend_back(): jnp.einsum('qk,qd->kd', scores_low, grad_numer, preferred_element_type=jn...  42.3 us
    dot_general x32, matrix products, attend_head(): jnp.einsum('qf,kf->qk', mapped_query, mapped_key, preferred_element_type=...  35.2 us
  transfers between devices with their start and end apart: 8, of which 4 were waited for; matrix products, arithmetic and copies ran while one was open for 48% of the time, Pallas kernels for 0%

commit v1 on v0

--- a/solution.py
+++ b/solution.py
@@ -4,6 +4,8 @@
 import jax
 import jax.numpy as jnp
 from jax import lax
+from jax.experimental import pallas as pl
+from jax.experimental.pallas import tpu as pltpu
 from jax.sharding import PartitionSpec as P
 
 D = 1024
@@ -161,7 +163,7 @@
     return tuple(jax.tree.map(jnp.add, tuple(running), tuple(update)))
 
 
-def per_device(
+def per_device_plain(
     tokens,
     lengths,
     mix_weight,
@@ -287,37 +289,940 @@
     )
 
 
+MESH_ID = pl.DeviceIdType.MESH
+LOW = jnp.bfloat16
+WIDE = jnp.float32
+
+
+def here(nz):
+    dp = lax.axis_index("dp")
+    fs = lax.axis_index("fsdp")
+    return dp // 2, dp % 2, fs // 2, fs % 2
+
+
+class Places:
+    def __init__(self, ny, nz):
+        self.ny, self.nz = ny, nz
+        self.y, self.x, self.z, self.c = here(nz)
+
+    def at(self, y, x, z, c):
+        return (y * 2 + x, z * 2 + c)
+
+    def member(self, r):
+        x = 1 - self.x if r & 2 else self.x
+        c = 1 - self.c if r & 1 else self.c
+        return x, c
+
+    def member_id(self, r):
+        x, c = self.member(r)
+        return self.at(self.y, x, self.z, c)
+
+    def yid(self):
+        return self.at(1 - self.y, self.x, self.z, self.c)
+
+    def zid(self, step):
+        return self.at(self.y, self.x, (self.z + step) % self.nz, self.c)
+
+    def zsrc(self, step):
+        return (self.z + self.nz - step) % self.nz
+
+    def greet(self):
+        barrier = pltpu.get_barrier_semaphore()
+        ids = [self.member_id(r) for r in (1, 2, 3)] + [self.yid()]
+        ids += [self.zid(step) for step in range(1, self.nz)]
+        for one in ids:
+            pl.semaphore_signal(barrier, inc=1, device_id=one, device_id_type=MESH_ID)
+        pl.semaphore_wait(barrier, len(ids))
+
+
+class Copy:
+    def __init__(self, describe):
+        self.describe = describe
+
+    def start(self):
+        self.describe().start()
+
+    def wait_recv(self):
+        self.describe().wait_recv()
+
+    def wait_send(self):
+        self.describe().wait_send()
+
+
+class Links:
+    def __init__(self, send, recv):
+        self.send, self.recv, self.count, self.open = send, recv, 0, []
+
+    def plan(self, src, dst, device):
+        i = self.count
+        self.count += 1
+
+        def describe():
+            return pltpu.make_async_remote_copy(
+                src() if callable(src) else src,
+                dst() if callable(dst) else dst,
+                self.send.at[i],
+                self.recv.at[i],
+                device_id=device() if callable(device) else device,
+                device_id_type=MESH_ID,
+            )
+
+        copy = Copy(describe)
+        self.open.append(copy)
+        return copy
+
+    def start(self, src, dst, device):
+        copy = self.plan(src, dst, device)
+        copy.start()
+        return copy
+
+
+class Locals:
+    def __init__(self, sems):
+        self.sems, self.count = sems, 0
+
+    def start(self, src, dst):
+        copy = pltpu.make_async_copy(src, dst, self.sems.at[self.count])
+        self.count += 1
+        copy.start()
+        return copy
+
+
+class Gather:
+    def __init__(self, links, place, block):
+        self.links, self.place, self.block = links, place, block
+
+    def begin(self, own=None):
+        place = self.place
+        target = self.block(place.y, place.z)
+        own = target if own is None else own
+        self.zs = [
+            self.links.start(own, target, place.zid(step)) for step in range(1, place.nz)
+        ]
+        self.ys = [self.links.start(own, target, place.yid())]
+
+    def forward(self):
+        place = self.place
+        for step in range(1, place.nz):
+            self.zs[step - 1].wait_recv()
+            held = self.block(place.y, place.zsrc(step))
+            self.ys.append(self.links.start(held, held, place.yid()))
+
+    def finish(self):
+        for copy in self.ys:
+            copy.wait_recv()
+
+
+def dot_nn(a, b):
+    return jnp.dot(a, b, preferred_element_type=WIDE)
+
+
+def dot_nt(a, b):
+    return lax.dot_general(a, b, (((1,), (1,)), ((), ())), preferred_element_type=WIDE)
+
+
+def dot_tn(a, b):
+    return lax.dot_general(a, b, (((0,), (0,)), ((), ())), preferred_element_type=WIDE)
+
+
+def fold_rows(values):
+    rows, cols = values.shape
+    return jnp.sum(values.reshape(rows // 8, 8, cols), axis=0)
+
+
+def gather_kernel(
+    ny, nz,
+    tok, cot, meta, up_own, mix_own, down_own, out_own, small_own,
+    mix_all, out_all, na_out, xh_out, cot_out, feed_out, gxf_out, gdown_out, gup_out,
+    meta_all, gains, gains_feed,
+    xs, gs, nf, na, act, gp, feed, gxf, up, down, gup, gdown, small,
+    send, recv, sems, sems_out,
+):
+    place = Places(ny, nz)
+    y, x, z, c = place.y, place.x, place.z, place.c
+    me = x * 2 + c
+    rows = xs.shape[1]
+    width = xs.shape[2]
+    half = up.shape[-1]
+    place.greet()
+    links = Links(send, recv)
+    local = Locals(sems)
+    tile = 256
+    per = rows // tile
+
+    up_mine = local.start(up_own.at[:, me], up.at[:, y, x, z, c])
+    mix_mine = local.start(mix_own.at[me], mix_all.at[y, x, z, c])
+    tok_mine = local.start(tok, xs.at[0])
+    cot_mine = local.start(cot, gs.at[0])
+    small_mine = local.start(small_own, small.at[y, x, z, c])
+    meta_mine = local.start(meta, meta_all.at[0])
+    down_mine = [
+        local.start(down_own.at[:, pl.ds(k * half, half)], down.at[k, y, z]) for k in range(2)
+    ]
+    out_mine = local.start(out_own, out_all.at[y, z // 2, z % 2, c])
+
+    up_swaps, small_swaps, mix_swaps, meta_swaps = [], [], [], []
+    for r in (1, 2, 3):
+        mx, mc = place.member(r)
+        to = place.member_id(r)
+        small_swaps.append(links.start(small_own, small.at[y, x, z, c], to))
+        up_swaps.append(links.start(up_own.at[:, mx * 2 + mc], up.at[:, y, x, z, c], to))
+    tok_sib = links.start(tok, xs.at[1], place.member_id(1))
+    tok_far = links.start(tok, xs.at[2], place.member_id(2))
+    out_gather = Gather(links, place, lambda by, bz: out_all.at[by, bz // 2, bz % 2, c])
+    out_gather.begin(out_own)
+
+    small_mine.wait()
+    for copy in small_swaps:
+        copy.wait_recv()
+    small_gather = Gather(links, place, lambda by, bz: small.at[by, :, bz])
+    small_gather.begin()
+    up_mine.wait()
+    for copy in up_swaps:
+        copy.wait_recv()
+    up_gather = [Gather(links, place, lambda by, bz, k=k: up.at[k, by, :, bz]) for k in range(2)]
+    up_gather[0].begin()
+    up_gather[1].begin()
+    for r in (1, 2, 3):
+        mx, mc = place.member(r)
+        to = place.member_id(r)
+        mix_swaps.append(links.start(mix_own.at[mx * 2 + mc], mix_all.at[y, x, z, c], to))
+        meta_swaps.append(links.start(meta, meta_all.at[r], to))
+    small_gather.forward()
+    small_gather.finish()
+    count = ny * 2 * nz * 2
+    packed = jnp.sum(small[...].reshape(count, 8, 128), axis=1).astype(LOW)
+    each = width // count
+    lane = lax.broadcasted_iota(jnp.int32, (128, width), 0)
+    col = lax.broadcasted_iota(jnp.int32, (128, width), 1)
+    owner = lax.broadcasted_iota(jnp.int32, (count, width), 0)
+    owned = lax.broadcasted_iota(jnp.int32, (count, width), 1)
+    for k in range(4):
+        pick = jnp.where(lane == k * each + col % each, 1.0, 0.0).astype(LOW)
+        spread = jnp.where(owned // each == owner, dot_nn(packed, pick), 0.0)
+        gains[k : k + 1, :] = jnp.sum(spread, axis=0, keepdims=True)
+    gains[4:8, :] = jnp.zeros((4, width), WIDE)
+    gains_feed[...] = jnp.zeros_like(gains_feed)
+
+    def norm(j):
+        def body(i, carry):
+            rs = pl.ds(pl.multiple_of(i * 128, 128), 128)
+            values = xs[j, rs, :].astype(WIDE)
+            center = values - jnp.mean(values, axis=1, keepdims=True)
+            spread = jnp.mean(center * center, axis=1, keepdims=True)
+            hat = center * lax.rsqrt(spread + epsilon)
+            na[j, rs, :] = (hat * gains[0:1, :] + gains[1:2, :]).astype(LOW)
+            nf[j, rs, :] = (hat * gains[2:3, :] + gains[3:4, :]).astype(LOW)
+            xs[j, rs, :] = hat.astype(LOW)
+            return carry
+
+        lax.fori_loop(0, rows // 128, body, 0)
+
+    def hidden(first, last, k):
+        weight = up.at[k]
+
+        def body(i, carry):
+            j = i // per
+            rs = pl.ds(pl.multiple_of((i % per) * tile, tile), tile)
+            h = dot_nn(nf[j, rs, :], weight[...].reshape(width, half))
+            cdf = 0.5 * (1.0 + lax.erf(h * math.sqrt(0.5)))
+            pdf = jnp.exp(-0.5 * h * h) * (1.0 / math.sqrt(2.0 * math.pi))
+            act[j, rs, pl.ds(k * half, half)] = (h * cdf).astype(LOW)
+            gp[j, rs, pl.ds(k * half, half)] = (cdf + h * pdf).astype(LOW)
+            return carry
+
+        lax.fori_loop(first * per, last * per, body, 0)
+
+    def back(first, last):
+        def body(i, carry):
+            j = i // per
+            rs = pl.ds(pl.multiple_of((i % per) * tile, tile), tile)
+            ga = jnp.zeros((tile, 2 * half), WIDE)
+            for k in range(2):
+                d = down[k].reshape(2 * half, half)
+                feed[j, rs, pl.ds(k * half, half)] = dot_nn(act[j, rs, :], d).astype(LOW)
+                ga += dot_nt(gs[j, rs, pl.ds(k * half, half)], d)
+            gh = (ga * gp[j, rs, :].astype(WIDE)).astype(LOW)
+            gp[j, rs, :] = gh
+            gn = jnp.zeros((tile, width), WIDE)
+            for k in range(2):
+                gn += dot_nt(gh[:, k * half : (k + 1) * half], up[k].reshape(width, half))
+            gains_feed[0:8, :] += fold_rows(gn * xs[j, rs, :].astype(WIDE))
+            gains_feed[8:16, :] += fold_rows(gn)
+            gxf[j, rs, :] = (gn * gains[2:3, :]).astype(LOW)
+            return carry
+
+        lax.fori_loop(first * per, last * per, body, 0)
+
+    def outer(a, b, dst):
+        whole = a.shape[0] * a.shape[1]
+
+        def body(i, carry):
+            cols = pl.ds(pl.multiple_of(i * 256, 256), 256)
+            part = dot_tn(a[:, :, cols].reshape(whole, 256), b[...].reshape(whole, width))
+            dst[pl.ds(pl.multiple_of(i * 256, 256), 256), :] = part.astype(LOW)
+            return carry
+
+        lax.fori_loop(0, width // 256, body, 0)
+
+    stores = Locals(sems_out)
+    written = []
+
+    tok_mine.wait()
+    norm(0)
+    tok_sib.wait_recv()
+    norm(1)
+    cot_sib = links.start(cot, gs.at[1], place.member_id(1))
+    cot_far = links.start(cot, gs.at[2], place.member_id(2))
+    out_gather.forward()
+    mix_mine.wait()
+    for copy in mix_swaps:
+        copy.wait_recv()
+    for copy in down_mine:
+        copy.wait()
+    down_gather = [Gather(links, place, lambda by, bz, k=k: down.at[k, by, bz]) for k in range(2)]
+    mix_gather = Gather(links, place, lambda by, bz: mix_all.at[by, :, bz])
+    up_gather[0].forward()
+    down_gather[0].begin()
+    up_gather[1].forward()
+    down_gather[1].begin()
+    up_gather[0].finish()
+    hidden(0, 2, 0)
+    tok_far.wait_recv()
+    tok_fwd = links.start(xs.at[2], xs.at[3], place.member_id(1))
+    up_gather[1].finish()
+    hidden(0, 2, 1)
+    down_gather[0].forward()
+    mix_gather.begin()
+    tok_fwd.wait_recv()
+    tok_fwd.wait_send()
+    norm(2)
+    norm(3)
+    for j in range(4):
+        written.append(stores.start(na.at[j], na_out.at[j]))
+        written.append(stores.start(xs.at[j], xh_out.at[j]))
+    hidden(2, 4, 0)
+    hidden(2, 4, 1)
+    down_gather[1].forward()
+    cot_far.wait_recv()
+    cot_fwd = links.start(gs.at[2], gs.at[3], place.member_id(1))
+    cot_mine.wait()
+    cot_sib.wait_recv()
+    down_gather[0].finish()
+    down_gather[1].finish()
+    back(0, 2)
+    mix_gather.forward()
+    cot_fwd.wait_recv()
+    for j in range(4):
+        written.append(stores.start(gs.at[j], cot_out.at[j]))
+    back(2, 4)
+    for j in range(4):
+        written.append(stores.start(feed.at[j], feed_out.at[j]))
+        written.append(stores.start(gxf.at[j], gxf_out.at[j]))
+    outer(act, gs, gdown)
+    written.append(stores.start(gdown, gdown_out))
+    outer(nf, gp, gup)
+    written.append(stores.start(gup, gup_out))
+    out_mine.wait()
+    out_gather.finish()
+    out_swap = links.start(
+        out_all.at[:, :, 1 - c, c], out_all.at[:, :, 1 - c, c], place.member_id(1)
+    )
+    mix_gather.finish()
+    meta_mine.wait()
+    for copy in meta_swaps:
+        copy.wait_recv()
+    out_swap.wait_recv()
+    for copy in written:
+        copy.wait()
+    links.open.remove(tok_fwd)
+    for copy in links.open:
+        copy.wait_send()
+
+
+class Scatter:
+    def __init__(self, links, place, theirs, mine, ybuf, zbuf):
+        self.links, self.place = links, place
+        self.theirs, self.mine, self.ybuf, self.zbuf = theirs, mine, ybuf, zbuf
+        self.ys = [self.plan_y(step) for step in range(place.nz)]
+        self.zs = [None] + [self.plan_z(step) for step in range(1, place.nz)]
+
+    def at(self, step):
+        return (self.place.z + step) % self.place.nz
+
+    def plan_y(self, step):
+        return self.links.plan(
+            lambda: self.theirs(self.at(step)), lambda: self.ybuf(self.at(step)), self.place.yid
+        )
+
+    def plan_z(self, step):
+        return self.links.plan(
+            lambda: self.ybuf(self.at(step)),
+            lambda: self.zbuf(step - 1),
+            lambda: self.place.zid(step),
+        )
+
+    def begin(self, step):
+        self.ys[step].start()
+
+    def turn(self, step):
+        self.ys[step].wait_recv()
+        if step:
+            at = self.at(step)
+            land = self.ybuf(at)
+            land[...] = (land[...].astype(WIDE) + self.mine(at)[...].astype(WIDE)).astype(LOW)
+            self.zs[step].start()
+
+    def total(self):
+        at = self.place.z
+        total = self.ybuf(at)[...].astype(WIDE) + self.mine(at)[...].astype(WIDE)
+        for step in range(1, self.place.nz):
+            self.zs[step].wait_recv()
+            total += self.zbuf(step - 1)[...].astype(WIDE)
+        return total
+
+
+def scatter_kernel(
+    ny, nz,
+    na_in, xh_in, cot_in, feed_in, gxf_in, mix_in, out_in, gdown_in, gup_in, meta_in,
+    gains, gains_feed, table, scale, spread, tok, cot,
+    out_rows, grad_rows, gmix_out, gout_out, gup_out, gdown_out, gains_out,
+    na, xh, gs, feed, gxf, mix, outw, down_own, up_own, meta, gmixed, attended, gmix, gout, gout_by,
+    ydown, zdown, yup, zup, ymix, zmix, yout, zout, up_send, up_recv, mix_send, mix_recv,
+    sib_out, sib_gx, own_out, own_gx, far_out, far_gx, gacc, gsum, gy, g2, gz, g3, gm,
+    send, recv, sems, sib_sems, own_sems, far_sems,
+):
+    place = Places(ny, nz)
+    y, x, z, c = place.y, place.x, place.z, place.c
+    width = na.shape[-1]
+    span = na.shape[2]
+    heads = 4
+    group = heads * HEAD
+    local = Locals(sems)
+    up_half = local.start(gup_in.at[y], up_own)
+    down_half = local.start(gdown_in.at[y], down_own)
+    meta_load = local.start(meta_in, meta)
+    mix_load = local.start(mix_in, mix)
+    out_load = local.start(out_in.at[:, :, c], outw)
+    loads = {}
+    for j in (3, 2, 1, 0):
+        loads[j] = [
+            local.start(src.at[j], dst.at[j])
+            for src, dst in ((na_in, na), (feed_in, feed), (gxf_in, gxf), (xh_in, xh), (cot_in, gs))
+        ]
+    place.greet()
+    links = Links(send, recv)
+
+    down_sum = Scatter(
+        links, place, lambda at: gdown_in.at[1 - y, at], lambda at: down_own.at[at],
+        lambda at: ydown.at[at], lambda k: zdown.at[k],
+    )
+    up_sum = Scatter(
+        links, place, lambda at: gup_in.at[1 - y, :, at], lambda at: up_own.at[:, at],
+        lambda at: yup.at[:, at], lambda k: zup.at[k],
+    )
+    mix_sum = Scatter(
+        links, place, lambda at: gmix.at[1 - y, :, at], lambda at: gmix.at[y, :, at],
+        lambda at: ymix.at[:, at], lambda k: zmix.at[k],
+    )
+    out_sum = Scatter(
+        links, place, lambda at: gout_by.at[1 - y, at // 2, at % 2], lambda at: gout_by.at[y, at // 2, at % 2],
+        lambda at: yout.at[at], lambda k: zout.at[k],
+    )
+    steps = list(range(1, nz)) + [0]
+    for step in steps:
+        down_sum.begin(step)
+    gacc[...] = jnp.zeros_like(gacc)
+    meta_load.wait()
+    mix_load.wait()
+    out_load.wait()
+    for copy in loads[3]:
+        copy.wait()
+
+    lane = lax.broadcasted_iota(jnp.int32, (1, group), 1)
+    of_head = [lane // HEAD == h for h in range(heads)]
+    low_lane = lax.broadcasted_iota(jnp.int32, (1, 128), 1) % HEAD < ROT // 2
+    key_at = lax.broadcasted_iota(jnp.int32, (span, span), 1)
+    query_at = lax.broadcasted_iota(jnp.int32, (span, span), 0)
+    causal = key_at <= query_at
+    wide_mix = mix.shape[-1]
+
+    def turn(values, cosine, sine):
+        parts = []
+        for first in range(0, group, 128):
+            part = values[:, first : first + 128]
+            other = jnp.where(
+                low_lane, pltpu.roll(part, 128 - ROT // 2, 1), pltpu.roll(part, ROT // 2, 1)
+            )
+            parts.append(part * cosine + other * sine)
+        return jnp.concatenate(parts, axis=1)
+
+    def spread_meta(j, s, first, last):
+        return lax.dot_general(
+            meta[j, s], spread[:, first:last], (((0,), (0,)), ((), ())),
+            precision=lax.Precision.HIGHEST, preferred_element_type=WIDE,
+        )
+
+    def sib_copy(s, kind):
+        buf, dst = ((feed, sib_out), (gxf, sib_gx))[kind]
+        return pltpu.make_async_remote_copy(
+            buf.at[3, s], dst.at[s], sib_sems.at[0, kind, s], sib_sems.at[1, kind, s],
+            device_id=place.member_id(1), device_id_type=MESH_ID,
+        )
+
+    def far_copy(s, kind):
+        buf, dst = ((feed, far_out), (gxf, far_gx))[kind]
+        return pltpu.make_async_remote_copy(
+            buf.at[2, s], dst.at[s], far_sems.at[0, kind, s], far_sems.at[1, kind, s],
+            device_id=place.member_id(2), device_id_type=MESH_ID,
+        )
+
+    def own_copy(s, kind):
+        buf, dst = ((feed, own_out), (gxf, own_gx))[kind]
+        return pltpu.make_async_remote_copy(
+            buf.at[1, s], dst.at[s], own_sems.at[0, kind, s], own_sems.at[1, kind, s],
+            device_id=place.member_id(1), device_id_type=MESH_ID,
+        )
+
+    def hand_on(j, s, value, kind):
+        buf = (feed, gxf)[kind]
+        landed = (sib_out, sib_gx)[kind]
+
+        @pl.when(j != 2)
+        def _():
+            buf[j, s] = value.astype(LOW)
+
+        @pl.when(j == 3)
+        def _():
+            sib_copy(s, kind).start()
+
+        @pl.when(j == 2)
+        def _():
+            sib_copy(s, kind).wait_recv()
+            buf[j, s] = (value + landed[s].astype(WIDE)).astype(LOW)
+            far_copy(s, kind).start()
+
+        @pl.when(j == 1)
+        def _():
+            own_copy(s, kind).start()
+
+    events = {}
+
+    def pump(i, place_in):
+        for at, event in events.items():
+            if at[1] == place_in:
+                pl.when(i == at[0])(event)
+
+    def slot(i, carry):
+        j = 3 - i // 2
+        s = i % 2
+        pump(i, 0)
+        rows = na[j, s]
+        mixed = dot_nn(rows, mix[...].reshape(width, wide_mix))
+        turns = spread_meta(j, s, 0, 384)
+        cosine, sine, owner = turns[:, :128], turns[:, 128:256], turns[:, 256:384]
+        owner = jnp.concatenate([owner, owner], axis=1)
+        allowed = (owner == meta[j, s, 16:17, :]) & causal
+        query = turn(mixed[:, :group], cosine, sine).astype(LOW)
+        key = turn(mixed[:, group : 2 * group], cosine, sine).astype(LOW)
+        value = mixed[:, 2 * group : 3 * group].astype(LOW)
+        raised_query = scale[0:1, :] * jnp.exp(dot_nn(query, table[...]))
+        raised_key = scale[0:1, :] * jnp.exp(dot_nn(key, table[...]))
+        phi_query = raised_query.astype(LOW)
+        phi_key = raised_key.astype(LOW)
+        none = jnp.zeros((), LOW)
+        scores, totals = [], []
+        numer = jnp.zeros((span, group), WIDE)
+        total = jnp.zeros((span, group), WIDE)
+        for h in range(heads):
+            score = dot_nt(jnp.where(of_head[h], phi_query, none), phi_key)
+            score = jnp.where(allowed, score, 0.0)
+            totals.append(jnp.sum(score, axis=1, keepdims=True))
+            scores.append(score.astype(LOW))
+            numer += dot_nn(scores[h], jnp.where(of_head[h], value, none))
+            total = jnp.where(of_head[h], totals[h], total)
+        att = (numer / total).astype(LOW)
+        attended[j, s] = att
+        attn_rows = dot_nn(att, outw[...].reshape(group, width))
+        hand_on(j, s, attn_rows + feed[j, s].astype(WIDE), 0)
+        pump(i, 1)
+        grad_att = dot_nt(gs[j, s], outw[...].reshape(group, width))
+        grad_numer = (grad_att / total).astype(LOW)
+        product = grad_att * numer
+        grad_query = jnp.zeros((span, group), WIDE)
+        grad_key = jnp.zeros((span, group), WIDE)
+        grad_value = jnp.zeros((span, group), WIDE)
+        for h in range(heads):
+            grad_total = -jnp.sum(jnp.where(of_head[h], product, 0.0), axis=1, keepdims=True)
+            grad_total = grad_total / (totals[h] * totals[h])
+            numer_h = jnp.where(of_head[h], grad_numer, none)
+            grad_score = dot_nt(numer_h, value) + grad_total
+            grad_score = jnp.where(allowed, grad_score, 0.0).astype(LOW)
+            grad_query += dot_nn(grad_score, jnp.where(of_head[h], phi_key, none))
+            grad_key += dot_tn(grad_score, jnp.where(of_head[h], phi_query, none))
+            grad_value += dot_tn(scores[h], numer_h)
+        back_query = turn(
+            dot_nt((grad_query * raised_query).astype(LOW), table[...]), cosine, -sine
+        )
+        back_key = turn(dot_nt((grad_key * raised_key).astype(LOW), table[...]), cosine, -sine)
+        grad_mixed = jnp.concatenate(
+            [back_query.astype(LOW), back_key.astype(LOW), grad_value.astype(LOW)], axis=1
+        )
+        gmixed[j, s] = grad_mixed
+        grad_normed = dot_nt(grad_mixed, mix[...].reshape(width, wide_mix))
+        gacc[0:8, :] += fold_rows(grad_normed * xh[j, s].astype(WIDE))
+        gacc[8:16, :] += fold_rows(grad_normed)
+        hand_on(j, s, grad_normed * gains[0:1, :] + gxf[j, s].astype(WIDE), 1)
+        return carry
+
+    def waits(j):
+        def event():
+            for copy in loads[j]:
+                copy.wait()
+
+        return event
+
+    def both(*fns):
+        def event():
+            for fn in fns:
+                fn()
+
+        return event
+
+    def begin_up():
+        up_half.wait()
+        down_half.wait()
+        for step in steps:
+            up_sum.begin(step)
+
+    events[(0, 1)] = begin_up
+    events[(1, 1)] = lambda: down_sum.turn(steps[0])
+    events[(2, 0)] = waits(2)
+    events[(2, 1)] = lambda: down_sum.turn(steps[1])
+    events[(4, 0)] = both(waits(1), lambda: down_sum.turn(steps[2]))
+    events[(5, 1)] = lambda: down_sum.turn(steps[3])
+    events[(6, 0)] = both(waits(0), lambda: up_sum.turn(steps[0]))
+    events[(7, 1)] = lambda: up_sum.turn(steps[1])
+    lax.fori_loop(0, 8, slot, 0)
+
+    rest = 4 * 2 * span
+    part = dot_tn(attended[...].reshape(rest, group), gs[...].reshape(rest, width))
+    gout[...] = part.astype(LOW).reshape(gout.shape)
+    out_swap = links.start(gout.at[:, :, 1 - c], gout_by.at[:, :, c], place.member_id(1))
+    gout_by[:, :, c] = gout[:, :, c]
+
+    gsum[...] = jnp.zeros_like(gsum)
+    gsum[0:1, :] = jnp.sum(gacc[0:8, :], axis=0, keepdims=True)
+    gsum[1:2, :] = jnp.sum(gacc[8:16, :], axis=0, keepdims=True)
+    gsum[2:3, :] = jnp.sum(gains_feed[0:8, :], axis=0, keepdims=True)
+    gsum[3:4, :] = jnp.sum(gains_feed[8:16, :], axis=0, keepdims=True)
+    gain_y = links.start(gsum, gy, place.yid())
+
+    def outer_mix(first):
+        def body(i, carry):
+            at_y = (y + 1 + i // 2) % ny
+            cols = pl.ds(pl.multiple_of((at_y * 2 + i % 2) * 256, 256), 256)
+            part = dot_tn(na[:, :, :, cols].reshape(rest, 256), gmixed[...].reshape(rest, wide_mix))
+            gmix[at_y, i % 2] = part.astype(LOW).reshape(gmix.shape[2:])
+            return carry
+
+        lax.fori_loop(first, first + 2, body, 0)
+
+    outer_mix(0)
+    out_swap.wait_recv()
+    for step in steps:
+        out_sum.begin(step)
+    for step in steps:
+        mix_sum.begin(step)
+    up_sum.turn(steps[2])
+    gain_y.wait_recv()
+    g2[...] = gsum[...] + gy[...]
+    gain_zs = [links.start(g2, gz.at[step - 1], place.zid(step)) for step in range(1, nz)]
+    outer_mix(2)
+    up_sum.turn(steps[3])
+    gdown_out[...] = down_sum.total()
+
+    def finish(s, carry):
+        for kind in (0, 1):
+            own_copy(s, kind).wait_recv()
+            far_copy(s, kind).wait_recv()
+        keep = spread_meta(0, s, 384, 512)[:, :1]
+        values = tok[s].astype(WIDE)
+        added = feed[0, s].astype(WIDE) + own_out[s].astype(WIDE) + far_out[s].astype(WIDE)
+        out_rows[s] = (values + keep * added).astype(LOW)
+        grad = gxf[0, s].astype(WIDE) + own_gx[s].astype(WIDE) + far_gx[s].astype(WIDE)
+        center = values - jnp.mean(values, axis=1, keepdims=True)
+        rate = lax.rsqrt(jnp.mean(center * center, axis=1, keepdims=True) + epsilon)
+        hat = center * rate
+        inner = jnp.mean(grad * hat, axis=1, keepdims=True)
+        grad = grad - jnp.mean(grad, axis=1, keepdims=True) - hat * inner
+        grad_rows[s] = cot[s].astype(WIDE) + rate * grad
+        return carry
+
+    lax.fori_loop(0, 2, finish, 0)
+    for step in steps:
+        out_sum.turn(step)
+    for step in range(1, nz):
+        gain_zs[step - 1].wait_recv()
+    g3[...] = g2[...] + sum(gz[step - 1] for step in range(1, nz))
+    gain_ms = [links.start(g3, gm.at[r - 1], place.member_id(r)) for r in (1, 2, 3)]
+    for step in steps:
+        mix_sum.turn(step)
+
+    def share(total, hold, land):
+        hold[...] = total.astype(LOW).reshape(hold.shape)
+        copies = []
+        for r in (1, 2, 3):
+            mx, mc = place.member(r)
+            copies.append(links.start(hold.at[mx, mc], land.at[r - 1], place.member_id(r)))
+        return copies
+
+    def collect(copies, hold, land, dst):
+        dst[x * 2 + c] = hold[x, c].astype(WIDE)
+        for r in (1, 2, 3):
+            mx, mc = place.member(r)
+            copies[r - 1].wait_recv()
+            dst[mx * 2 + mc] = land[r - 1].astype(WIDE)
+
+    up_shares = share(up_sum.total(), up_send, up_recv)
+    gout_out[...] = out_sum.total()
+    for copy in gain_ms:
+        copy.wait_recv()
+    gains_out[...] = g3[...] + gm[0] + gm[1] + gm[2]
+    mix_shares = share(mix_sum.total(), mix_send, mix_recv)
+    collect(up_shares, up_send, up_recv, gup_out)
+    collect(mix_shares, mix_send, mix_recv, gmix_out)
+    for copy in links.open:
+        copy.wait_send()
+    for kind in (0, 1):
+        for s in (0, 1):
+            sib_copy(s, kind).wait_send()
+            far_copy(s, kind).wait_send()
+            own_copy(s, kind).wait_send()
+
+
+VMEM = pl.BlockSpec(memory_space=pltpu.VMEM)
+ANY = pl.BlockSpec(memory_space=pl.ANY)
+SHAPE = jax.ShapeDtypeStruct
+LIMIT = 60 * 2**20
+
+
+def turn_table(position):
+    half = ROT // 2
+    inverse = 10000.0 ** (-2.0 * jnp.arange(half, dtype=WIDE) / ROT)
+    angle = position[..., None] * inverse
+    return jnp.cos(angle), jnp.sin(angle)
+
+
+def spread_rows():
+    row = jnp.arange(24)[:, None]
+    lane = jnp.arange(512)[None, :]
+    part, dim = lane // 128, lane % HEAD
+    half = ROT // 2
+    cosine = (part == 0) & (dim < ROT) & (row == dim % half)
+    cosine = cosine | ((part == 0) & (dim >= ROT) & (row == 17))
+    sine = (part == 1) & (dim < ROT) & (row == half + dim % half)
+    rest = ((part == 2) & (row == 16)) | ((part == 3) & (row == 18))
+    sign = jnp.where((part == 1) & (dim < half), -1.0, 1.0)
+    return jnp.where(cosine | sine | rest, sign, 0.0).astype(WIDE)
+
+
+def per_device_group(
+    ny,
+    nz,
+    tokens,
+    lengths,
+    mix_weight,
+    out_weight,
+    up_weight,
+    down_weight,
+    attn_gain,
+    attn_bias,
+    feed_gain,
+    feed_bias,
+    feature_freq,
+    feature_scale,
+    cotangent,
+):
+    micro, span, width = tokens.shape
+    rows = micro * span
+    shard = mix_weight.shape[0]
+    feed_shard = down_weight.shape[0]
+    count = ny * 2 * nz * 2
+    heads = width // HEAD // 4
+    group = heads * HEAD
+    hidden = feed_shard * ny * nz
+    half = hidden // 2
+
+    segment, position, valid = slot_layout(lengths[:, 0], span)
+    cosine, sine = turn_table(position)
+    facts = jnp.concatenate(
+        [
+            cosine,
+            sine,
+            segment.astype(WIDE)[..., None],
+            jnp.ones((micro, span, 1), WIDE),
+            valid[..., None],
+            jnp.zeros((micro, span, 5), WIDE),
+        ],
+        axis=-1,
+    )
+    meta = jnp.swapaxes(facts, 1, 2)
+    table = feature_table(feature_freq)
+    table_wide = jnp.kron(jnp.eye(heads, dtype=LOW), table)
+    scale = jnp.broadcast_to(jnp.tile(feature_scale, heads)[None], (8, group))
+    branch = jnp.where(valid[..., None] > 0.0, cotangent, jnp.zeros_like(cotangent))
+    up_own = up_weight.reshape(shard, ny, 2, nz, 2, feed_shard).transpose(2, 4, 0, 1, 3, 5)
+    up_own = up_own.reshape(4, shard, 2, half).transpose(2, 0, 1, 3)
+    mix_own = mix_weight.reshape(shard, 3, ny, 2, nz // 2, 2, HEAD).transpose(3, 5, 0, 1, 2, 4, 6)
+    mix_own = mix_own.reshape(4, shard, 3 * group)
+    small = jnp.concatenate([attn_gain, attn_bias, feed_gain, feed_bias]).astype(WIDE)
+    small = jnp.pad(small[None], ((0, 7), (0, 0)))
+
+    dma = pltpu.SemaphoreType.DMA
+    names = [
+        ("mix_all", (ny, 2, nz, 2, shard, 3 * group), LOW),
+        ("out_all", (ny, nz // 2, 2, 2, shard, width), LOW),
+        ("na", (4, rows, width), LOW),
+        ("xh", (4, rows, width), LOW),
+        ("cot", (4, rows, width), LOW),
+        ("feed", (4, rows, width), LOW),
+        ("gxf", (4, rows, width), LOW),
+        ("gdown", (hidden, width), LOW),
+        ("gup", (width, hidden), LOW),
+        ("meta", (4, micro, 24, span), WIDE),
+        ("gains", (8, width), WIDE),
+        ("gains_feed", (16, width), WIDE),
+    ]
+    full = pltpu.VMEM((4, rows, width), LOW)
+    first = pl.pallas_call(
+        partial(gather_kernel, ny, nz),
+        out_shape=[SHAPE(shape, kind) for _, shape, kind in names],
+        in_specs=[ANY] * 8,
+        out_specs=[ANY] * 10 + [VMEM] * 2,
+        scratch_shapes=[full] * 8
+        + [
+            pltpu.VMEM((2, ny, 2, nz, 2, shard, half), LOW),
+            pltpu.VMEM((2, ny, nz, feed_shard, half), LOW),
+            pltpu.VMEM((width, hidden), LOW),
+            pltpu.VMEM((hidden, width), LOW),
+            pltpu.VMEM((ny, 2, nz, 2, 8, 128), WIDE),
+            dma((80,)),
+            dma((80,)),
+            dma((12,)),
+            dma((24,)),
+        ],
+        name="gather_feed",
+        cost_estimate=pl.CostEstimate(flops=25 * 10**9, bytes_accessed=40 * 10**6, transcendentals=0),
+        compiler_params=pltpu.CompilerParams(
+            collective_id=0, has_side_effects=True, vmem_limit_bytes=LIMIT
+        ),
+    )(
+        tokens.reshape(rows, width), branch.reshape(rows, width), meta, up_own, mix_own,
+        down_weight, out_weight, small,
+    )
+    mix_all, out_all, na, xh, cot, feed, gxf, gdown, gup, meta_all, gains, gains_feed = first
+
+    by_slot = (4, micro, span, width)
+    slots = pltpu.VMEM(by_slot, LOW)
+    landing = pltpu.VMEM((micro, span, width), LOW)
+    pair = 2 * shard
+    results = [
+        SHAPE((micro, span, width), LOW),
+        SHAPE((micro, span, width), WIDE),
+        SHAPE((4, shard, 3 * group), WIDE),
+        SHAPE((shard, width), WIDE),
+        SHAPE((4, shard, hidden), WIDE),
+        SHAPE((feed_shard, width), WIDE),
+        SHAPE((8, width), WIDE),
+    ]
+    second = pl.pallas_call(
+        partial(scatter_kernel, ny, nz),
+        out_shape=results,
+        in_specs=[ANY] * 10 + [VMEM] * 7,
+        out_specs=[VMEM] * 7,
+        scratch_shapes=[slots] * 5
+        + [
+            pltpu.VMEM((ny, 2, nz, 2, shard, 3 * group), LOW),
+            pltpu.VMEM((ny, nz // 2, 2, shard, width), LOW),
+            pltpu.VMEM((nz, feed_shard, width), LOW),
+            pltpu.VMEM((2, nz, pair, hidden), LOW),
+            pltpu.VMEM((4, micro, 24, span), WIDE),
+            pltpu.VMEM((4, micro, span, 3 * group), LOW),
+            pltpu.VMEM((4, micro, span, group), LOW),
+            pltpu.VMEM((ny, 2, nz, pair, 3 * group), LOW),
+            pltpu.VMEM((ny, nz // 2, 2, shard, width), LOW),
+            pltpu.VMEM((ny, nz // 2, 2, shard, width), LOW),
+            pltpu.VMEM((nz, feed_shard, width), LOW),
+            pltpu.VMEM((nz - 1, feed_shard, width), LOW),
+            pltpu.VMEM((2, nz, pair, hidden), LOW),
+            pltpu.VMEM((nz - 1, 2, pair, hidden), LOW),
+            pltpu.VMEM((2, nz, pair, 3 * group), LOW),
+            pltpu.VMEM((nz - 1, 2, pair, 3 * group), LOW),
+            pltpu.VMEM((nz, shard, width), LOW),
+            pltpu.VMEM((nz - 1, shard, width), LOW),
+            pltpu.VMEM((2, 2, shard, hidden), LOW),
+            pltpu.VMEM((3, shard, hidden), LOW),
+            pltpu.VMEM((2, 2, shard, 3 * group), LOW),
+            pltpu.VMEM((3, shard, 3 * group), LOW),
+        ]
+        + [landing] * 6
+        + [
+            pltpu.VMEM((16, width), WIDE),
+            pltpu.VMEM((8, width), WIDE),
+            pltpu.VMEM((8, width), WIDE),
+            pltpu.VMEM((8, width), WIDE),
+            pltpu.VMEM((nz - 1, 8, width), WIDE),
+            pltpu.VMEM((8, width), WIDE),
+            pltpu.VMEM((3, 8, width), WIDE),
+            dma((80,)),
+            dma((80,)),
+            dma((28,)),
+            dma((2, 2, 2)),
+            dma((2, 2, 2)),
+            dma((2, 2, 2)),
+        ],
+        name="attend_scatter",
+        cost_estimate=pl.CostEstimate(flops=25 * 10**9, bytes_accessed=40 * 10**6, transcendentals=0),
+        compiler_params=pltpu.CompilerParams(
+            collective_id=1, has_side_effects=True, vmem_limit_bytes=LIMIT
+        ),
+    )(
+        na.reshape(by_slot), xh.reshape(by_slot), cot.reshape(by_slot), feed.reshape(by_slot),
+        gxf.reshape(by_slot), mix_all, out_all,
+        gdown.reshape(ny, nz, feed_shard, width), gup.reshape(ny, 2, nz, pair, hidden), meta_all,
+        gains, gains_feed, table_wide, scale, spread_rows(), tokens, cotangent,
+    )
+    out_rows, grad_rows, gmix, gout, gup, gdown, gains_out = second
+    gmix = gmix.reshape(2, 2, shard, 3, ny, nz // 2, HEAD).transpose(2, 3, 4, 0, 5, 1, 6)
+    gup = gup.reshape(2, 2, shard, ny, nz, feed_shard).transpose(2, 3, 0, 4, 1, 5)
+    index = lax.axis_index("dp") * (2 * nz) + lax.axis_index("fsdp")
+    gains_out = lax.dynamic_slice_in_dim(gains_out, index * shard, shard, 1)
+    return (
+        out_rows,
+        grad_rows,
+        gmix.reshape(mix_weight.shape),
+        gout,
+        gup.reshape(up_weight.shape),
+        gdown,
+        gains_out[0],
+        gains_out[1],
+        gains_out[2],
+        gains_out[3],
+    )
+
+
 def solution(mesh):
-    placed = (
-        P(None, ("dp", "fsdp"), None),
-        P(None, ("dp", "fsdp"), None),
-        P(("dp", "fsdp"), None),
-        P(("dp", "fsdp"), None),
-        P(("dp", "fsdp"), None),
-        P(("dp", "fsdp"), None),
-        P(("dp", "fsdp")),
-        P(("dp", "fsdp")),
-        P(("dp", "fsdp")),
-        P(("dp", "fsdp")),
-        P(),
-        P(),
-        P(None, ("dp", "fsdp"), None),
-    )
+    ny, nz = mesh.shape["dp"] // 2, mesh.shape["fsdp"] // 2
+    grouped = ny == 2 and nz % 2 == 0 and D // mesh.size % 32 == 0
+    body = partial(per_device_group, ny, nz) if grouped else per_device_plain
+    rows = P(("dp", "fsdp"), None)
+    vector = P(("dp", "fsdp"))
+    slots = P(None, ("dp", "fsdp"), None)
     return jax.shard_map(
-        per_device,
+        body,
         mesh=mesh,
-        in_specs=placed,
-        out_specs=(
-            P(None, ("dp", "fsdp"), None),
-            P(None, ("dp", "fsdp"), None),
-            P(("dp", "fsdp"), None),
-            P(("dp", "fsdp"), None),
-            P(("dp", "fsdp"), None),
-            P(("dp", "fsdp"), None),
-            P(("dp", "fsdp")),
-            P(("dp", "fsdp")),
-            P(("dp", "fsdp")),
-            P(("dp", "fsdp")),
-        ),
+        in_specs=(slots, slots, *[rows] * 4, *[vector] * 4, P(), P(), slots),
+        out_specs=(slots, slots, *[rows] * 4, *[vector] * 4),
         check_vma=False,
     )

time: 1080 us -> 233 us (0.22); the launches traced: 1060 us -> 231 us
  matrix products: 468 us -> 0.36 us
  waiting for transfers between devices: 440 us -> 0 us
  Pallas kernels: 0 us -> 205 us
  blocking collectives: 82.4 us -> 0 us
  local copies, waits for them, and re-layouts: 40.1 us -> 19.5 us
  between operations: 15.6 us -> 0.92 us
    dot_general x288 -> x0, matrix products: 467 us -> none  [the longest x32 53.9 us: attend_back(): jnp.einsum('qk,qf->kf', grad_scores, mapped_query, preferred_element_type...]
    reduce_scatter x4 -> x0, waiting for transfers between devices: 363 us -> none  [the longest x1 187 us: reduce_feed(): lax.psum_scatter(grads[1], ('dp', 'fsdp'), scatter_dimension=0, tiled=True)]
    pallas_call x0 -> x2, Pallas kernels: none -> 205 us  [the longest x1 111 us: per_device_group(): pl.pallas_call(partial(gather_kernel, ny, nz), out_shape=[SHAPE(shape, ki...]
    unnamed x2 -> x0, blocking collectives: 82.4 us -> none
    all_gather x4 -> x0, waiting for transfers between devices: 74.6 us -> none  [the longest x1 65.8 us: fetch_attention(): lax.all_gather(shards[0], ('dp', 'fsdp'), axis=0, tiled=True)]
    unnamed x146 -> x26, local copies, waits for them, and re-layouts: 21.6 us -> 5.63 us
  transfers between devices with their start and end apart: 8 -> 0, of which waited for: 4 -> 0; matrix products, arithmetic and copies ran while one was open for 48% -> 0% of each run, Pallas kernels for 0% -> 0%
where the time goes in v1:
time: 233 us; the launch traced here: 231 us
  Pallas kernels  205 us (88%)
  local copies, waits for them, and re-layouts  19.5 us (8%)
  other arithmetic  5.93 us (3%)
    pallas_call x1, Pallas kernels, per_device_group(): pl.pallas_call(partial(gather_kernel, ny, nz), out_shape=[SHAPE(shape, ki...  111 us
    pallas_call x1, Pallas kernels, per_device_group(): pl.pallas_call(partial(scatter_kernel, ny, nz), out_shape=results, in_spe...  93.3 us
    unnamed x26, local copies, waits for them, and re-layouts  5.63 us

profile of v1, /device:TPU:0, one launch (start us, length us, event | category | flops | bytes accessed | tf_op | source)
XLA Modules:
  0.0 231.3 jit_solution(411140139375135664)
XLA Ops:
  0.6 0.0 copy-start
  0.7 0.0 copy-start.4
  0.7 0.0 copy-start.9
  0.7 0.0 copy-start.8
  0.7 0.0 copy-start.7
  0.7 0.0 copy-start.6
  0.7 0.9 reduce_window_sum.13
  1.6 0.1 convert_reduce_fusion
  1.7 0.7 fusion.40
  2.4 0.1 select_reduce_fusion
  2.5 0.2 slice_reduce_fusion
  2.6 0.1 fusion.44
  2.7 0.1 multiply_sine_fusion
  2.9 1.8 concatenate.21
  4.8 2.3 %broadcast_select_fusion = bf16[2,256,1024]{2,1,0:T(8,128)(2,1)} fusion(bf16[2,256,1024]{2,1,0:T(8,128)(2,1)} %cot.1, pred[2,256]{1,0:T(4,128)(4,1)S(1)} %get-tuple-element.55), kind=kLoop, calls=%fused_computation.2 | loop fusion | flops 524288 | bytes 2097664 | tf_op jit(solution)/shard_map/jit(_where)/select_n | solution.py:1074
  7.1 1.2 reshape.342
  8.3 0.2 copy.42
  8.6 0.9 reshape.343.mix_own
  9.5 0.0 copy-done.4
  9.5 0.2 reshape.340
  9.7 0.1 copy.43
  9.8 0.8 reshape.341
  10.6 0.0 copy-done.9
  10.6 0.7 fusion.30.small_own
  11.3 111.3 %gather_feed.1 = (bf16[2,2,4,2,32,768]{5,4,3,2,1,0:T(8,128)(2,1)}, bf16[2,2,2,2,32,1024]{5,4,3,2,1,0:T(8,128)(2,1)}, bf16[4,512,1024]{2,1,0:T(8,128)(2,1)}, bf16...) custom-call(bf16[512,1024]{1,0:T(8,128)(2,1)} %bitcast.55, ...), custom_call_target="tpu_custom_call" | custom-call | flops 24999999488 | bytes 40000000 | tf_op jit(solution)/shard_map/gather_feed/pallas_call | solution.py:1098
  122.7 0.7 fusion.5.spread
  123.4 0.4 fusion
  123.8 0.2 broadcast_multiply_fusion
  123.9 0.9 mul.103.table
  124.8 0.0 copy-done.10
  124.8 0.1 broadcast_in_dim.108
  124.9 0.6 broadcast_in_dim.109.scale
  125.5 93.3 %attend_scatter.1 = (bf16[2,256,1024]{2,1,0:T(8,128)(2,1)}, f32[2,256,1024]{2,1,0:T(8,128)}, f32[4,32,768]{2,1,0:T(8,128)}, f32[32,1024]{1,0:T(8,128)}, f32[4,32...) custom-call(bf16[4,2,256,1024]{3,2,1,0:T(8,128)(2,1)} %bitcast.56, bf16[4,2,256,1024]{3,2,1,0:T(8,128)(2,1)} %bitcast.57, ...), custom_call_target="tpu_custom_call" | custom-call | flops 24999999488 | bytes 40000000 | tf_op jit(solution)/shard_map/attend_scatter/pallas_call | solution.py:1139
  218.9 1.6 reshape.351
  220.5 0.6 copy.38
  221.1 1.4 reshape.352
  222.5 0.2 reshape.353
  222.8 0.4 copy.39
  223.2 1.2 reshape.354
  224.4 0.8 constant_dynamic-slice_fusion
  225.2 0.5 slice_bitcast_fusion
  225.7 0.0 copy-done.1
  225.7 1.0 copy.48
  226.7 3.2 %copy.49 = f32[2,256,1024]{2,1,0:T(8,128)} copy(f32[2,256,1024]{2,1,0:T(8,128)} %get-tuple-element.79) | data formatting | bytes 4194304
  229.9 0.0 copy-done.5
  229.9 0.7 copy.50
  230.5 0.0 copy-done.2
  230.5 0.8 copy.51
  (26 shorter events, 0.1 us)
Async XLA Ops:
  0.6 122.7 %copy-start = (f32[64,64]{1,0:T(8,128)S(1)}, f32[64,64]{1,0:T(8,128)}, u32[]{:S(2)}) copy-start(f32[64,64]{1,0:T(8,128)} %param.23) | copy-start | bytes 49156
  0.7 8.8 %copy-start.4 = (bf16[32,4096]{1,0:T(8,128)(2,1)S(1)}, bf16[32,4096]{1,0:T(8,128)(2,1)}, u32[]{:S(2)}) copy-start(bf16[32,4096]{1,0:T(8,128)(2,1)} %param.17) | copy-start | bytes 786436
  0.7 9.9 %copy-start.9 = (bf16[32]{0:T(256)(128)(2,1)S(1)}, bf16[32]{0:T(256)(128)(2,1)}, u32[]{:S(2)}) copy-start(bf16[32]{0:T(256)(128)(2,1)} %param.19) | copy-start | bytes 196
  0.7 9.9 %copy-start.8 = (bf16[32]{0:T(256)(128)(2,1)S(1)}, bf16[32]{0:T(256)(128)(2,1)}, u32[]{:S(2)}) copy-start(bf16[32]{0:T(256)(128)(2,1)} %param.20) | copy-start | bytes 196
  0.7 9.9 %copy-start.7 = (bf16[32]{0:T(256)(128)(2,1)S(1)}, bf16[32]{0:T(256)(128)(2,1)}, u32[]{:S(2)}) copy-start(bf16[32]{0:T(256)(128)(2,1)} %param.21) | copy-start | bytes 196
  0.7 9.9 %copy-start.6 = (bf16[32]{0:T(256)(128)(2,1)S(1)}, bf16[32]{0:T(256)(128)(2,1)}, u32[]{:S(2)}) copy-start(bf16[32]{0:T(256)(128)(2,1)} %param.22) | copy-start | bytes 196
  11.2 113.5 %copy-start.10 = (f32[64]{0:T(128)S(1)}, f32[64]{0:T(128)}, u32[]{:S(2)}) copy-start(f32[64]{0:T(128)} %param.24) | copy-start | bytes 772
  218.8 3.7 %copy-start.3 = (f32[4,32,1024]{2,1,0:T(8,128)S(1)}, f32[4,32,1024]{2,1,0:T(8,128)}, u32[]{:S(2)}) copy-start(f32[4,32,1024]{2,1,0:T(8,128)} %get-tuple-element.45) | copy-start | bytes 1572868
  218.8 6.9 %copy-start.1 = (bf16[2,256,1024]{2,1,0:T(8,128)(2,1)S(1)}, bf16[2,256,1024]{2,1,0:T(8,128)(2,1)}, u32[]{:S(2)}) copy-start(bf16[2,256,1024]{2,1,0:T(8,128)(2,1)} %get-tuple-element.78) | copy-start | bytes 3145732
  222.8 7.1 %copy-start.5 = (f32[32,1024]{1,0:T(8,128)S(1)}, f32[32,1024]{1,0:T(8,128)}, u32[]{:S(2)}) copy-start(f32[32,1024]{1,0:T(8,128)} %get-tuple-element.81) | copy-start | bytes 393220
  222.8 7.7 %copy-start.2 = (f32[128,1024]{1,0:T(8,128)S(1)}, f32[128,1024]{1,0:T(8,128)}, u32[]{:S(2)}) copy-start(f32[128,1024]{1,0:T(8,128)} %get-tuple-element.83) | copy-start | bytes 1572868

commit v2 on v0

--- a/solution.py
+++ b/solution.py
@@ -3,7 +3,10 @@
 
 import jax
 import jax.numpy as jnp
+import numpy as np
 from jax import lax
+from jax.experimental import pallas as pl
+from jax.experimental.pallas import tpu as pltpu
 from jax.sharding import PartitionSpec as P
 
 D = 1024
@@ -161,7 +164,7 @@
     return tuple(jax.tree.map(jnp.add, tuple(running), tuple(update)))
 
 
-def per_device(
+def per_device_plain(
     tokens,
     lengths,
     mix_weight,
@@ -287,37 +290,1256 @@
     )
 
 
+MESH_ID = pl.DeviceIdType.MESH
+LOW = jnp.bfloat16
+WIDE = jnp.float32
+
+
+def here(nz):
+    dp = lax.axis_index("dp")
+    fs = lax.axis_index("fsdp")
+    return dp // 2, dp % 2, fs // 2, fs % 2
+
+
+class Places:
+    def __init__(self, ny, nz):
+        self.ny, self.nz = ny, nz
+        self.y, self.x, self.z, self.c = here(nz)
+
+    def at(self, y, x, z, c):
+        return (y * 2 + x, z * 2 + c)
+
+    def member(self, r):
+        x = 1 - self.x if r & 2 else self.x
+        c = 1 - self.c if r & 1 else self.c
+        return x, c
+
+    def member_id(self, r):
+        x, c = self.member(r)
+        return self.at(self.y, x, self.z, c)
+
+    def yid(self):
+        return self.at(1 - self.y, self.x, self.z, self.c)
+
+    def zid(self, step):
+        return self.at(self.y, self.x, (self.z + step) % self.nz, self.c)
+
+    def zsrc(self, step):
+        return (self.z + self.nz - step) % self.nz
+
+    def signal(self):
+        barrier = pltpu.get_barrier_semaphore()
+        ids = [self.member_id(r) for r in (1, 2, 3)] + [self.yid()]
+        ids += [self.zid(step) for step in range(1, self.nz)]
+        for one in ids:
+            pl.semaphore_signal(barrier, inc=1, device_id=one, device_id_type=MESH_ID)
+
+    def meet(self):
+        pl.semaphore_wait(pltpu.get_barrier_semaphore(), self.nz + 3)
+
+
+class Copy:
+    def __init__(self, describe):
+        self.describe, self.sent = describe, False
+
+    def start(self):
+        self.describe().start()
+
+    def wait_recv(self):
+        self.describe().wait_recv()
+
+    def wait_send(self):
+        if not self.sent:
+            self.describe().wait_send()
+            self.sent = True
+
+
+class Links:
+    def __init__(self, send, recv):
+        self.send, self.recv, self.count, self.open = send, recv, 0, []
+
+    def plan(self, src, dst, device):
+        i = self.count
+        self.count += 1
+
+        def describe():
+            return pltpu.make_async_remote_copy(
+                src() if callable(src) else src,
+                dst() if callable(dst) else dst,
+                self.send.at[i],
+                self.recv.at[i],
+                device_id=device() if callable(device) else device,
+                device_id_type=MESH_ID,
+            )
+
+        return Copy(describe)
+
+    def start(self, src, dst, device):
+        copy = self.plan(src, dst, device)
+        copy.start()
+        self.open.append(copy)
+        return copy
+
+    def drain(self):
+        for copy in self.open:
+            copy.wait_send()
+
+
+class Locals:
+    def __init__(self, sems):
+        self.sems, self.count = sems, 0
+
+    def start(self, src, dst):
+        copy = pltpu.make_async_copy(src, dst, self.sems.at[self.count])
+        self.count += 1
+        copy.start()
+        return copy
+
+
+class Line:
+    def __init__(self, place):
+        z = place.z
+        self.place = place
+        self.way = 1 - 2 * (z // 2)
+        self.inner = (z // 2) * (3 - z) + (1 - z // 2) * z
+
+    def off(self, end, inner):
+        return self.place.z + self.way * ((1 - self.inner) * end + self.inner * inner)
+
+    def near(self):
+        return self.off(1, -1)
+
+    def second(self):
+        return self.off(2, 1)
+
+    def third(self):
+        return self.off(3, 2)
+
+    def id(self, z):
+        return self.place.at(self.place.y, self.place.x, z, self.place.c)
+
+    def at_end(self, event):
+        pl.when(self.inner == 0)(event)
+
+    def at_inner(self, event):
+        pl.when(self.inner == 1)(event)
+
+
+class Spread:
+    def __init__(self, links, line, block, own=None):
+        z = line.place.z
+        mine = own if own is not None else lambda: block(z)
+
+        def here():
+            return block(z)
+
+        def second():
+            return block(line.second())
+
+        def third():
+            return block(line.third())
+
+        self.line = line
+        self.beside = links.plan(mine, here, lambda: line.id(line.near()))
+        self.across = links.plan(mine, here, lambda: line.id(line.second()))
+        self.far = links.plan(mine, here, lambda: line.id(line.second()))
+        self.hand_second = links.plan(second, second, lambda: line.id(line.near()))
+        self.hand_third = links.plan(third, third, lambda: line.id(line.near()))
+
+    def begin(self):
+        self.beside.start()
+        self.line.at_inner(self.across.start)
+        self.line.at_end(self.far.start)
+
+    def arrive_near(self, then=None):
+        self.beside.wait_recv()
+        if then:
+            then[0].start()
+
+    def arrive_inner(self, then=None):
+        @self.line.at_inner
+        def _():
+            self.across.wait_recv()
+            self.hand_second.start()
+            if then:
+                then[1].start()
+            self.far.wait_recv()
+            self.hand_third.start()
+            if then:
+                then[2].start()
+
+    def arrive_end(self, then=None):
+        @self.line.at_end
+        def _():
+            self.hand_second.wait_recv()
+            if then:
+                then[1].start()
+            self.hand_third.wait_recv()
+            if then:
+                then[2].start()
+
+    def drain(self):
+        self.beside.wait_send()
+
+        @self.line.at_inner
+        def _():
+            for copy in (self.across, self.hand_second, self.hand_third):
+                copy.wait_send()
+
+        self.line.at_end(self.far.wait_send)
+
+
+class Gather:
+    def __init__(self, links, place, line, block, own=None):
+        def plane(z):
+            return block(place.y, z)
+
+        self.spread = Spread(links, line, plane, own)
+        mine = own if own is not None else lambda: plane(place.z)
+        self.cross = links.plan(mine, lambda: plane(place.z), place.yid)
+        self.cross_on = [
+            links.plan(lambda at=at: plane(at()), lambda at=at: plane(at()), place.yid)
+            for at in (line.near, line.second, line.third)
+        ]
+
+    def begin(self):
+        self.spread.begin()
+        self.cross.start()
+
+    def forward(self):
+        self.spread.arrive_near(self.cross_on)
+        self.spread.arrive_inner(self.cross_on)
+
+    def late(self):
+        self.spread.arrive_end(self.cross_on)
+
+    def finish(self):
+        for copy in [self.cross] + self.cross_on:
+            copy.wait_recv()
+
+    def drain(self):
+        self.spread.drain()
+        for copy in [self.cross] + self.cross_on:
+            copy.wait_send()
+
+
+class GatherCross:
+    def __init__(self, links, place, line, block, own=None):
+        def plane(z):
+            return block(place.y, z)
+
+        def other(z):
+            return block(1 - place.y, z)
+
+        mine = own if own is not None else lambda: plane(place.z)
+        self.cross = links.plan(mine, lambda: plane(place.z), place.yid)
+        self.spread = Spread(links, line, plane, own)
+        self.spread_other = Spread(links, line, other)
+
+    def begin(self):
+        self.cross.start()
+        self.spread.begin()
+
+    def forward(self):
+        self.cross.wait_recv()
+        self.spread_other.begin()
+        self.spread.arrive_near()
+        self.spread.arrive_inner()
+
+    def late(self):
+        self.spread.arrive_end()
+        self.spread_other.arrive_near()
+        self.spread_other.arrive_inner()
+
+    def finish(self):
+        self.spread_other.arrive_end()
+
+    def drain(self):
+        self.cross.wait_send()
+        self.spread.drain()
+        self.spread_other.drain()
+
+
+def dot_nn(a, b):
+    return jnp.dot(a, b, preferred_element_type=WIDE)
+
+
+def dot_nt(a, b):
+    return lax.dot_general(a, b, (((1,), (1,)), ((), ())), preferred_element_type=WIDE)
+
+
+def dot_tn(a, b):
+    return lax.dot_general(a, b, (((0,), (0,)), ((), ())), preferred_element_type=WIDE)
+
+
+def fold_rows(values):
+    rows, cols = values.shape
+    return jnp.sum(values.reshape(rows // 8, 8, cols), axis=0)
+
+
+class Fold:
+    def __init__(self, links, line, block, land):
+        self.line, self.block, self.land = line, block, land
+
+        def to(at, where, slot):
+            return links.plan(lambda: block(at()), lambda: land(slot), lambda: line.id(where()))
+
+        self.beside = to(line.near, line.near, 0)
+        self.across = to(line.second, line.second, 1)
+        self.far = to(line.second, line.second, 2)
+        self.hand = to(line.third, line.near, 3)
+        self.handed = to(line.third, line.third, 1)
+
+    def send(self, k):
+        if k == 0:
+            self.line.at_end(self.hand.start)
+        if k == 1:
+            self.line.at_inner(self.across.start)
+            self.line.at_end(self.far.start)
+        if k == 2:
+            self.beside.start()
+
+    def hand_on(self):
+        @self.line.at_inner
+        def _():
+            self.hand.wait_recv()
+            block = self.block(self.line.third())
+            block[...] = (block[...].astype(WIDE) + self.land(3)[...].astype(WIDE)).astype(LOW)
+            self.handed.start()
+
+    def total(self, own, emit):
+        self.beside.wait_recv()
+
+        @self.line.at_end
+        def _():
+            self.handed.wait_recv()
+            emit(own() + self.land(0)[...].astype(WIDE) + self.land(1)[...].astype(WIDE))
+
+        @self.line.at_inner
+        def _():
+            self.across.wait_recv()
+            self.far.wait_recv()
+            total = own() + self.land(0)[...].astype(WIDE) + self.land(1)[...].astype(WIDE)
+            emit(total + self.land(2)[...].astype(WIDE))
+
+    def drain(self):
+        self.beside.wait_send()
+
+        @self.line.at_inner
+        def _():
+            self.across.wait_send()
+            self.handed.wait_send()
+
+        @self.line.at_end
+        def _():
+            self.far.wait_send()
+            self.hand.wait_send()
+
+
+class Scatter:
+    def __init__(self, links, place, line, theirs, mine, ybuf, zbuf):
+        self.place, self.line, self.mine, self.ybuf = place, line, mine, ybuf
+        self.order = [line.third, line.second, line.near, lambda: place.z]
+        self.ys = [
+            links.plan(lambda at=at: theirs(at()), lambda at=at: ybuf(at()), place.yid)
+            for at in self.order
+        ]
+        self.fold = Fold(links, line, ybuf, zbuf)
+
+    def begin(self):
+        for copy in self.ys:
+            copy.start()
+
+    def turn(self, k):
+        self.ys[k].wait_recv()
+        if k < 3:
+            at = self.order[k]()
+            land = self.ybuf(at)
+            land[...] = (land[...].astype(WIDE) + self.mine(at)[...].astype(WIDE)).astype(LOW)
+        self.fold.send(k)
+        if k == 2:
+            self.fold.hand_on()
+
+    def total(self, emit):
+        z = self.place.z
+        self.fold.total(
+            lambda: self.ybuf(z)[...].astype(WIDE) + self.mine(z)[...].astype(WIDE), emit
+        )
+
+    def drain(self):
+        for copy in self.ys:
+            copy.wait_send()
+        self.fold.drain()
+
+
+class ScatterCross:
+    def __init__(self, links, place, line, parts, zbuf, hold, land):
+        self.place, self.parts, self.hold, self.land = place, parts, hold, land
+        self.fold = Fold(links, line, parts, zbuf)
+        self.cross = links.plan(lambda: hold.at[1 - place.y], lambda: land, place.yid)
+
+    def begin(self):
+        for k in range(3):
+            self.fold.send(k)
+
+    def hand_on(self):
+        self.fold.hand_on()
+
+    def turn(self):
+        def emit(total):
+            self.hold[...] = total.astype(LOW)
+
+        self.fold.total(lambda: self.parts(self.place.z)[...].astype(WIDE), emit)
+        self.cross.start()
+
+    def total(self):
+        self.cross.wait_recv()
+        return self.hold[self.place.y].astype(WIDE) + self.land[...].astype(WIDE)
+
+    def drain(self):
+        self.cross.wait_send()
+        self.fold.drain()
+
+
+def layer_kernel(
+    ny, nz,
+    lens, tok, cot, mix_w, out_w, up_w, down_w, norms, freq, scale_in, dct, spread,
+    out_rows, grad_rows, gmix_out, gout_out, gup_out, gdown_out, gains_out,
+    xs, gs, nf, na, act, gp, feed, gxf, gm,
+    up, down, mix, outw, small, gains, meta, table, scale,
+    gdown, gout, gout_by, ydown, zdown, ymix, zmix,
+    zval, hval, yval, zout, hout, yout,
+    up_send, up_recv, mix_send, mix_recv, gacc, gsum, gy, g2, gz, g3, gm_sum,
+    send, recv, sems, sib_sems, own_sems, far_sems, sib_free, far_free, act_free,
+):
+    place = Places(ny, nz)
+    y, x, z, c = place.y, place.x, place.z, place.c
+    me = x * 2 + c
+    micro, span, width = xs.shape[1:]
+    shard = out_w.shape[0]
+    feed_shard = down_w.shape[0]
+    half = up.shape[-1]
+    quarter = half // 2
+    heads = width // HEAD // 4
+    group = heads * HEAD
+    none = jnp.zeros((), LOW)
+    local = Locals(sems)
+
+    def raw(n):
+        return feed.at[3, 0, pl.ds(n * shard, shard)]
+
+    def raw_load(weight, first):
+        count = weight.shape[1] // width
+        return [
+            local.start(weight.at[:, pl.ds(n * width, width)], raw(first + n)) for n in range(count)
+        ]
+
+    mix_load = raw_load(mix_w, 0)
+    up_load = raw_load(up_w, len(mix_load))
+    out_mine = local.start(out_w, outw.at[y, z // 2, z % 2, c])
+    tok_mine = local.start(tok, gp.at[0])
+    cot_mine = local.start(cot, gs.at[0])
+    down_mine = [
+        local.start(down_w.at[:, pl.ds(k * half, half)], down.at[k, y, z]) for k in range(2)
+    ]
+    place.signal()
+
+    row = lax.broadcasted_iota(jnp.int32, (8, 128), 0)
+    lane = lax.broadcasted_iota(jnp.int32, (8, 128), 1)
+    facts = jnp.zeros((8, 128), WIDE)
+    for s in range(micro):
+        for k in range(lens.shape[1]):
+            facts = jnp.where((row == 1 + s) & (lane == k), lens[s, k].astype(WIDE), facts)
+    at_row = lax.broadcasted_iota(jnp.int32, (shard, 128), 0)
+    at_lane = lax.broadcasted_iota(jnp.int32, (shard, 128), 1)
+    for k in range(4):
+        pick = jnp.where(at_lane == at_row + k * shard, 1.0, 0.0).astype(LOW)
+        facts = jnp.where(row == 0, facts + dot_nn(norms[k : k + 1, :], pick), facts)
+    small[y, x, z, c] = facts
+
+    def up_stage(q):
+        return gdown.at[:, q, pl.ds(0, shard), pl.ds(0, half)]
+
+    def mix_stage(t, q):
+        return gdown.at[0, q, pl.ds((t + 1) * shard, shard), pl.ds(half, group)]
+
+    def raw_cols(base, first, count):
+        at = first % width
+        return raw(base + first // width)[:, at : at + count]
+
+    for copy in mix_load:
+        copy.wait()
+    pair = group // ny
+    for q in range(4):
+        for t in range(3):
+            for by in range(ny):
+                first = t * width + ((by * 2 + q // 2) * 2 + q % 2) * pair
+                mix_stage(t, q)[:, by * pair : (by + 1) * pair] = raw_cols(0, first, pair)
+    for copy in up_load:
+        copy.wait()
+    for q in range(4):
+        for by in range(ny):
+            for bz in range(nz):
+                first = (((by * 2 + q // 2) * nz + bz) * 2 + q % 2) * feed_shard
+                cols = slice(bz * feed_shard, (bz + 1) * feed_shard)
+                up_stage(q)[by, :, cols] = raw_cols(len(mix_load), first, feed_shard)
+    up[:, y, x, z, c] = up_stage(me)[...]
+    for t in range(3):
+        mix[t, y, x, z, c] = mix_stage(t, me)[...]
+    place.meet()
+    links = Links(send, recv)
+    line = Line(place)
+
+    def swap(src, dst):
+        copies = []
+        for r in (1, 2, 3):
+            mx, mc = place.member(r)
+            copies.append(links.start(src(mx * 2 + mc), dst, place.member_id(r)))
+        return copies
+
+    def landed(copies):
+        for copy in copies:
+            copy.wait_recv()
+
+    small_swaps = swap(lambda q: small.at[y, x, z, c], small.at[y, x, z, c])
+    mix_swaps = []
+    for t in range(3):
+        mix_swaps += swap(lambda q, t=t: mix_stage(t, q), mix.at[t, y, x, z, c])
+    up_swaps = swap(up_stage, up.at[:, y, x, z, c])
+    chunks = [GatherCross(links, place, line, lambda by, bz: outw.at[by, bz // 2, bz % 2, c])]
+    for t in range(3):
+        chunks.append(Gather(links, place, line, lambda by, bz, t=t: mix.at[t, by, :, bz]))
+    halves = [(k, pl.ds(h * quarter, quarter)) for k in range(2) for h in range(2)]
+    for k, cols in halves:
+        chunks.append(
+            Gather(
+                links, place, line,
+                lambda by, bz, k=k, cols=cols: up.at[k, by, :, bz, :, :, cols],
+            )
+        )
+    for k, cols in halves:
+        way = GatherCross if (k, cols) == halves[-1] else Gather
+        chunks.append(
+            way(links, place, line, lambda by, bz, k=k, cols=cols: down.at[k, by, bz, :, cols])
+        )
+    of_mix, of_up, of_down = range(1, 4), range(4, 8), range(8, 12)
+    ahead = 3
+    hurried = [3]
+
+    def turn_chunk(i):
+        chunks[i].forward()
+        if i and i - 1 not in hurried:
+            chunks[i - 1].late()
+        if i + ahead < len(chunks):
+            chunks[i + ahead].begin()
+
+    out_mine.wait()
+    chunks[0].begin()
+    tok_mine.wait()
+    tok_sib = links.start(gp.at[0], gp.at[1], place.member_id(1))
+    tok_far = links.start(gp.at[0], gp.at[2], place.member_id(2))
+    small_gather = Gather(links, place, line, lambda by, bz: small.at[by, :, bz])
+    landed(small_swaps)
+    small_gather.begin()
+    landed(mix_swaps)
+    chunks[1].begin()
+    chunks[2].begin()
+    cot_mine.wait()
+    at_place = lax.broadcasted_iota(jnp.int32, (span, 1), 0)
+    for s in range(micro):
+        used = lens[s, 0]
+        for k in range(1, lens.shape[1]):
+            used = used + lens[s, k]
+        gs[0, s] = jnp.where(at_place < used, gs[0, s], none)
+    cot_sib = links.start(gs.at[0], gs.at[1], place.member_id(1))
+    cot_far = links.start(gs.at[0], gs.at[2], place.member_id(2))
+
+    raw = lax.dot_general(
+        dct[...], freq[...], (((0,), (1,)), ((), ())),
+        precision=lax.Precision.HIGHEST, preferred_element_type=WIDE,
+    ) / math.sqrt(HEAD)
+    raw = raw.astype(LOW)
+    tile_row = lax.broadcasted_iota(jnp.int32, (HEAD, group), 0)
+    tile_col = lax.broadcasted_iota(jnp.int32, (HEAD, group), 1)
+    tiled = jnp.where(tile_col % HEAD == tile_row, 1.0, 0.0).astype(LOW)
+    wide_table = dot_tn(tiled, dot_nn(raw, tiled).astype(LOW))
+    block_row = lax.broadcasted_iota(jnp.int32, (group, group), 0) // HEAD
+    block_col = lax.broadcasted_iota(jnp.int32, (group, group), 1) // HEAD
+    table[...] = jnp.where(block_row == block_col, wide_table, 0.0).astype(LOW)
+    scale[...] = lax.dot_general(
+        jnp.broadcast_to(scale_in[...], (8, HEAD)), tiled.astype(WIDE), (((1,), (0,)), ((), ())),
+        precision=lax.Precision.HIGHEST, preferred_element_type=WIDE,
+    )
+
+    small_gather.forward()
+    small_gather.late()
+    turn_chunk(0)
+    small_gather.finish()
+    count = ny * 2 * nz * 2
+    packed = jnp.sum(jnp.where(row == 0, small[...].reshape(count, 8, 128), 0.0), axis=1)
+    packed = packed.astype(LOW)
+    pick_row = lax.broadcasted_iota(jnp.int32, (128, width), 0)
+    pick_col = lax.broadcasted_iota(jnp.int32, (128, width), 1) % shard
+    owner = lax.broadcasted_iota(jnp.int32, (count, width), 0)
+    owned = lax.broadcasted_iota(jnp.int32, (count, width), 1) // shard
+    for k in range(4):
+        pick = jnp.where(pick_row == pick_col + k * shard, 1.0, 0.0).astype(LOW)
+        part = jnp.where(owned == owner, dot_nn(packed, pick), 0.0)
+        gains[k : k + 1, :] = jnp.sum(part, axis=0, keepdims=True)
+    gacc[...] = jnp.zeros_like(gacc)
+
+    places = lax.broadcasted_iota(jnp.int32, (1, span), 1).astype(WIDE)
+    turn_row = lax.broadcasted_iota(jnp.int32, (ROT // 2, 1), 0)
+    inverse = jnp.zeros((ROT // 2, 1), WIDE)
+    for k in range(ROT // 2):
+        inverse = jnp.where(turn_row == k, 10000.0 ** (-2.0 * k / ROT), inverse)
+    fact_row = lax.broadcasted_iota(jnp.int32, (8, span), 0)
+    for r in range(4):
+        mx, mc = place.member(r)
+        facts = small[y, mx, z, mc]
+        for s in range(micro):
+            end = jnp.zeros((1, 1), WIDE)
+            segment = jnp.zeros((1, span), WIDE)
+            begin = jnp.zeros((1, span), WIDE)
+            for k in range(lens.shape[1]):
+                end = end + facts[1 + s : 2 + s, k : k + 1]
+                past = places >= end
+                segment = segment + jnp.where(past, 1.0, 0.0)
+                begin = jnp.where(past, end, begin)
+            angle = inverse * (places - begin)
+            meta[r, s, 0:8, :] = jnp.cos(angle)
+            meta[r, s, 8:16, :] = jnp.sin(angle)
+            valid = jnp.where(segment < lens.shape[1], 1.0, 0.0)
+            rest = jnp.where(fact_row == 0, segment, jnp.where(fact_row == 1, 1.0, 0.0))
+            meta[r, s, 16:24, :] = jnp.where(fact_row == 2, valid, rest)
+
+    def norm(j):
+        def body(i, carry):
+            s = i // (span // 128)
+            rs = pl.ds(pl.multiple_of(i % (span // 128) * 128, 128), 128)
+            values = gp[j, s, rs, :].astype(WIDE)
+            center = values - jnp.mean(values, axis=1, keepdims=True)
+            deviation = jnp.mean(center * center, axis=1, keepdims=True)
+            hat = center * lax.rsqrt(deviation + epsilon)
+            na[j, s, rs, :] = (hat * gains[0:1, :] + gains[1:2, :]).astype(LOW)
+            nf[j, s, rs, :] = (hat * gains[2:3, :] + gains[3:4, :]).astype(LOW)
+            xs[j, s, rs, :] = hat.astype(LOW)
+            return carry
+
+        lax.fori_loop(0, micro * span // 128, body, 0)
+
+    def loop(first, last, body, events):
+        def step(i, carry):
+            def pump(part):
+                for (at, which), event in events.items():
+                    if which == part:
+
+                        @pl.when(i == at)
+                        def _(event=event):
+                            event()
+
+            body(i, pump)
+            return carry
+
+        lax.fori_loop(first, last, step, 0)
+
+    head_lane = lax.broadcasted_iota(jnp.int32, (1, group), 1)
+    of_head = [head_lane // HEAD == h for h in range(heads)]
+    low_lane = lax.broadcasted_iota(jnp.int32, (1, 128), 1) % HEAD < ROT // 2
+    key_at = lax.broadcasted_iota(jnp.int32, (span, span), 1)
+    query_at = lax.broadcasted_iota(jnp.int32, (span, span), 0)
+    wide_mix = 3 * group
+
+    def turn(values, cosine, sine):
+        parts = []
+        for first in range(0, group, 128):
+            part = values[:, first : first + 128]
+            other = jnp.where(
+                low_lane, pltpu.roll(part, 128 - ROT // 2, 1), pltpu.roll(part, ROT // 2, 1)
+            )
+            parts.append(part * cosine + other * sine)
+        return jnp.concatenate(parts, axis=1)
+
+    def spread_meta(j, s, first, last):
+        return lax.dot_general(
+            meta[j, s], spread[:, first:last], (((0,), (0,)), ((), ())),
+            precision=lax.Precision.HIGHEST, preferred_element_type=WIDE,
+        )
+
+    def attend_forward(j, s):
+        rows = na[j, s]
+        turns = spread_meta(j, s, 0, 384)
+        cosine, sine, owner = turns[:, :128], turns[:, 128:256], turns[:, 256:384]
+        owner = jnp.concatenate([owner, owner], axis=1)
+        allowed = (owner == meta[j, s, 16:17, :]) & (key_at <= query_at)
+        query, key, value = (dot_nn(rows, mix[t].reshape(width, group)) for t in range(3))
+        query = turn(query, cosine, sine).astype(LOW)
+        key = turn(key, cosine, sine).astype(LOW)
+        value = value.astype(LOW)
+        raised_query = scale[0:1, :] * jnp.exp(dot_nn(query, table[...]))
+        raised_key = scale[0:1, :] * jnp.exp(dot_nn(key, table[...]))
+        phi_query = raised_query.astype(LOW)
+        phi_key = raised_key.astype(LOW)
+        scores, totals = [], []
+        numer = jnp.zeros((span, group), WIDE)
+        total = jnp.zeros((span, group), WIDE)
+        for h in range(heads):
+            score = dot_nt(jnp.where(of_head[h], phi_query, none), phi_key)
+            score = jnp.where(allowed, score, 0.0)
+            totals.append(jnp.sum(score, axis=1, keepdims=True))
+            scores.append(score.astype(LOW))
+            numer += dot_nn(scores[h], jnp.where(of_head[h], value, none))
+            total = jnp.where(of_head[h], totals[h], total)
+        att = (numer / total).astype(LOW)
+        gm[j, s, :, wide_mix:] = att
+        feed[j, s] = dot_nn(att, outw[:, c].reshape(group, width)).astype(LOW)
+        return (cosine, sine, allowed, raised_query, raised_key, phi_query, phi_key, value,
+                scores, totals, numer, total)
+
+    def attend_back(j, s, kept):
+        (cosine, sine, allowed, raised_query, raised_key, phi_query, phi_key, value,
+         scores, totals, numer, total) = kept
+        grad_att = dot_nt(gs[j, s], outw[:, c].reshape(group, width))
+        grad_numer = (grad_att / total).astype(LOW)
+        product = grad_att * numer
+        grad_query = jnp.zeros((span, group), WIDE)
+        grad_key = jnp.zeros((span, group), WIDE)
+        grad_value = jnp.zeros((span, group), WIDE)
+        for h in range(heads):
+            grad_total = -jnp.sum(jnp.where(of_head[h], product, 0.0), axis=1, keepdims=True)
+            grad_total = grad_total / (totals[h] * totals[h])
+            numer_h = jnp.where(of_head[h], grad_numer, none)
+            grad_score = dot_nt(numer_h, value) + grad_total
+            grad_score = jnp.where(allowed, grad_score, 0.0).astype(LOW)
+            grad_query += dot_nn(grad_score, jnp.where(of_head[h], phi_key, none))
+            grad_key += dot_tn(grad_score, jnp.where(of_head[h], phi_query, none))
+            grad_value += dot_tn(scores[h], numer_h)
+        back_query = turn(
+            dot_nt((grad_query * raised_query).astype(LOW), table[...]), cosine, -sine
+        )
+        back_key = turn(dot_nt((grad_key * raised_key).astype(LOW), table[...]), cosine, -sine)
+        parts = (back_query.astype(LOW), back_key.astype(LOW), grad_value.astype(LOW))
+        grad_normed = jnp.zeros((span, width), WIDE)
+        for t in range(3):
+            gm[j, s, :, t * group : (t + 1) * group] = parts[t]
+            grad_normed += dot_nt(parts[t], mix[t].reshape(width, group))
+        gacc[0:8, :] += fold_rows(grad_normed * xs[j, s].astype(WIDE))
+        gacc[8:16, :] += fold_rows(grad_normed)
+        gxf[j, s] = (grad_normed * gains[0:1, :]).astype(LOW)
+
+    def attend(j, pump):
+        pump(0)
+        kept = [attend_forward(j, s) for s in range(micro)]
+        pump(1)
+        for s in range(micro):
+            attend_back(j, s, kept[s])
+        pump(2)
+
+    def hidden(k):
+        def body(i, pump):
+            j, s = i // micro, i % micro
+            pump(0)
+            h = dot_nn(nf[j, s], up[k].reshape(width, half))
+            cdf = 0.5 * (1.0 + lax.erf(h * math.sqrt(0.5)))
+            pdf = jnp.exp(-0.5 * h * h) * (1.0 / math.sqrt(2.0 * math.pi))
+            act[j, s, :, pl.ds(k * half, half)] = (h * cdf).astype(LOW)
+            gp[j, s, :, pl.ds(k * half, half)] = (cdf + h * pdf).astype(LOW)
+
+        return body
+
+    rest = 4 * micro * span
+    blocks = width // 256
+
+    def other_first(i):
+        return (i + (1 - y) * (blocks // 2)) % blocks
+
+    def outer(a, b, first, last, store):
+        def body(i, carry):
+            at = other_first(i)
+            cols = pl.ds(pl.multiple_of(at * 256, 256), 256)
+            store(at, dot_tn(a[:, :, :, cols].reshape(rest, 256), b().reshape(rest, -1)))
+            return carry
+
+        lax.fori_loop(first, last, body, 0)
+
+    def keep_down(at, part):
+        per = 256 // feed_shard
+        for k in range(per):
+            block = at * per + k
+            rows = slice(k * feed_shard, (k + 1) * feed_shard)
+            gdown[block // nz, block % nz] = part[rows].astype(LOW)
+
+    def keep_up(at, part):
+        xs[at, 0] = part.astype(LOW)
+
+    def up_block(ref, first, s, at):
+        size = 2 * shard
+        return ref.at[pl.ds(first, 2), s, pl.ds(pl.multiple_of(at * size, size), size)]
+
+    def keep_mix(at, part):
+        for t in range(3):
+            cols = part[:, t * group : (t + 1) * group].astype(LOW)
+            mix[t, at // 2, at % 2] = cols.reshape(nz, 2, shard, group)
+
+    def outer_down(first, last):
+        outer(act, lambda: gs[...], first, last, keep_down)
+
+    def outer_up(first, last):
+        outer(nf, lambda: gp[...], first, last, keep_up)
+
+    def outer_mix(first, last):
+        outer(na, lambda: gm[:, :, :, 0:wide_mix], first, last, keep_mix)
+
+    down_sum = Scatter(
+        links, place, line, lambda at: gdown.at[1 - y, at], lambda at: gdown.at[y, at],
+        lambda at: ydown.at[at], lambda k: zdown.at[k],
+    )
+    up_sum = Scatter(
+        links, place, line, lambda at: up_block(xs, (1 - y) * 2, 0, at),
+        lambda at: up_block(xs, y * 2, 0, at), lambda at: up_block(act, 0, 0, at),
+        lambda k: up_block(act, 0, 1, k),
+    )
+    two = pl.ds(0, 2)
+    mix_sum = Scatter(
+        links, place, line, lambda at: mix.at[two, 1 - y, :, at],
+        lambda at: mix.at[two, y, :, at], lambda at: ymix.at[at], lambda k: zmix.at[k],
+    )
+    val_sum = ScatterCross(
+        links, place, line, lambda at: mix.at[2, :, :, at], lambda k: zval.at[k], hval, yval
+    )
+    out_sum = ScatterCross(
+        links, place, line, lambda at: gout_by.at[:, at // 2, at % 2], lambda k: zout.at[k],
+        hout, yout,
+    )
+
+    landed(up_swaps)
+    turn_chunk(1)
+    norm(0)
+    landed([tok_sib])
+    norm(1)
+    turn_chunk(2)
+    chunks[0].finish()
+    out_here = outw.at[:, 1 - c, :, c]
+    out_swap = links.start(out_here, out_here, place.member_id(1))
+    turn_chunk(3)
+    for copy in down_mine:
+        copy.wait()
+    landed([out_swap, cot_sib])
+    chunks[3].late()
+    for i in of_mix:
+        chunks[i].finish()
+    tok_fwd = links.plan(gp.at[2], gp.at[3], partial(place.member_id, 1))
+
+    def take_tokens():
+        tok_far.wait_recv()
+        tok_fwd.start()
+
+    loop(
+        0, 2, attend,
+        {
+            (0, 1): lambda: (turn_chunk(4), take_tokens()),
+            (0, 2): lambda: turn_chunk(5),
+            (1, 1): lambda: turn_chunk(6),
+            (1, 2): lambda: turn_chunk(7),
+        },
+    )
+    norm(2)
+    landed([tok_fwd])
+    norm(3)
+    for copy in (tok_sib, tok_far, tok_fwd):
+        copy.wait_send()
+    for i in of_up[:2]:
+        chunks[i].finish()
+    loop(0, 4 * micro, hidden(0), {})
+    turn_chunk(8)
+    landed([cot_far])
+    cot_fwd = links.start(gs.at[2], gs.at[3], place.member_id(1))
+    for copy in mix_swaps + up_swaps:
+        copy.wait_send()
+    landed([cot_fwd])
+
+    loop(
+        2, 4, attend,
+        {
+            (2, 1): lambda: turn_chunk(9),
+            (2, 2): lambda: turn_chunk(10),
+            (3, 1): lambda: turn_chunk(11),
+        },
+    )
+    for i in of_mix:
+        chunks[i].drain()
+    outer_mix(0, blocks // 2)
+    mix_sum.begin()
+    outer_mix(blocks // 2, blocks)
+    val_sum.begin()
+    part = dot_tn(gm[:, :, :, wide_mix:].reshape(rest, group), gs[...].reshape(rest, width))
+    gout[...] = part.astype(LOW).reshape(gout.shape)
+    grad_swap = links.start(gout.at[:, :, 1 - c], gout_by.at[:, c], place.member_id(1))
+    gout_by[:, c] = gout[:, :, c]
+    for sem, r in ((sib_free, 1), (far_free, 2)):
+        pl.semaphore_signal(sem, inc=1, device_id=place.member_id(r), device_id_type=MESH_ID)
+    for i in of_up[2:]:
+        chunks[i].finish()
+    loop(0, 4 * micro, hidden(1), {})
+    landed([grad_swap])
+    out_sum.begin()
+    val_sum.hand_on()
+    outer_down(0, blocks // 2)
+    down_sum.begin()
+    mix_sum.turn(0)
+    chunks[of_down[-1]].late()
+    for i in of_down:
+        chunks[i].finish()
+    for sem in (sib_free, far_free):
+        pl.semaphore_wait(sem, 1)
+
+    def rows_copy(sem, j, r, land):
+        def copy(s, kind):
+            buf = (feed, gxf)[kind]
+            return pltpu.make_async_remote_copy(
+                buf.at[j, s], land(kind, s), sem.at[0, kind, s], sem.at[1, kind, s],
+                device_id=place.member_id(r), device_id_type=MESH_ID,
+            )
+
+        return copy
+
+    sib_copy = rows_copy(sib_sems, 3, 1, lambda kind, s: gm.at[2 + kind, s])
+    far_copy = rows_copy(far_sems, 2, 2, lambda kind, s: na.at[kind, s])
+    own_copy = rows_copy(own_sems, 1, 1, lambda kind, s: gm.at[kind, s])
+
+    def hand_on(j, s, value, kind):
+        buf = (feed, gxf)[kind]
+
+        @pl.when(j != 2)
+        def _():
+            buf[j, s] = value.astype(LOW)
+
+        @pl.when(j == 3)
+        def _():
+            sib_copy(s, kind).start()
+
+        @pl.when(j == 2)
+        def _():
+            sib_copy(s, kind).wait_recv()
+            buf[j, s] = (value + gm[2 + kind, s].astype(WIDE)).astype(LOW)
+            far_copy(s, kind).start()
+
+        @pl.when(j == 1)
+        def _():
+            own_copy(s, kind).start()
+
+    def back(i, pump):
+        late, r = i // 4, i % 4
+        j = (1 - late) * (3 - r % 2) + late * (1 - r // 2)
+        s = (1 - late) * (r // 2) + late * (r % 2)
+        pump(0)
+        rows = act[j, s]
+        sums = [dot_nn(rows, down[k].reshape(2 * half, half)) for k in range(2)]
+        hand_on(j, s, jnp.concatenate(sums, axis=1) + feed[j, s].astype(WIDE), 0)
+        ga = dot_nt(gs[j, s, :, 0:half], down[0].reshape(2 * half, half))
+        ga += dot_nt(gs[j, s, :, half : 2 * half], down[1].reshape(2 * half, half))
+        gh = (ga * gp[j, s].astype(WIDE)).astype(LOW)
+        gp[j, s] = gh
+        gn = dot_nt(gh[:, :half], up[0].reshape(width, half))
+        gn += dot_nt(gh[:, half:], up[1].reshape(width, half))
+        gacc[16:24, :] += fold_rows(gn * xs[j, s].astype(WIDE))
+        gacc[24:32, :] += fold_rows(gn)
+        hand_on(j, s, gn * gains[2:3, :] + gxf[j, s].astype(WIDE), 1)
+
+    loop(
+        0, 4 * micro, back,
+        {
+            (0, 0): lambda: out_sum.hand_on(),
+            (1, 0): lambda: mix_sum.turn(1),
+            (2, 0): lambda: mix_sum.turn(2),
+            (3, 0): lambda: mix_sum.turn(3),
+            (5, 0): lambda: val_sum.turn(),
+            (6, 0): lambda: out_sum.turn(),
+        },
+    )
+
+    gsum[...] = jnp.zeros_like(gsum)
+    for k in range(4):
+        gsum[k : k + 1, :] = jnp.sum(gacc[8 * k : 8 * k + 8, :], axis=0, keepdims=True)
+    gain_y = links.start(gsum, gy, place.yid())
+    own_again = local.start(tok, na.at[2])
+    outer_down(blocks // 2, blocks)
+    for one in [place.yid()] + [place.zid(step) for step in range(1, nz)]:
+        pl.semaphore_signal(act_free, inc=1, device_id=one, device_id_type=MESH_ID)
+    outer_up(0, blocks // 2)
+    pl.semaphore_wait(act_free, nz)
+    up_sum.begin()
+    for k in range(3):
+        down_sum.turn(k)
+    outer_up(blocks // 2, blocks)
+    landed([gain_y])
+    g2[...] = gsum[...] + gy[...]
+    gain_zs = [links.start(g2, gz.at[step - 1], place.zid(step)) for step in range(1, nz)]
+
+    def finish(s, carry):
+        for kind in (0, 1):
+            own_copy(s, kind).wait_recv()
+            far_copy(s, kind).wait_recv()
+        keep = spread_meta(0, s, 384, 512)[:, :1]
+        values = na[2, s].astype(WIDE)
+        added = feed[0, s].astype(WIDE) + gm[0, s].astype(WIDE) + na[0, s].astype(WIDE)
+        feed[0, s] = (values + keep * added).astype(LOW)
+        grad = gxf[0, s].astype(WIDE) + gm[1, s].astype(WIDE) + na[1, s].astype(WIDE)
+        center = values - jnp.mean(values, axis=1, keepdims=True)
+        rate = lax.rsqrt(jnp.mean(center * center, axis=1, keepdims=True) + epsilon)
+        hat = center * rate
+        inner = jnp.mean(grad * hat, axis=1, keepdims=True)
+        grad = grad - jnp.mean(grad, axis=1, keepdims=True) - hat * inner
+        gxf[0, s] = (rate * grad).astype(LOW)
+        return carry
+
+    def put_up(qx, qc, values):
+        for by in range(ny):
+            rows = pl.ds(pl.multiple_of((by * 2 + qx) * shard, shard), shard)
+            for bz in range(nz):
+                first = (bz * 2 + qc) * feed_shard
+                cols = pl.ds(pl.multiple_of(first, feed_shard), feed_shard)
+                at = (by * nz + bz) * feed_shard
+                nf[0, 0, rows, cols] = values[:, at : at + feed_shard]
+
+    def put_mix(qx, qc, values):
+        for t in range(3):
+            for by in range(ny):
+                first = ((by * 2 + qx) * 2 + qc) * pair
+                cols = pl.ds(pl.multiple_of(first, pair), pair)
+                nf[0, 1, t * shard : (t + 1) * shard, cols] = values[t, :, by * pair : (by + 1) * pair]
+
+    def put_out(first, dst):
+        count = dst.shape[1] // width
+        return [
+            local.start(nf.at[0, first, pl.ds(n * shard, shard)], dst.at[:, pl.ds(n * width, width)])
+            for n in range(count)
+        ]
+
+    def share(hold, at, land):
+        copies = []
+        for r in (1, 2, 3):
+            mx, mc = place.member(r)
+            copies.append(links.start(at(hold, mx, mc), land.at[r - 1], place.member_id(r)))
+        return copies
+
+    def of_mix_share(hold, mx, mc):
+        return hold.at[:, mx, mc]
+
+    def of_up_share(hold, mx, mc):
+        return hold.at[mx, pl.ds(pl.multiple_of(mc * shard, shard), shard)]
+
+    def collect(copies, hold, at, land, put):
+        put(x, c, at(hold, x, c)[...])
+        for r in (1, 2, 3):
+            mx, mc = place.member(r)
+            copies[r - 1].wait_recv()
+            put(mx, mc, land[r - 1])
+
+    def keep_sum(hold):
+        def emit(total):
+            hold[...] = total.astype(LOW)
+
+        return emit
+
+    mix_sum.total(keep_sum(mix_send.at[two]))
+    mix_send[2] = val_sum.total().astype(LOW)
+    mix_shares = share(mix_send, of_mix_share, mix_recv)
+    down_sum.turn(3)
+    nf[1, 1, 0:shard, :] = out_sum.total().astype(LOW)
+    written = [local.start(nf.at[1, 1, pl.ds(0, shard)], gout_out)]
+    collect(mix_shares, mix_send, of_mix_share, mix_recv, put_mix)
+    written += put_out(1, gmix_out)
+    up_sum.turn(0)
+    landed(gain_zs)
+    g3[...] = g2[...] + sum(gz[step - 1] for step in range(1, nz))
+    gain_ms = [links.start(g3, gm_sum.at[r - 1], place.member_id(r)) for r in (1, 2, 3)]
+    up_sum.turn(1)
+    up_sum.turn(2)
+    down_sum.total(keep_sum(nf.at[1, 0, pl.ds(0, feed_shard)]))
+    written.append(local.start(nf.at[1, 0, pl.ds(0, feed_shard)], gdown_out))
+    own_again.wait()
+    lax.fori_loop(0, micro, finish, 0)
+    rows_out = local.start(feed.at[0], out_rows)
+    grads_out = local.start(gxf.at[0], grad_rows)
+    up_sum.turn(3)
+    landed(gain_ms)
+    totals = g3[...] + gm_sum[0] + gm_sum[1] + gm_sum[2]
+    mine = ((y * 2 + x) * nz + z) * 2 + c
+    pick_row = lax.broadcasted_iota(jnp.int32, (width, shard), 0) - mine * shard
+    pick_col = lax.broadcasted_iota(jnp.int32, (width, shard), 1)
+    gains_out[...] = lax.dot_general(
+        totals, jnp.where(pick_row == pick_col, 1.0, 0.0), (((1,), (0,)), ((), ())),
+        precision=lax.Precision.HIGHEST, preferred_element_type=WIDE,
+    )
+    up_sum.total(keep_sum(up_send))
+    up_shares = share(up_send, of_up_share, up_recv)
+    collect(up_shares, up_send, of_up_share, up_recv, put_up)
+    written += put_out(0, gup_out)
+    for copy in written + [rows_out, grads_out]:
+        copy.wait()
+    links.drain()
+    for one in chunks + [small_gather, down_sum, up_sum, mix_sum, val_sum, out_sum]:
+        one.drain()
+    for kind in (0, 1):
+        for s in range(micro):
+            sib_copy(s, kind).wait_send()
+            far_copy(s, kind).wait_send()
+            own_copy(s, kind).wait_send()
+
+
+VMEM = pl.BlockSpec(memory_space=pltpu.VMEM)
+SMEM = pl.BlockSpec(memory_space=pltpu.SMEM)
+ANY = pl.BlockSpec(memory_space=pl.ANY)
+SHAPE = jax.ShapeDtypeStruct
+LIMIT = 59 * 2**20
+
+
+def cosine_basis():
+    order, sample = np.arange(HEAD)[:, None], np.arange(HEAD)[None, :]
+    factor = np.where(order == 0, math.sqrt(1.0 / HEAD), math.sqrt(2.0 / HEAD))
+    return (factor * np.cos(math.pi * (2 * sample + 1) * order / (2 * HEAD))).astype(np.float32)
+
+
+def spread_rows():
+    row = np.arange(24)[:, None]
+    lane = np.arange(512)[None, :]
+    part, dim = lane // 128, lane % HEAD
+    half = ROT // 2
+    cosine = (part == 0) & (dim < ROT) & (row == dim % half)
+    cosine = cosine | ((part == 0) & (dim >= ROT) & (row == 17))
+    sine = (part == 1) & (dim < ROT) & (row == half + dim % half)
+    rest = ((part == 2) & (row == 16)) | ((part == 3) & (row == 18))
+    sign = np.where((part == 1) & (dim < half), -1.0, 1.0)
+    return np.where(cosine | sine | rest, sign, 0.0).astype(np.float32)
+
+
+def per_device_group(
+    ny,
+    nz,
+    tokens,
+    lengths,
+    mix_weight,
+    out_weight,
+    up_weight,
+    down_weight,
+    attn_gain,
+    attn_bias,
+    feed_gain,
+    feed_bias,
+    feature_freq,
+    feature_scale,
+    cotangent,
+):
+    micro, span, width = tokens.shape
+    shard = mix_weight.shape[0]
+    feed_shard = down_weight.shape[0]
+    group = width // 4
+    hidden = feed_shard * ny * nz
+    half = hidden // 2
+    norms = jnp.stack([attn_gain, attn_bias, feed_gain, feed_bias])
+
+    dma = pltpu.SemaphoreType.DMA
+    whole = pltpu.VMEM((4, micro, span, width), LOW)
+
+    def low(*shape):
+        return pltpu.VMEM(shape, LOW)
+
+    def wide(*shape):
+        return pltpu.VMEM(shape, WIDE)
+
+    out_rows, grad_rows, gmix, gout, gup, gdown, gains = pl.pallas_call(
+        partial(layer_kernel, ny, nz),
+        out_shape=[
+            SHAPE((micro, span, width), LOW),
+            SHAPE((micro, span, width), LOW),
+            SHAPE(mix_weight.shape, LOW),
+            SHAPE(out_weight.shape, LOW),
+            SHAPE(up_weight.shape, LOW),
+            SHAPE(down_weight.shape, LOW),
+            SHAPE((8, shard), WIDE),
+        ],
+        in_specs=[SMEM] + [ANY] * 6 + [VMEM] * 5,
+        out_specs=[ANY] * 6 + [VMEM],
+        scratch_shapes=[whole] * 9
+        + [
+            low(2, ny, 2, nz, 2, shard, half),
+            low(2, ny, nz, feed_shard, half),
+            low(3, ny, 2, nz, 2, shard, group),
+            low(ny, nz // 2, 2, 2, shard, width),
+            wide(ny, 2, nz, 2, 8, 128),
+            wide(8, width),
+            wide(4, micro, 24, span),
+            low(group, group),
+            wide(8, group),
+            low(ny, nz, feed_shard, width),
+            low(ny, 2, 2, shard, width),
+            low(ny, nz // 2, 2, shard, width),
+            low(nz, feed_shard, width),
+            low(4, feed_shard, width),
+            low(nz, 2, 2, 2, shard, group),
+            low(4, 2, 2, 2, shard, group),
+            low(4, ny, 2, 2, shard, group),
+            low(ny, 2, 2, shard, group),
+            low(2, 2, shard, group),
+            low(4, ny, shard, width),
+            low(ny, shard, width),
+            low(shard, width),
+            low(2, 2 * shard, hidden),
+            low(3, shard, hidden),
+            low(3, 2, 2, shard, group),
+            low(3, 3, shard, group),
+            wide(32, width),
+            wide(8, width),
+            wide(8, width),
+            wide(8, width),
+            wide(nz - 1, 8, width),
+            wide(8, width),
+            wide(3, 8, width),
+            dma((200,)),
+            dma((200,)),
+            dma((28,)),
+            dma((2, 2, 2)),
+            dma((2, 2, 2)),
+            dma((2, 2, 2)),
+            pltpu.SemaphoreType.REGULAR,
+            pltpu.SemaphoreType.REGULAR,
+            pltpu.SemaphoreType.REGULAR,
+        ],
+        name="layer",
+        cost_estimate=pl.CostEstimate(flops=45 * 10**9, bytes_accessed=20 * 10**6, transcendentals=0),
+        compiler_params=pltpu.CompilerParams(
+            collective_id=0, has_side_effects=True, vmem_limit_bytes=LIMIT
+        ),
+    )(
+        lengths[:, 0], tokens, cotangent, mix_weight, out_weight, up_weight, down_weight, norms,
+        feature_freq, feature_scale[None], cosine_basis(), spread_rows(),
+    )
+    return (
+        out_rows,
+        cotangent.astype(WIDE) + grad_rows.astype(WIDE),
+        gmix.astype(WIDE),
+        gout.astype(WIDE),
+        gup.astype(WIDE),
+        gdown.astype(WIDE),
+        gains[0],
+        gains[1],
+        gains[2],
+        gains[3],
+    )
+
+
 def solution(mesh):
-    placed = (
-        P(None, ("dp", "fsdp"), None),
-        P(None, ("dp", "fsdp"), None),
-        P(("dp", "fsdp"), None),
-        P(("dp", "fsdp"), None),
-        P(("dp", "fsdp"), None),
-        P(("dp", "fsdp"), None),
-        P(("dp", "fsdp")),
-        P(("dp", "fsdp")),
-        P(("dp", "fsdp")),
-        P(("dp", "fsdp")),
-        P(),
-        P(),
-        P(None, ("dp", "fsdp"), None),
-    )
+    ny, nz = mesh.shape["dp"] // 2, mesh.shape["fsdp"] // 2
+    grouped = ny == 2 and nz == 4 and D // mesh.size % 32 == 0
+    body = partial(per_device_group, ny, nz) if grouped else per_device_plain
+    rows = P(("dp", "fsdp"), None)
+    vector = P(("dp", "fsdp"))
+    slots = P(None, ("dp", "fsdp"), None)
     return jax.shard_map(
-        per_device,
+        body,
         mesh=mesh,
-        in_specs=placed,
-        out_specs=(
-            P(None, ("dp", "fsdp"), None),
-            P(None, ("dp", "fsdp"), None),
-            P(("dp", "fsdp"), None),
-            P(("dp", "fsdp"), None),
-            P(("dp", "fsdp"), None),
-            P(("dp", "fsdp"), None),
-            P(("dp", "fsdp")),
-            P(("dp", "fsdp")),
-            P(("dp", "fsdp")),
-            P(("dp", "fsdp")),
-        ),
+        in_specs=(slots, slots, *[rows] * 4, *[vector] * 4, P(), P(), slots),
+        out_specs=(slots, slots, *[rows] * 4, *[vector] * 4),
         check_vma=False,
     )

time: 1080 us -> 194 us (0.18); the launches traced: 1060 us -> 194 us
  matrix products: 468 us -> 0 us
  waiting for transfers between devices: 440 us -> 0 us
  Pallas kernels: 0 us -> 184 us
  blocking collectives: 82.4 us -> 0 us
  local copies, waits for them, and re-layouts: 40.1 us -> 2.34 us
  between operations: 15.6 us -> 0.68 us
    dot_general x289 -> x0, matrix products: 468 us -> none  [the longest x32 53.9 us: attend_back(): jnp.einsum('qk,qf->kf', grad_scores, mapped_query, preferred_element_type...]
    reduce_scatter x4 -> x0, waiting for transfers between devices: 363 us -> none  [the longest x1 187 us: reduce_feed(): lax.psum_scatter(grads[1], ('dp', 'fsdp'), scatter_dimension=0, tiled=True)]
    pallas_call x0 -> x1, Pallas kernels: none -> 184 us  [per_device_group(): pl.pallas_call(partial(layer_kernel, ny, nz), out_shape=[SHAPE((micro, sp...]
    unnamed x2 -> x0, blocking collectives: 82.4 us -> none
    all_gather x4 -> x0, waiting for transfers between devices: 74.6 us -> none  [the longest x1 65.8 us: fetch_attention(): lax.all_gather(shards[0], ('dp', 'fsdp'), axis=0, tiled=True)]
    unnamed x146 -> x13, local copies, waits for them, and re-layouts: 21.6 us -> 0.99 us
  transfers between devices with their start and end apart: 8 -> 0, of which waited for: 4 -> 0; matrix products, arithmetic and copies ran while one was open for 48% -> 0% of each run, Pallas kernels for 0% -> 0%
where the time goes in v2:
time: 194 us
  Pallas kernels  184 us (95%)
  other arithmetic  7.39 us (4%)
  local copies, waits for them, and re-layouts  2.34 us (1%)
    pallas_call x1, Pallas kernels, per_device_group(): pl.pallas_call(partial(layer_kernel, ny, nz), out_shape=[SHAPE((micro, sp...  184 us

profile of v2, /device:TPU:0, one launch (start us, length us, event | category | flops | bytes accessed | tf_op | source)
XLA Modules:
  0.0 194.2 jit_solution(18306181053135131271)
XLA Ops:
  0.6 1.3 pad_maximum_fusion.norms
  1.9 0.0 copy-start.1
  1.9 183.8 %layer.1 = (bf16[2,256,1024]{2,1,0:T(8,128)(2,1)}, bf16[2,256,1024]{2,1,0:T(8,128)(2,1)}, bf16[32,3072]{1,0:T(8,128)(2,1)}, bf16[32,1024]{1,0:T(8,128)(2,1)}, bf...) custom-call(s32[2,4]{1,0:T(2,128)} %bitcast.18, bf16[2,256,1024]{2,1,0:T(8,128)(2,1)} %tok.1, ...), custom_call_target="tpu_custom_call" | custom-call | flops 44999999488 | bytes 20000000 | tf_op jit(solution)/shard_map/layer/pallas_call | solution.py:1451
  185.7 1.3 slice_bitcast_fusion
  187.1 0.0 copy-done.1
  187.1 0.0 copy-start.3
  187.1 0.0 copy-start.2
  187.1 0.0 copy-start.4
  187.1 3.0 %convert_add_fusion = f32[2,256,1024]{2,1,0:T(8,128)} fusion(bf16[2,256,1024]{2,1,0:T(8,128)(2,1)} %get-tuple-element.18, bf16[2,256,1024]{2,1,0:T(8,128)(2,1)S(1)} %copy-done.1), kind=kLoop, calls=%fused_computation | loop fusion | flops 1572864 | bytes 4194304 | tf_op jit(solution)/shard_map/add | solution.py:1520
  190.1 0.0 copy-start.5
  190.1 0.0 copy-start
  190.1 0.0 copy-done.3
  190.1 0.8 convert_element_type.22
  190.9 0.0 copy-done.2
  190.9 0.8 convert_element_type.23
  191.8 0.0 copy-done.4
  191.8 0.8 convert_element_type.20
  192.5 0.0 copy-done.5
  192.5 0.7 convert_element_type.21
  193.2 0.0 copy-done
  193.2 1.0 copy.26
Async XLA Ops:
  1.9 185.1 %copy-start.1 = (bf16[2,256,1024]{2,1,0:T(8,128)(2,1)S(1)}, bf16[2,256,1024]{2,1,0:T(8,128)(2,1)}, u32[]{:S(2)}) copy-start(bf16[2,256,1024]{2,1,0:T(8,128)(2,1)} %cot.1) | copy-start | bytes 3145732
  187.1 3.0 %copy-start.3 = (bf16[32,4096]{1,0:T(8,128)(2,1)S(1)}, bf16[32,4096]{1,0:T(8,128)(2,1)}, u32[]{:S(2)}) copy-start(bf16[32,4096]{1,0:T(8,128)(2,1)} %get-tuple-element.21) | copy-start | bytes 786436
  187.1 3.9 %copy-start.2 = (bf16[128,1024]{1,0:T(8,128)(2,1)S(1)}, bf16[128,1024]{1,0:T(8,128)(2,1)}, u32[]{:S(2)}) copy-start(bf16[128,1024]{1,0:T(8,128)(2,1)} %get-tuple-element.22) | copy-start | bytes 786436
  187.1 4.7 %copy-start.4 = (bf16[32,3072]{1,0:T(8,128)(2,1)S(1)}, bf16[32,3072]{1,0:T(8,128)(2,1)}, u32[]{:S(2)}) copy-start(bf16[32,3072]{1,0:T(8,128)(2,1)} %get-tuple-element.19) | copy-start | bytes 589828
  190.1 2.5 %copy-start.5 = (bf16[32,1024]{1,0:T(8,128)(2,1)S(1)}, bf16[32,1024]{1,0:T(8,128)(2,1)}, u32[]{:S(2)}) copy-start(bf16[32,1024]{1,0:T(8,128)(2,1)} %get-tuple-element.20) | copy-start | bytes 196612
  190.1 3.1 %copy-start = (bf16[2,256,1024]{2,1,0:T(8,128)(2,1)S(1)}, bf16[2,256,1024]{2,1,0:T(8,128)(2,1)}, u32[]{:S(2)}) copy-start(bf16[2,256,1024]{2,1,0:T(8,128)(2,1)} %get-tuple-element.38) | copy-start | bytes 3145732

commit v3 on v2

--- a/solution.py
+++ b/solution.py
@@ -440,6 +440,7 @@
             return block(line.third())
 
         self.line = line
+        self.sources = [line.near, line.second, line.third]
         self.beside = links.plan(mine, here, lambda: line.id(line.near()))
         self.across = links.plan(mine, here, lambda: line.id(line.second()))
         self.far = links.plan(mine, here, lambda: line.id(line.second()))
@@ -489,17 +490,48 @@
         self.line.at_end(self.far.wait_send)
 
 
+class Direct:
+    def __init__(self, links, line, block, own=None):
+        place = line.place
+        self.sources = [partial(place.zsrc, step) for step in range(1, place.nz)]
+        mine = own if own is not None else lambda: block(place.z)
+        self.copies = [
+            links.plan(mine, lambda: block(place.z), partial(place.zid, step))
+            for step in range(1, place.nz)
+        ]
+
+    def begin(self):
+        for copy in self.copies:
+            copy.start()
+
+    def arrive_near(self, then=()):
+        for k, copy in enumerate(self.copies):
+            copy.wait_recv()
+            if then:
+                then[k].start()
+
+    def arrive_inner(self, then=None):
+        pass
+
+    def arrive_end(self, then=None):
+        pass
+
+    def drain(self):
+        for copy in self.copies:
+            copy.wait_send()
+
+
 class Gather:
-    def __init__(self, links, place, line, block, own=None):
+    def __init__(self, links, place, line, block, own=None, way=Spread):
         def plane(z):
             return block(place.y, z)
 
-        self.spread = Spread(links, line, plane, own)
+        self.spread = way(links, line, plane, own)
         mine = own if own is not None else lambda: plane(place.z)
         self.cross = links.plan(mine, lambda: plane(place.z), place.yid)
         self.cross_on = [
             links.plan(lambda at=at: plane(at()), lambda at=at: plane(at()), place.yid)
-            for at in (line.near, line.second, line.third)
+            for at in self.spread.sources
         ]
 
     def begin(self):
@@ -524,7 +556,7 @@
 
 
 class GatherCross:
-    def __init__(self, links, place, line, block, own=None):
+    def __init__(self, links, place, line, block, own=None, way=Spread):
         def plane(z):
             return block(place.y, z)
 
@@ -533,8 +565,8 @@
 
         mine = own if own is not None else lambda: plane(place.z)
         self.cross = links.plan(mine, lambda: plane(place.z), place.yid)
-        self.spread = Spread(links, line, plane, own)
-        self.spread_other = Spread(links, line, other)
+        self.spread = way(links, line, plane, own)
+        self.spread_other = way(links, line, other)
 
     def begin(self):
         self.cross.start()
@@ -592,10 +624,10 @@
 
     def send(self, k):
         if k == 0:
-            self.line.at_end(self.hand.start)
-        if k == 1:
             self.line.at_inner(self.across.start)
             self.line.at_end(self.far.start)
+        if k == 1:
+            self.line.at_end(self.hand.start)
         if k == 2:
             self.beside.start()
 
@@ -639,7 +671,7 @@
 class Scatter:
     def __init__(self, links, place, line, theirs, mine, ybuf, zbuf):
         self.place, self.line, self.mine, self.ybuf = place, line, mine, ybuf
-        self.order = [line.third, line.second, line.near, lambda: place.z]
+        self.order = [line.second, line.third, line.near, lambda: place.z]
         self.ys = [
             links.plan(lambda at=at: theirs(at()), lambda at=at: ybuf(at()), place.yid)
             for at in self.order
@@ -707,10 +739,10 @@
     out_rows, grad_rows, gmix_out, gout_out, gup_out, gdown_out, gains_out,
     xs, gs, nf, na, act, gp, feed, gxf, gm,
     up, down, mix, outw, small, gains, meta, table, scale,
-    gdown, gout, gout_by, ydown, zdown, ymix, zmix,
+    gdown, ydown, zdown, ymix, zmix,
     zval, hval, yval, zout, hout, yout,
     up_send, up_recv, mix_send, mix_recv, gacc, gsum, gy, g2, gz, g3, gm_sum,
-    send, recv, sems, sib_sems, own_sems, far_sems, sib_free, far_free, act_free,
+    send, recv, sems, sib_sems, own_sems, far_sems, out_free, sib_free, far_free, act_free,
 ):
     place = Places(ny, nz)
     y, x, z, c = place.y, place.x, place.z, place.c
@@ -907,11 +939,16 @@
                 segment = segment + jnp.where(past, 1.0, 0.0)
                 begin = jnp.where(past, end, begin)
             angle = inverse * (places - begin)
-            meta[r, s, 0:8, :] = jnp.cos(angle)
-            meta[r, s, 8:16, :] = jnp.sin(angle)
             valid = jnp.where(segment < lens.shape[1], 1.0, 0.0)
             rest = jnp.where(fact_row == 0, segment, jnp.where(fact_row == 1, 1.0, 0.0))
-            meta[r, s, 16:24, :] = jnp.where(fact_row == 2, valid, rest)
+            rest = jnp.where(fact_row == 2, valid, rest)
+            left = jnp.concatenate([jnp.cos(angle), jnp.sin(angle)], axis=0)
+            for first in (0, 24, 40):
+                part = left.astype(LOW)
+                left = left - part.astype(WIDE)
+                meta[r, s, first : first + 16, :] = part
+            meta[r, s, 16:24, :] = rest.astype(LOW)
+            meta[r, s, 56:64, :] = jnp.zeros((8, span), LOW)
 
     def norm(j):
         def body(i, carry):
@@ -961,17 +998,14 @@
         return jnp.concatenate(parts, axis=1)
 
     def spread_meta(j, s, first, last):
-        return lax.dot_general(
-            meta[j, s], spread[:, first:last], (((0,), (0,)), ((), ())),
-            precision=lax.Precision.HIGHEST, preferred_element_type=WIDE,
-        )
+        return dot_tn(meta[j, s], spread[:, first:last])
 
     def attend_forward(j, s):
         rows = na[j, s]
         turns = spread_meta(j, s, 0, 384)
         cosine, sine, owner = turns[:, :128], turns[:, 128:256], turns[:, 256:384]
         owner = jnp.concatenate([owner, owner], axis=1)
-        allowed = (owner == meta[j, s, 16:17, :]) & (key_at <= query_at)
+        allowed = (owner == meta[j, s, 16:24, :][0:1, :].astype(WIDE)) & (key_at <= query_at)
         query, key, value = (dot_nn(rows, mix[t].reshape(width, group)) for t in range(3))
         query = turn(query, cosine, sine).astype(LOW)
         key = turn(key, cosine, sine).astype(LOW)
@@ -992,13 +1026,13 @@
             total = jnp.where(of_head[h], totals[h], total)
         att = (numer / total).astype(LOW)
         gm[j, s, :, wide_mix:] = att
+        return (att, cosine, sine, allowed, raised_query, raised_key, phi_query, phi_key, value,
+                scores, totals, numer, total)
+
+    def attend_back(j, s, kept):
+        (att, cosine, sine, allowed, raised_query, raised_key, phi_query, phi_key, value,
+         scores, totals, numer, total) = kept
         feed[j, s] = dot_nn(att, outw[:, c].reshape(group, width)).astype(LOW)
-        return (cosine, sine, allowed, raised_query, raised_key, phi_query, phi_key, value,
-                scores, totals, numer, total)
-
-    def attend_back(j, s, kept):
-        (cosine, sine, allowed, raised_query, raised_key, phi_query, phi_key, value,
-         scores, totals, numer, total) = kept
         grad_att = dot_nt(gs[j, s], outw[:, c].reshape(group, width))
         grad_numer = (grad_att / total).astype(LOW)
         product = grad_att * numer
@@ -1028,12 +1062,13 @@
         gxf[j, s] = (grad_normed * gains[0:1, :]).astype(LOW)
 
     def attend(j, pump):
-        pump(0)
-        kept = [attend_forward(j, s) for s in range(micro)]
-        pump(1)
+        kept = []
+        for s in range(micro):
+            kept.append(attend_forward(j, s))
+            pump(s)
         for s in range(micro):
             attend_back(j, s, kept[s])
-        pump(2)
+            pump(micro + s)
 
     def hidden(k):
         def body(i, pump):
@@ -1070,11 +1105,11 @@
             gdown[block // nz, block % nz] = part[rows].astype(LOW)
 
     def keep_up(at, part):
-        xs[at, 0] = part.astype(LOW)
-
-    def up_block(ref, first, s, at):
+        na[2 + at // 2, at % 2] = part.astype(LOW)
+
+    def up_block(ref, j, at, cols):
         size = 2 * shard
-        return ref.at[pl.ds(first, 2), s, pl.ds(pl.multiple_of(at * size, size), size)]
+        return ref.at[j, :, pl.ds(pl.multiple_of(at * size, size), size), cols]
 
     def keep_mix(at, part):
         for t in range(3):
@@ -1094,11 +1129,18 @@
         links, place, line, lambda at: gdown.at[1 - y, at], lambda at: gdown.at[y, at],
         lambda at: ydown.at[at], lambda k: zdown.at[k],
     )
-    up_sum = Scatter(
-        links, place, line, lambda at: up_block(xs, (1 - y) * 2, 0, at),
-        lambda at: up_block(xs, y * 2, 0, at), lambda at: up_block(act, 0, 0, at),
-        lambda k: up_block(act, 0, 1, k),
-    )
+    up_sums = []
+    for k in range(2):
+        cols = pl.ds(k * half, half)
+        up_sums.append(
+            Scatter(
+                links, place, line,
+                lambda at, cols=cols: up_block(na, 3 - y, at, cols),
+                lambda at, cols=cols: up_block(na, 2 + y, at, cols),
+                lambda at, cols=cols: up_block(act, 2, at, cols),
+                lambda at, cols=cols: up_block(act, 3, at, cols),
+            )
+        )
     two = pl.ds(0, 2)
     mix_sum = Scatter(
         links, place, line, lambda at: mix.at[two, 1 - y, :, at],
@@ -1108,7 +1150,7 @@
         links, place, line, lambda at: mix.at[2, :, :, at], lambda k: zval.at[k], hval, yval
     )
     out_sum = ScatterCross(
-        links, place, line, lambda at: gout_by.at[:, at // 2, at % 2], lambda k: zout.at[k],
+        links, place, line, lambda at: outw.at[:, at // 2, at % 2, c], lambda k: zout.at[k],
         hout, yout,
     )
 
@@ -1137,9 +1179,10 @@
     loop(
         0, 2, attend,
         {
-            (0, 1): lambda: (turn_chunk(4), take_tokens()),
+            (0, 0): lambda: turn_chunk(4),
+            (0, 1): take_tokens,
             (0, 2): lambda: turn_chunk(5),
-            (1, 1): lambda: turn_chunk(6),
+            (1, 0): lambda: turn_chunk(6),
             (1, 2): lambda: turn_chunk(7),
         },
     )
@@ -1152,18 +1195,28 @@
         chunks[i].finish()
     loop(0, 4 * micro, hidden(0), {})
     turn_chunk(8)
-    landed([cot_far])
-    cot_fwd = links.start(gs.at[2], gs.at[3], place.member_id(1))
+    cot_fwd = links.plan(gs.at[2], gs.at[3], partial(place.member_id, 1))
+
+    def take_cot():
+        cot_far.wait_recv()
+        cot_fwd.start()
+
     for copy in mix_swaps + up_swaps:
         copy.wait_send()
-    landed([cot_fwd])
+
+    chunks[0].drain()
+    out_swap.wait_send()
+    pl.semaphore_signal(out_free, inc=1, device_id=place.member_id(1), device_id_type=MESH_ID)
 
     loop(
         2, 4, attend,
         {
-            (2, 1): lambda: turn_chunk(9),
+            (2, 0): lambda: turn_chunk(9),
+            (2, 1): take_cot,
             (2, 2): lambda: turn_chunk(10),
-            (3, 1): lambda: turn_chunk(11),
+            (3, 0): lambda: turn_chunk(11),
+            (3, 1): cot_fwd.wait_recv,
+            (3, 2): chunks[11].late,
         },
     )
     for i in of_mix:
@@ -1173,9 +1226,10 @@
     outer_mix(blocks // 2, blocks)
     val_sum.begin()
     part = dot_tn(gm[:, :, :, wide_mix:].reshape(rest, group), gs[...].reshape(rest, width))
-    gout[...] = part.astype(LOW).reshape(gout.shape)
-    grad_swap = links.start(gout.at[:, :, 1 - c], gout_by.at[:, c], place.member_id(1))
-    gout_by[:, c] = gout[:, :, c]
+    outw[:, c] = part.astype(LOW).reshape(ny, 2, 2, shard, width)
+    pl.semaphore_wait(out_free, 1)
+    of_sibling = outw.at[:, c, :, 1 - c]
+    grad_swap = links.start(of_sibling, of_sibling, place.member_id(1))
     for sem, r in ((sib_free, 1), (far_free, 2)):
         pl.semaphore_signal(sem, inc=1, device_id=place.member_id(r), device_id_type=MESH_ID)
     for i in of_up[2:]:
@@ -1187,7 +1241,6 @@
     outer_down(0, blocks // 2)
     down_sum.begin()
     mix_sum.turn(0)
-    chunks[of_down[-1]].late()
     for i in of_down:
         chunks[i].finish()
     for sem in (sib_free, far_free):
@@ -1228,60 +1281,86 @@
         def _():
             own_copy(s, kind).start()
 
-    def back(i, pump):
-        late, r = i // 4, i % 4
-        j = (1 - late) * (3 - r % 2) + late * (1 - r // 2)
-        s = (1 - late) * (r // 2) + late * (r % 2)
-        pump(0)
+    def grad_hidden(j, s):
+        ga = dot_nt(gs[j, s, :, 0:half], down[0].reshape(2 * half, half))
+        ga += dot_nt(gs[j, s, :, half : 2 * half], down[1].reshape(2 * half, half))
+        gp[j, s] = (ga * gp[j, s].astype(WIDE)).astype(LOW)
+
+    def rows_out_of(j, s):
         rows = act[j, s]
         sums = [dot_nn(rows, down[k].reshape(2 * half, half)) for k in range(2)]
         hand_on(j, s, jnp.concatenate(sums, axis=1) + feed[j, s].astype(WIDE), 0)
-        ga = dot_nt(gs[j, s, :, 0:half], down[0].reshape(2 * half, half))
-        ga += dot_nt(gs[j, s, :, half : 2 * half], down[1].reshape(2 * half, half))
-        gh = (ga * gp[j, s].astype(WIDE)).astype(LOW)
-        gp[j, s] = gh
+
+    def rows_back(j, s):
+        gh = gp[j, s]
         gn = dot_nt(gh[:, :half], up[0].reshape(width, half))
         gn += dot_nt(gh[:, half:], up[1].reshape(width, half))
         gacc[16:24, :] += fold_rows(gn * xs[j, s].astype(WIDE))
         gacc[24:32, :] += fold_rows(gn)
         hand_on(j, s, gn * gains[2:3, :] + gxf[j, s].astype(WIDE), 1)
 
+    def back_far(i, pump):
+        j, s = 3 - i % 2, i // 2
+        pump(0)
+        rows_out_of(j, s)
+        grad_hidden(j, s)
+        rows_back(j, s)
+
+    def back_own(i, pump):
+        pump(0)
+        grad_hidden(i // micro, i % micro)
+
+    def rows_own(i, pump):
+        j, s = 1 - i // micro, i % micro
+        pump(0)
+        rows_out_of(j, s)
+        rows_back(j, s)
+
     loop(
-        0, 4 * micro, back,
+        0, 2 * micro, back_far,
         {
             (0, 0): lambda: out_sum.hand_on(),
             (1, 0): lambda: mix_sum.turn(1),
             (2, 0): lambda: mix_sum.turn(2),
             (3, 0): lambda: mix_sum.turn(3),
-            (5, 0): lambda: val_sum.turn(),
-            (6, 0): lambda: out_sum.turn(),
         },
     )
-
+    outer_down(blocks // 2, blocks)
+    for one in [place.yid()] + [place.zid(step) for step in range(1, nz)]:
+        pl.semaphore_signal(act_free, inc=1, device_id=one, device_id_type=MESH_ID)
+    loop(
+        0, 2 * micro, back_own,
+        {
+            (0, 0): lambda: (val_sum.turn(), out_sum.turn()),
+            (1, 0): lambda: down_sum.turn(0),
+            (2, 0): lambda: down_sum.turn(1),
+        },
+    )
+    outer_up(0, blocks // 2)
+    pl.semaphore_wait(act_free, nz)
+    first_up, second_up = up_sums
+    first_up.begin()
+    loop(
+        0, 2 * micro, rows_own,
+        {
+            (0, 0): lambda: down_sum.turn(2),
+            (1, 0): lambda: down_sum.turn(3),
+        },
+    )
     gsum[...] = jnp.zeros_like(gsum)
     for k in range(4):
         gsum[k : k + 1, :] = jnp.sum(gacc[8 * k : 8 * k + 8, :], axis=0, keepdims=True)
     gain_y = links.start(gsum, gy, place.yid())
-    own_again = local.start(tok, na.at[2])
-    outer_down(blocks // 2, blocks)
-    for one in [place.yid()] + [place.zid(step) for step in range(1, nz)]:
-        pl.semaphore_signal(act_free, inc=1, device_id=one, device_id_type=MESH_ID)
-    outer_up(0, blocks // 2)
-    pl.semaphore_wait(act_free, nz)
-    up_sum.begin()
-    for k in range(3):
-        down_sum.turn(k)
+    second_up.begin()
     outer_up(blocks // 2, blocks)
-    landed([gain_y])
-    g2[...] = gsum[...] + gy[...]
-    gain_zs = [links.start(g2, gz.at[step - 1], place.zid(step)) for step in range(1, nz)]
+    own_again = local.start(tok, xs.at[0])
 
     def finish(s, carry):
         for kind in (0, 1):
             own_copy(s, kind).wait_recv()
             far_copy(s, kind).wait_recv()
         keep = spread_meta(0, s, 384, 512)[:, :1]
-        values = na[2, s].astype(WIDE)
+        values = xs[0, s].astype(WIDE)
         added = feed[0, s].astype(WIDE) + gm[0, s].astype(WIDE) + na[0, s].astype(WIDE)
         feed[0, s] = (values + keep * added).astype(LOW)
         grad = gxf[0, s].astype(WIDE) + gm[1, s].astype(WIDE) + na[1, s].astype(WIDE)
@@ -1293,14 +1372,12 @@
         gxf[0, s] = (rate * grad).astype(LOW)
         return carry
 
-    def put_up(qx, qc, values):
-        for by in range(ny):
-            rows = pl.ds(pl.multiple_of((by * 2 + qx) * shard, shard), shard)
-            for bz in range(nz):
-                first = (bz * 2 + qc) * feed_shard
-                cols = pl.ds(pl.multiple_of(first, feed_shard), feed_shard)
-                at = (by * nz + bz) * feed_shard
-                nf[0, 0, rows, cols] = values[:, at : at + feed_shard]
+    def put_up(k, qx, qc, values):
+        rows = pl.ds(pl.multiple_of((k * 2 + qx) * shard, shard), shard)
+        for bz in range(nz):
+            first = (bz * 2 + qc) * feed_shard
+            cols = pl.ds(pl.multiple_of(first, feed_shard), feed_shard)
+            nf[0, 0, rows, cols] = values[:, bz * feed_shard : (bz + 1) * feed_shard]
 
     def put_mix(qx, qc, values):
         for t in range(3):
@@ -1334,7 +1411,7 @@
         for r in (1, 2, 3):
             mx, mc = place.member(r)
             copies[r - 1].wait_recv()
-            put(mx, mc, land[r - 1])
+            put(mx, mc, land.at[r - 1][...])
 
     def keep_sum(hold):
         def emit(total):
@@ -1342,27 +1419,42 @@
 
         return emit
 
+    for one in chunks + [small_gather]:
+        one.drain()
     mix_sum.total(keep_sum(mix_send.at[two]))
     mix_send[2] = val_sum.total().astype(LOW)
     mix_shares = share(mix_send, of_mix_share, mix_recv)
-    down_sum.turn(3)
     nf[1, 1, 0:shard, :] = out_sum.total().astype(LOW)
     written = [local.start(nf.at[1, 1, pl.ds(0, shard)], gout_out)]
-    collect(mix_shares, mix_send, of_mix_share, mix_recv, put_mix)
-    written += put_out(1, gmix_out)
-    up_sum.turn(0)
+    first_up.turn(0)
+    first_up.turn(1)
+    down_sum.total(keep_sum(nf.at[1, 0, pl.ds(0, feed_shard)]))
+    written.append(local.start(nf.at[1, 0, pl.ds(0, feed_shard)], gdown_out))
+    first_up.turn(2)
+    for one in (down_sum, mix_sum, val_sum, out_sum):
+        one.drain()
+    first_up.turn(3)
+    landed([gain_y])
+    g2[...] = gsum[...] + gy[...]
+    gain_zs = [links.start(g2, gz.at[step - 1], place.zid(step)) for step in range(1, nz)]
+    second_up.turn(0)
+    second_up.turn(1)
+    second_up.turn(2)
+    first_up.total(keep_sum(up_send.at[0]))
+    up_shares = [share(up_send.at[0], of_up_share, up_recv.at[0])]
+    second_up.turn(3)
     landed(gain_zs)
     g3[...] = g2[...] + sum(gz[step - 1] for step in range(1, nz))
     gain_ms = [links.start(g3, gm_sum.at[r - 1], place.member_id(r)) for r in (1, 2, 3)]
-    up_sum.turn(1)
-    up_sum.turn(2)
-    down_sum.total(keep_sum(nf.at[1, 0, pl.ds(0, feed_shard)]))
-    written.append(local.start(nf.at[1, 0, pl.ds(0, feed_shard)], gdown_out))
     own_again.wait()
     lax.fori_loop(0, micro, finish, 0)
     rows_out = local.start(feed.at[0], out_rows)
     grads_out = local.start(gxf.at[0], grad_rows)
-    up_sum.turn(3)
+    collect(mix_shares, mix_send, of_mix_share, mix_recv, put_mix)
+    written += put_out(1, gmix_out)
+    collect(up_shares[0], up_send.at[0], of_up_share, up_recv.at[0], partial(put_up, 0))
+    second_up.total(keep_sum(up_send.at[1]))
+    up_shares.append(share(up_send.at[1], of_up_share, up_recv.at[1]))
     landed(gain_ms)
     totals = g3[...] + gm_sum[0] + gm_sum[1] + gm_sum[2]
     mine = ((y * 2 + x) * nz + z) * 2 + c
@@ -1372,14 +1464,13 @@
         totals, jnp.where(pick_row == pick_col, 1.0, 0.0), (((1,), (0,)), ((), ())),
         precision=lax.Precision.HIGHEST, preferred_element_type=WIDE,
     )
-    up_sum.total(keep_sum(up_send))
-    up_shares = share(up_send, of_up_share, up_recv)
-    collect(up_shares, up_send, of_up_share, up_recv, put_up)
+    collect(up_shares[1], up_send.at[1], of_up_share, up_recv.at[1], partial(put_up, 1))
     written += put_out(0, gup_out)
     for copy in written + [rows_out, grads_out]:
         copy.wait()
+    cot_fwd.wait_send()
     links.drain()
-    for one in chunks + [small_gather, down_sum, up_sum, mix_sum, val_sum, out_sum]:
+    for one in up_sums + [down_sum, mix_sum, val_sum, out_sum]:
         one.drain()
     for kind in (0, 1):
         for s in range(micro):
@@ -1402,16 +1493,17 @@
 
 
 def spread_rows():
-    row = np.arange(24)[:, None]
+    row = np.arange(64)[:, None]
+    turn = np.where(row < 16, row, np.where((row >= 24) & (row < 56), (row - 24) % 16, -1))
     lane = np.arange(512)[None, :]
     part, dim = lane // 128, lane % HEAD
     half = ROT // 2
-    cosine = (part == 0) & (dim < ROT) & (row == dim % half)
+    cosine = (part == 0) & (dim < ROT) & (turn == dim % half)
     cosine = cosine | ((part == 0) & (dim >= ROT) & (row == 17))
-    sine = (part == 1) & (dim < ROT) & (row == half + dim % half)
+    sine = (part == 1) & (dim < ROT) & (turn == half + dim % half)
     rest = ((part == 2) & (row == 16)) | ((part == 3) & (row == 18))
     sign = np.where((part == 1) & (dim < half), -1.0, 1.0)
-    return np.where(cosine | sine | rest, sign, 0.0).astype(np.float32)
+    return np.where(cosine | sine | rest, sign, 0.0).astype(jnp.bfloat16)
 
 
 def per_device_group(
@@ -1469,12 +1561,10 @@
             low(ny, nz // 2, 2, 2, shard, width),
             wide(ny, 2, nz, 2, 8, 128),
             wide(8, width),
-            wide(4, micro, 24, span),
+            low(4, micro, 64, span),
             low(group, group),
             wide(8, group),
             low(ny, nz, feed_shard, width),
-            low(ny, 2, 2, shard, width),
-            low(ny, nz // 2, 2, shard, width),
             low(nz, feed_shard, width),
             low(4, feed_shard, width),
             low(nz, 2, 2, 2, shard, group),
@@ -1485,8 +1575,8 @@
             low(4, ny, shard, width),
             low(ny, shard, width),
             low(shard, width),
-            low(2, 2 * shard, hidden),
-            low(3, shard, hidden),
+            low(2, 2, 2 * shard, half),
+            low(2, 3, shard, half),
             low(3, 2, 2, shard, group),
             low(3, 3, shard, group),
             wide(32, width),
@@ -1496,12 +1586,13 @@
             wide(nz - 1, 8, width),
             wide(8, width),
             wide(3, 8, width),
-            dma((200,)),
-            dma((200,)),
+            dma((240,)),
+            dma((240,)),
             dma((28,)),
             dma((2, 2, 2)),
             dma((2, 2, 2)),
             dma((2, 2, 2)),
+            pltpu.SemaphoreType.REGULAR,
             pltpu.SemaphoreType.REGULAR,
             pltpu.SemaphoreType.REGULAR,
             pltpu.SemaphoreType.REGULAR,

time: 194 us -> 173 us (0.89)
  Pallas kernels: 184 us -> 162 us
    pallas_call x1, Pallas kernels: 184 us -> 162 us  [per_device_group(): pl.pallas_call(partial(layer_kernel, ny, nz), out_shape=[SHAPE((micro, sp...]
where the time goes in v3:
time: 173 us; the launch traced here: 172 us
  Pallas kernels  162 us (94%)
  other arithmetic  7.39 us (4%)
  local copies, waits for them, and re-layouts  2.34 us (1%)
    pallas_call x1, Pallas kernels, per_device_group(): pl.pallas_call(partial(layer_kernel, ny, nz), out_shape=[SHAPE((micro, sp...  162 us

profile of v3, /device:TPU:0, one launch (start us, length us, event | category | flops | bytes accessed | tf_op | source)
XLA Modules:
  0.0 172.5 jit_solution(6659127883726700096)
XLA Ops:
  0.6 1.3 pad_maximum_fusion.norms
  1.9 0.0 copy-start.1
  1.9 162.1 %layer.1 = (bf16[2,256,1024]{2,1,0:T(8,128)(2,1)}, bf16[2,256,1024]{2,1,0:T(8,128)(2,1)}, bf16[32,3072]{1,0:T(8,128)(2,1)}, bf16[32,1024]{1,0:T(8,128)(2,1)}, bf...) custom-call(s32[2,4]{1,0:T(2,128)} %bitcast.18, bf16[2,256,1024]{2,1,0:T(8,128)(2,1)} %tok.1, ...), custom_call_target="tpu_custom_call" | custom-call | flops 44999999488 | bytes 20000000 | tf_op jit(solution)/shard_map/layer/pallas_call | solution.py:1543
  164.0 1.3 slice_bitcast_fusion
  165.4 0.0 copy-done.1
  165.4 0.0 copy-start.3
  165.4 0.0 copy-start.2
  165.4 0.0 copy-start.4
  165.4 3.0 %convert_add_fusion = f32[2,256,1024]{2,1,0:T(8,128)} fusion(bf16[2,256,1024]{2,1,0:T(8,128)(2,1)} %get-tuple-element.18, bf16[2,256,1024]{2,1,0:T(8,128)(2,1)S(1)} %copy-done.1), kind=kLoop, calls=%fused_computation | loop fusion | flops 1572864 | bytes 4194304 | tf_op jit(solution)/shard_map/add | solution.py:1611
  168.4 0.0 copy-start.5
  168.4 0.0 copy-start
  168.4 0.0 copy-done.3
  168.4 0.8 convert_element_type.22
  169.2 0.0 copy-done.2
  169.2 0.8 convert_element_type.23
  170.1 0.0 copy-done.4
  170.1 0.8 convert_element_type.20
  170.8 0.0 copy-done.5
  170.8 0.7 convert_element_type.21
  171.5 0.0 copy-done
  171.5 1.0 copy.26
Async XLA Ops:
  1.9 163.4 %copy-start.1 = (bf16[2,256,1024]{2,1,0:T(8,128)(2,1)S(1)}, bf16[2,256,1024]{2,1,0:T(8,128)(2,1)}, u32[]{:S(2)}) copy-start(bf16[2,256,1024]{2,1,0:T(8,128)(2,1)} %cot.1) | copy-start | bytes 3145732
  165.4 3.0 %copy-start.3 = (bf16[32,4096]{1,0:T(8,128)(2,1)S(1)}, bf16[32,4096]{1,0:T(8,128)(2,1)}, u32[]{:S(2)}) copy-start(bf16[32,4096]{1,0:T(8,128)(2,1)} %get-tuple-element.21) | copy-start | bytes 786436
  165.4 3.9 %copy-start.2 = (bf16[128,1024]{1,0:T(8,128)(2,1)S(1)}, bf16[128,1024]{1,0:T(8,128)(2,1)}, u32[]{:S(2)}) copy-start(bf16[128,1024]{1,0:T(8,128)(2,1)} %get-tuple-element.22) | copy-start | bytes 786436
  165.4 4.7 %copy-start.4 = (bf16[32,3072]{1,0:T(8,128)(2,1)S(1)}, bf16[32,3072]{1,0:T(8,128)(2,1)}, u32[]{:S(2)}) copy-start(bf16[32,3072]{1,0:T(8,128)(2,1)} %get-tuple-element.19) | copy-start | bytes 589828
  168.4 2.5 %copy-start.5 = (bf16[32,1024]{1,0:T(8,128)(2,1)S(1)}, bf16[32,1024]{1,0:T(8,128)(2,1)}, u32[]{:S(2)}) copy-start(bf16[32,1024]{1,0:T(8,128)(2,1)} %get-tuple-element.20) | copy-start | bytes 196612
  168.4 3.1 %copy-start = (bf16[2,256,1024]{2,1,0:T(8,128)(2,1)S(1)}, bf16[2,256,1024]{2,1,0:T(8,128)(2,1)}, u32[]{:S(2)}) copy-start(bf16[2,256,1024]{2,1,0:T(8,128)(2,1)} %get-tuple-element.38) | copy-start | bytes 3145732

commit v4 on v3

--- a/solution.py
+++ b/solution.py
@@ -689,8 +689,9 @@
             land = self.ybuf(at)
             land[...] = (land[...].astype(WIDE) + self.mine(at)[...].astype(WIDE)).astype(LOW)
         self.fold.send(k)
-        if k == 2:
-            self.fold.hand_on()
+
+    def hand_on(self):
+        self.fold.hand_on()
 
     def total(self, emit):
         z = self.place.z
@@ -735,10 +736,10 @@
 
 def layer_kernel(
     ny, nz,
-    lens, tok, cot, mix_w, out_w, up_w, down_w, norms, freq, scale_in, dct, spread,
+    lens, tok, cot, mix_w, out_w, up_w, down_w, norms_in, freq_in, scale_ref, dct_in, spread_in,
     out_rows, grad_rows, gmix_out, gout_out, gup_out, gdown_out, gains_out,
     xs, gs, nf, na, act, gp, feed, gxf, gm,
-    up, down, mix, outw, small, gains, meta, table, scale,
+    up, down, mix, outw, small, gains, meta, table, scale, norms, freq, scale_in, dct, spread,
     gdown, ydown, zdown, ymix, zmix,
     zval, hval, yval, zout, hout, yout,
     up_send, up_recv, mix_send, mix_recv, gacc, gsum, gy, g2, gz, g3, gm_sum,
@@ -766,6 +767,7 @@
             local.start(weight.at[:, pl.ds(n * width, width)], raw(first + n)) for n in range(count)
         ]
 
+    norms_load = local.start(norms_in, norms)
     mix_load = raw_load(mix_w, 0)
     up_load = raw_load(up_w, len(mix_load))
     out_mine = local.start(out_w, outw.at[y, z // 2, z % 2, c])
@@ -775,6 +777,10 @@
         local.start(down_w.at[:, pl.ds(k * half, half)], down.at[k, y, z]) for k in range(2)
     ]
     place.signal()
+    table_loads = [
+        local.start(src, dst)
+        for src, dst in ((freq_in, freq), (scale_ref, scale_in), (dct_in, dct), (spread_in, spread))
+    ]
 
     row = lax.broadcasted_iota(jnp.int32, (8, 128), 0)
     lane = lax.broadcasted_iota(jnp.int32, (8, 128), 1)
@@ -782,6 +788,7 @@
     for s in range(micro):
         for k in range(lens.shape[1]):
             facts = jnp.where((row == 1 + s) & (lane == k), lens[s, k].astype(WIDE), facts)
+    norms_load.wait()
     at_row = lax.broadcasted_iota(jnp.int32, (shard, 128), 0)
     at_lane = lax.broadcasted_iota(jnp.int32, (shard, 128), 1)
     for k in range(4):
@@ -807,6 +814,27 @@
             for by in range(ny):
                 first = t * width + ((by * 2 + q // 2) * 2 + q % 2) * pair
                 mix_stage(t, q)[:, by * pair : (by + 1) * pair] = raw_cols(0, first, pair)
+    for t in range(3):
+        mix[t, y, x, z, c] = mix_stage(t, me)[...]
+    place.meet()
+    links = Links(send, recv)
+    line = Line(place)
+
+    def swap(src, dst):
+        copies = []
+        for r in (1, 2, 3):
+            mx, mc = place.member(r)
+            copies.append(links.start(src(mx * 2 + mc), dst, place.member_id(r)))
+        return copies
+
+    def landed(copies):
+        for copy in copies:
+            copy.wait_recv()
+
+    small_swaps = swap(lambda q: small.at[y, x, z, c], small.at[y, x, z, c])
+    mix_swaps = []
+    for t in range(3):
+        mix_swaps += swap(lambda q, t=t: mix_stage(t, q), mix.at[t, y, x, z, c])
     for copy in up_load:
         copy.wait()
     for q in range(4):
@@ -816,27 +844,6 @@
                 cols = slice(bz * feed_shard, (bz + 1) * feed_shard)
                 up_stage(q)[by, :, cols] = raw_cols(len(mix_load), first, feed_shard)
     up[:, y, x, z, c] = up_stage(me)[...]
-    for t in range(3):
-        mix[t, y, x, z, c] = mix_stage(t, me)[...]
-    place.meet()
-    links = Links(send, recv)
-    line = Line(place)
-
-    def swap(src, dst):
-        copies = []
-        for r in (1, 2, 3):
-            mx, mc = place.member(r)
-            copies.append(links.start(src(mx * 2 + mc), dst, place.member_id(r)))
-        return copies
-
-    def landed(copies):
-        for copy in copies:
-            copy.wait_recv()
-
-    small_swaps = swap(lambda q: small.at[y, x, z, c], small.at[y, x, z, c])
-    mix_swaps = []
-    for t in range(3):
-        mix_swaps += swap(lambda q, t=t: mix_stage(t, q), mix.at[t, y, x, z, c])
     up_swaps = swap(up_stage, up.at[:, y, x, z, c])
     chunks = [GatherCross(links, place, line, lambda by, bz: outw.at[by, bz // 2, bz % 2, c])]
     for t in range(3):
@@ -865,90 +872,92 @@
         if i + ahead < len(chunks):
             chunks[i + ahead].begin()
 
-    out_mine.wait()
-    chunks[0].begin()
-    tok_mine.wait()
-    tok_sib = links.start(gp.at[0], gp.at[1], place.member_id(1))
-    tok_far = links.start(gp.at[0], gp.at[2], place.member_id(2))
     small_gather = Gather(links, place, line, lambda by, bz: small.at[by, :, bz])
-    landed(small_swaps)
-    small_gather.begin()
-    landed(mix_swaps)
-    chunks[1].begin()
-    chunks[2].begin()
-    cot_mine.wait()
-    at_place = lax.broadcasted_iota(jnp.int32, (span, 1), 0)
-    for s in range(micro):
-        used = lens[s, 0]
-        for k in range(1, lens.shape[1]):
-            used = used + lens[s, k]
-        gs[0, s] = jnp.where(at_place < used, gs[0, s], none)
-    cot_sib = links.start(gs.at[0], gs.at[1], place.member_id(1))
-    cot_far = links.start(gs.at[0], gs.at[2], place.member_id(2))
-
-    raw = lax.dot_general(
-        dct[...], freq[...], (((0,), (1,)), ((), ())),
-        precision=lax.Precision.HIGHEST, preferred_element_type=WIDE,
-    ) / math.sqrt(HEAD)
-    raw = raw.astype(LOW)
-    tile_row = lax.broadcasted_iota(jnp.int32, (HEAD, group), 0)
-    tile_col = lax.broadcasted_iota(jnp.int32, (HEAD, group), 1)
-    tiled = jnp.where(tile_col % HEAD == tile_row, 1.0, 0.0).astype(LOW)
-    wide_table = dot_tn(tiled, dot_nn(raw, tiled).astype(LOW))
-    block_row = lax.broadcasted_iota(jnp.int32, (group, group), 0) // HEAD
-    block_col = lax.broadcasted_iota(jnp.int32, (group, group), 1) // HEAD
-    table[...] = jnp.where(block_row == block_col, wide_table, 0.0).astype(LOW)
-    scale[...] = lax.dot_general(
-        jnp.broadcast_to(scale_in[...], (8, HEAD)), tiled.astype(WIDE), (((1,), (0,)), ((), ())),
-        precision=lax.Precision.HIGHEST, preferred_element_type=WIDE,
-    )
-
-    small_gather.forward()
-    small_gather.late()
-    turn_chunk(0)
-    small_gather.finish()
-    count = ny * 2 * nz * 2
-    packed = jnp.sum(jnp.where(row == 0, small[...].reshape(count, 8, 128), 0.0), axis=1)
-    packed = packed.astype(LOW)
-    pick_row = lax.broadcasted_iota(jnp.int32, (128, width), 0)
-    pick_col = lax.broadcasted_iota(jnp.int32, (128, width), 1) % shard
-    owner = lax.broadcasted_iota(jnp.int32, (count, width), 0)
-    owned = lax.broadcasted_iota(jnp.int32, (count, width), 1) // shard
-    for k in range(4):
-        pick = jnp.where(pick_row == pick_col + k * shard, 1.0, 0.0).astype(LOW)
-        part = jnp.where(owned == owner, dot_nn(packed, pick), 0.0)
-        gains[k : k + 1, :] = jnp.sum(part, axis=0, keepdims=True)
-    gacc[...] = jnp.zeros_like(gacc)
-
-    places = lax.broadcasted_iota(jnp.int32, (1, span), 1).astype(WIDE)
-    turn_row = lax.broadcasted_iota(jnp.int32, (ROT // 2, 1), 0)
-    inverse = jnp.zeros((ROT // 2, 1), WIDE)
-    for k in range(ROT // 2):
-        inverse = jnp.where(turn_row == k, 10000.0 ** (-2.0 * k / ROT), inverse)
-    fact_row = lax.broadcasted_iota(jnp.int32, (8, span), 0)
-    for r in range(4):
-        mx, mc = place.member(r)
-        facts = small[y, mx, z, mc]
+    tok_sib = links.plan(gp.at[0], gp.at[1], partial(place.member_id, 1))
+    tok_far = links.plan(gp.at[0], gp.at[2], partial(place.member_id, 2))
+    cot_sib = links.plan(gs.at[0], gs.at[1], partial(place.member_id, 1))
+    cot_far = links.plan(gs.at[0], gs.at[2], partial(place.member_id, 2))
+
+    def send_tokens():
+        tok_mine.wait()
+        tok_sib.start()
+        tok_far.start()
+
+    def send_cot():
+        cot_mine.wait()
+        at_place = lax.broadcasted_iota(jnp.int32, (span, 1), 0)
         for s in range(micro):
-            end = jnp.zeros((1, 1), WIDE)
-            segment = jnp.zeros((1, span), WIDE)
-            begin = jnp.zeros((1, span), WIDE)
-            for k in range(lens.shape[1]):
-                end = end + facts[1 + s : 2 + s, k : k + 1]
-                past = places >= end
-                segment = segment + jnp.where(past, 1.0, 0.0)
-                begin = jnp.where(past, end, begin)
-            angle = inverse * (places - begin)
-            valid = jnp.where(segment < lens.shape[1], 1.0, 0.0)
-            rest = jnp.where(fact_row == 0, segment, jnp.where(fact_row == 1, 1.0, 0.0))
-            rest = jnp.where(fact_row == 2, valid, rest)
-            left = jnp.concatenate([jnp.cos(angle), jnp.sin(angle)], axis=0)
-            for first in (0, 24, 40):
-                part = left.astype(LOW)
-                left = left - part.astype(WIDE)
-                meta[r, s, first : first + 16, :] = part
-            meta[r, s, 16:24, :] = rest.astype(LOW)
-            meta[r, s, 56:64, :] = jnp.zeros((8, span), LOW)
+            used = lens[s, 0]
+            for k in range(1, lens.shape[1]):
+                used = used + lens[s, k]
+            gs[0, s] = jnp.where(at_place < used, gs[0, s], none)
+        cot_sib.start()
+        cot_far.start()
+
+    def make_table():
+        for copy in table_loads:
+            copy.wait()
+        raw = lax.dot_general(
+            dct[...], freq[...], (((0,), (1,)), ((), ())),
+            precision=lax.Precision.HIGHEST, preferred_element_type=WIDE,
+        ) / math.sqrt(HEAD)
+        raw = raw.astype(LOW)
+        tile_row = lax.broadcasted_iota(jnp.int32, (HEAD, group), 0)
+        tile_col = lax.broadcasted_iota(jnp.int32, (HEAD, group), 1)
+        tiled = jnp.where(tile_col % HEAD == tile_row, 1.0, 0.0).astype(LOW)
+        wide_table = dot_tn(tiled, dot_nn(raw, tiled).astype(LOW))
+        block_row = lax.broadcasted_iota(jnp.int32, (group, group), 0) // HEAD
+        block_col = lax.broadcasted_iota(jnp.int32, (group, group), 1) // HEAD
+        table[...] = jnp.where(block_row == block_col, wide_table, 0.0).astype(LOW)
+        scale[...] = lax.dot_general(
+            jnp.broadcast_to(scale_in[...], (8, HEAD)), tiled.astype(WIDE), (((1,), (0,)), ((), ())),
+            precision=lax.Precision.HIGHEST, preferred_element_type=WIDE,
+        )
+
+    def make_gains():
+        count = ny * 2 * nz * 2
+        packed = jnp.sum(jnp.where(row == 0, small[...].reshape(count, 8, 128), 0.0), axis=1)
+        packed = packed.astype(LOW)
+        pick_row = lax.broadcasted_iota(jnp.int32, (128, width), 0)
+        pick_col = lax.broadcasted_iota(jnp.int32, (128, width), 1) % shard
+        owner = lax.broadcasted_iota(jnp.int32, (count, width), 0)
+        owned = lax.broadcasted_iota(jnp.int32, (count, width), 1) // shard
+        for k in range(4):
+            pick = jnp.where(pick_row == pick_col + k * shard, 1.0, 0.0).astype(LOW)
+            part = jnp.where(owned == owner, dot_nn(packed, pick), 0.0)
+            gains[k : k + 1, :] = jnp.sum(part, axis=0, keepdims=True)
+        gacc[...] = jnp.zeros_like(gacc)
+
+    def make_turns():
+        places = lax.broadcasted_iota(jnp.int32, (1, span), 1).astype(WIDE)
+        turn_row = lax.broadcasted_iota(jnp.int32, (ROT // 2, 1), 0)
+        inverse = jnp.zeros((ROT // 2, 1), WIDE)
+        for k in range(ROT // 2):
+            inverse = jnp.where(turn_row == k, 10000.0 ** (-2.0 * k / ROT), inverse)
+        fact_row = lax.broadcasted_iota(jnp.int32, (8, span), 0)
+        for r in range(4):
+            mx, mc = place.member(r)
+            facts = small[y, mx, z, mc]
+            for s in range(micro):
+                end = jnp.zeros((1, 1), WIDE)
+                segment = jnp.zeros((1, span), WIDE)
+                begin = jnp.zeros((1, span), WIDE)
+                for k in range(lens.shape[1]):
+                    end = end + facts[1 + s : 2 + s, k : k + 1]
+                    past = places >= end
+                    segment = segment + jnp.where(past, 1.0, 0.0)
+                    begin = jnp.where(past, end, begin)
+                angle = inverse * (places - begin)
+                valid = jnp.where(segment < lens.shape[1], 1.0, 0.0)
+                rest = jnp.where(fact_row == 0, segment, jnp.where(fact_row == 1, 1.0, 0.0))
+                rest = jnp.where(fact_row == 2, valid, rest)
+                left = jnp.concatenate([jnp.cos(angle), jnp.sin(angle)], axis=0)
+                for first in (0, 24, 40):
+                    part = left.astype(LOW)
+                    left = left - part.astype(WIDE)
+                    meta[r, s, first : first + 16, :] = part
+                meta[r, s, 16:24, :] = rest.astype(LOW)
+                meta[r, s, 56:64, :] = jnp.zeros((8, span), LOW)
 
     def norm(j):
         def body(i, carry):
@@ -1154,22 +1163,50 @@
         hout, yout,
     )
 
+    out_here = outw.at[:, 1 - c, :, c]
+    out_swap = links.plan(out_here, out_here, partial(place.member_id, 1))
+    landed(small_swaps)
+    small_gather.begin()
+    out_mine.wait()
+    chunks[0].begin()
+    send_tokens()
+    landed(mix_swaps[0:3])
+    chunks[1].begin()
+    landed(mix_swaps[3:6])
+    chunks[2].begin()
+    send_cot()
+    small_gather.forward()
+    small_gather.late()
+    landed(mix_swaps[6:9])
+    chunks[0].forward()
+    chunks[3].begin()
+    chunks[1].forward()
     landed(up_swaps)
-    turn_chunk(1)
-    norm(0)
+    make_table()
+    small_gather.finish()
+    make_gains()
+    make_turns()
+    chunks[0].late()
+    chunks[2].forward()
     landed([tok_sib])
     norm(1)
-    turn_chunk(2)
+    chunks[1].late()
+    chunks[3].forward()
+    chunks[4].begin()
     chunks[0].finish()
-    out_here = outw.at[:, 1 - c, :, c]
-    out_swap = links.start(out_here, out_here, place.member_id(1))
-    turn_chunk(3)
+    chunks[5].begin()
+    out_swap.start()
+    chunks[2].late()
+    out_swap.wait_recv()
+    landed([cot_sib])
+    chunks[1].finish()
+    norm(0)
     for copy in down_mine:
         copy.wait()
-    landed([out_swap, cot_sib])
     chunks[3].late()
-    for i in of_mix:
-        chunks[i].finish()
+    chunks[2].finish()
+    chunks[3].finish()
+    chunks[6].begin()
     tok_fwd = links.plan(gp.at[2], gp.at[3], partial(place.member_id, 1))
 
     def take_tokens():
@@ -1321,38 +1358,40 @@
         {
             (0, 0): lambda: out_sum.hand_on(),
             (1, 0): lambda: mix_sum.turn(1),
-            (2, 0): lambda: mix_sum.turn(2),
+            (2, 0): lambda: (mix_sum.turn(2), outer_down(blocks // 2, blocks)),
             (3, 0): lambda: mix_sum.turn(3),
         },
     )
-    outer_down(blocks // 2, blocks)
     for one in [place.yid()] + [place.zid(step) for step in range(1, nz)]:
         pl.semaphore_signal(act_free, inc=1, device_id=one, device_id_type=MESH_ID)
     loop(
         0, 2 * micro, back_own,
         {
-            (0, 0): lambda: (val_sum.turn(), out_sum.turn()),
-            (1, 0): lambda: down_sum.turn(0),
-            (2, 0): lambda: down_sum.turn(1),
+            (0, 0): lambda: down_sum.turn(0),
+            (1, 0): lambda: (val_sum.turn(), out_sum.turn()),
+            (2, 0): lambda: (down_sum.turn(1), mix_sum.hand_on()),
         },
     )
     outer_up(0, blocks // 2)
     pl.semaphore_wait(act_free, nz)
     first_up, second_up = up_sums
     first_up.begin()
+    outer_up(blocks // 2, blocks)
     loop(
         0, 2 * micro, rows_own,
         {
             (0, 0): lambda: down_sum.turn(2),
             (1, 0): lambda: down_sum.turn(3),
+            (2, 0): lambda: first_up.turn(0),
+            (3, 0): lambda: (first_up.turn(1), down_sum.hand_on()),
         },
     )
+    links.drain()
     gsum[...] = jnp.zeros_like(gsum)
     for k in range(4):
         gsum[k : k + 1, :] = jnp.sum(gacc[8 * k : 8 * k + 8, :], axis=0, keepdims=True)
     gain_y = links.start(gsum, gy, place.yid())
     second_up.begin()
-    outer_up(blocks // 2, blocks)
     own_again = local.start(tok, xs.at[0])
 
     def finish(s, carry):
@@ -1419,30 +1458,30 @@
 
         return emit
 
-    for one in chunks + [small_gather]:
-        one.drain()
+    first_up.turn(2)
     mix_sum.total(keep_sum(mix_send.at[two]))
     mix_send[2] = val_sum.total().astype(LOW)
     mix_shares = share(mix_send, of_mix_share, mix_recv)
     nf[1, 1, 0:shard, :] = out_sum.total().astype(LOW)
     written = [local.start(nf.at[1, 1, pl.ds(0, shard)], gout_out)]
-    first_up.turn(0)
-    first_up.turn(1)
-    down_sum.total(keep_sum(nf.at[1, 0, pl.ds(0, feed_shard)]))
-    written.append(local.start(nf.at[1, 0, pl.ds(0, feed_shard)], gdown_out))
-    first_up.turn(2)
-    for one in (down_sum, mix_sum, val_sum, out_sum):
-        one.drain()
     first_up.turn(3)
     landed([gain_y])
     g2[...] = gsum[...] + gy[...]
     gain_zs = [links.start(g2, gz.at[step - 1], place.zid(step)) for step in range(1, nz)]
+    for one in chunks + [small_gather]:
+        one.drain()
     second_up.turn(0)
     second_up.turn(1)
+    first_up.hand_on()
+    for one in (mix_sum, val_sum, out_sum):
+        one.drain()
     second_up.turn(2)
+    second_up.turn(3)
+    second_up.hand_on()
+    down_sum.total(keep_sum(nf.at[1, 0, pl.ds(0, feed_shard)]))
+    written.append(local.start(nf.at[1, 0, pl.ds(0, feed_shard)], gdown_out))
     first_up.total(keep_sum(up_send.at[0]))
     up_shares = [share(up_send.at[0], of_up_share, up_recv.at[0])]
-    second_up.turn(3)
     landed(gain_zs)
     g3[...] = g2[...] + sum(gz[step - 1] for step in range(1, nz))
     gain_ms = [links.start(g3, gm_sum.at[r - 1], place.member_id(r)) for r in (1, 2, 3)]
@@ -1450,11 +1489,13 @@
     lax.fori_loop(0, micro, finish, 0)
     rows_out = local.start(feed.at[0], out_rows)
     grads_out = local.start(gxf.at[0], grad_rows)
+    second_up.total(keep_sum(up_send.at[1]))
+    up_shares.append(share(up_send.at[1], of_up_share, up_recv.at[1]))
     collect(mix_shares, mix_send, of_mix_share, mix_recv, put_mix)
     written += put_out(1, gmix_out)
     collect(up_shares[0], up_send.at[0], of_up_share, up_recv.at[0], partial(put_up, 0))
-    second_up.total(keep_sum(up_send.at[1]))
-    up_shares.append(share(up_send.at[1], of_up_share, up_recv.at[1]))
+    down_sum.drain()
+    first_up.drain()
     landed(gain_ms)
     totals = g3[...] + gm_sum[0] + gm_sum[1] + gm_sum[2]
     mine = ((y * 2 + x) * nz + z) * 2 + c
@@ -1468,10 +1509,10 @@
     written += put_out(0, gup_out)
     for copy in written + [rows_out, grads_out]:
         copy.wait()
-    cot_fwd.wait_send()
+    for copy in (cot_sib, cot_far, cot_fwd):
+        copy.wait_send()
     links.drain()
-    for one in up_sums + [down_sum, mix_sum, val_sum, out_sum]:
-        one.drain()
+    second_up.drain()
     for kind in (0, 1):
         for s in range(micro):
             sib_copy(s, kind).wait_send()
@@ -1504,6 +1545,52 @@
     rest = ((part == 2) & (row == 16)) | ((part == 3) & (row == 18))
     sign = np.where((part == 1) & (dim < half), -1.0, 1.0)
     return np.where(cosine | sine | rest, sign, 0.0).astype(jnp.bfloat16)
+
+
+def widen_kernel(
+    rows, grads, cot, gains, mix, out, up, down,
+    rows_out, grads_out, gain_one, bias_one, gain_two, bias_two, mix_out, out_out, up_out, down_out,
+    rows_low, grads_low, cot_low, grads_wide, mix_low, mix_wide, out_low, out_wide,
+    up_low, up_wide, down_low, down_wide, loaded, stored,
+):
+    parts = [(s, h) for s in range(rows.shape[0]) for h in range(2)]
+    half = rows.shape[1] // 2
+    weights = [
+        (mix, mix_low, mix_wide, mix_out),
+        (up, up_low, up_wide, up_out),
+        (down, down_low, down_wide, down_out),
+        (out, out_low, out_wide, out_out),
+    ]
+    copies = Locals(loaded)
+    stores = Locals(stored)
+    loads, written = [], []
+    for s, h in parts:
+        at = pl.ds(h * half, half)
+        loads.append(
+            (
+                copies.start(grads.at[s, at], grads_low.at[s, at]),
+                copies.start(cot.at[s, at], cot_low.at[s, at]),
+            )
+        )
+    weight_loads = [copies.start(src, low) for src, low, _, _ in weights]
+    row_loads = [copies.start(rows.at[s], rows_low.at[s]) for s in range(rows.shape[0])]
+    for k, ref in enumerate((gain_one, bias_one, gain_two, bias_two)):
+        ref[...] = gains[k : k + 1, :]
+    for (s, h), pair in zip(parts, loads):
+        for copy in pair:
+            copy.wait()
+        at = pl.ds(h * half, half)
+        grads_wide[s, at] = cot_low[s, at].astype(WIDE) + grads_low[s, at].astype(WIDE)
+        written.append(stores.start(grads_wide.at[s, at], grads_out.at[s, at]))
+    for load, (_, low, wide, dst) in zip(weight_loads, weights):
+        load.wait()
+        wide[...] = low[...].astype(WIDE)
+        written.append(stores.start(wide, dst))
+    for s, load in enumerate(row_loads):
+        load.wait()
+        written.append(stores.start(rows_low.at[s], rows_out.at[s]))
+    for copy in written:
+        copy.wait()
 
 
 def per_device_group(
@@ -1551,7 +1638,7 @@
             SHAPE(down_weight.shape, LOW),
             SHAPE((8, shard), WIDE),
         ],
-        in_specs=[SMEM] + [ANY] * 6 + [VMEM] * 5,
+        in_specs=[SMEM] + [ANY] * 11,
         out_specs=[ANY] * 6 + [VMEM],
         scratch_shapes=[whole] * 9
         + [
@@ -1564,6 +1651,11 @@
             low(4, micro, 64, span),
             low(group, group),
             wide(8, group),
+            low(4, shard),
+            wide(HEAD, HEAD),
+            wide(1, HEAD),
+            wide(HEAD, HEAD),
+            low(64, 512),
             low(ny, nz, feed_shard, width),
             low(nz, feed_shard, width),
             low(4, feed_shard, width),
@@ -1588,7 +1680,7 @@
             wide(3, 8, width),
             dma((240,)),
             dma((240,)),
-            dma((28,)),
+            dma((36,)),
             dma((2, 2, 2)),
             dma((2, 2, 2)),
             dma((2, 2, 2)),
@@ -1606,18 +1698,23 @@
         lengths[:, 0], tokens, cotangent, mix_weight, out_weight, up_weight, down_weight, norms,
         feature_freq, feature_scale[None], cosine_basis(), spread_rows(),
     )
-    return (
-        out_rows,
-        cotangent.astype(WIDE) + grad_rows.astype(WIDE),
-        gmix.astype(WIDE),
-        gout.astype(WIDE),
-        gup.astype(WIDE),
-        gdown.astype(WIDE),
-        gains[0],
-        gains[1],
-        gains[2],
-        gains[3],
-    )
+    shapes = [w.shape for w in (mix_weight, out_weight, up_weight, down_weight)]
+    one = SHAPE((1, shard), WIDE)
+    results = pl.pallas_call(
+        widen_kernel,
+        out_shape=[SHAPE(out_rows.shape, LOW), SHAPE(out_rows.shape, WIDE), one, one, one, one]
+        + [SHAPE(shape, WIDE) for shape in shapes],
+        in_specs=[ANY] * 3 + [VMEM] + [ANY] * 4,
+        out_specs=[ANY] * 2 + [VMEM] * 4 + [ANY] * 4,
+        scratch_shapes=[low(*out_rows.shape)] * 3
+        + [wide(*out_rows.shape)]
+        + [kind(*shape) for shape in shapes[:2] for kind in (low, wide)]
+        + [kind(*shape) for shape in shapes[2:] for kind in (low, wide)]
+        + [dma((16,)), dma((16,))],
+        name="widen",
+    )(out_rows, grad_rows, cotangent, gains, gmix, gout, gup, gdown)
+    rows, grads, *norm_grads = results[:6]
+    return (rows, grads, *results[6:], *(part.reshape(shard) for part in norm_grads))
 
 
 def solution(mesh):

time: 173 us -> 166 us (0.960)
  other arithmetic: 7.39 us -> 1.28 us
  local copies, waits for them, and re-layouts: 2.34 us -> 0 us
  Pallas kernels: 162 us -> 164 us
    pallas_call x0 -> x1, Pallas kernels: none -> 4.75 us  [per_device_group(): pl.pallas_call(widen_kernel, out_shape=[SHAPE(out_rows.shape, LOW), SHAPE...]
    convert_element_type x4 -> x0, other arithmetic: 3.11 us -> none  [the longest x1 0.84 us: per_device_group(): gdown.astype(WIDE)]
    add x1 -> x0, other arithmetic: 3 us -> none  [per_device_group(): cotangent.astype(WIDE) + grad_rows.astype(WIDE)]
    pallas_call x1, Pallas kernels: 162 us -> 159 us  [per_device_group(): pl.pallas_call(partial(layer_kernel, ny, nz), out_shape=[SHAPE((micro, sp...]
where the time goes in v4:
time: 166 us
  Pallas kernels  164 us (99%)
    pallas_call x1, Pallas kernels, per_device_group(): pl.pallas_call(partial(layer_kernel, ny, nz), out_shape=[SHAPE((micro, sp...  159 us
    pallas_call x1, Pallas kernels, per_device_group(): pl.pallas_call(widen_kernel, out_shape=[SHAPE(out_rows.shape, LOW), SHAPE...  4.75 us

profile of v4, /device:TPU:0, one launch (start us, length us, event | category | flops | bytes accessed | tf_op | source)
XLA Modules:
  0.0 166.3 jit_solution(18311290666664773866)
XLA Ops:
  0.6 1.3 pad_maximum_fusion.norms_in
  1.9 159.4 %layer.1 = (bf16[2,256,1024]{2,1,0:T(8,128)(2,1)}, bf16[2,256,1024]{2,1,0:T(8,128)(2,1)}, bf16[32,3072]{1,0:T(8,128)(2,1)}, bf16[32,1024]{1,0:T(8,128)(2,1)}, bf...) custom-call(s32[2,4]{1,0:T(2,128)} %bitcast.14, bf16[2,256,1024]{2,1,0:T(8,128)(2,1)} %tok.1, ...), custom_call_target="tpu_custom_call" | custom-call | flops 44999999488 | bytes 20000000 | tf_op jit(solution)/shard_map/layer/pallas_call | solution.py:1630
  161.3 4.8 %widen.1 = (bf16[2,256,1024]{2,1,0:T(8,128)(2,1)}, f32[2,256,1024]{2,1,0:T(8,128)}, f32[1,32]{1,0:T(1,128)}, f32[1,32]{1,0:T(1,128)}, f32[1,32]{1,0:T(1,128)}, /...) custom-call(bf16[2,256,1024]{2,1,0:T(8,128)(2,1)} %get-tuple-element., ...), custom_call_target="tpu_custom_call" | custom-call | tf_op jit(solution)/shard_map/widen/pallas_call | solution.py:1703

commit v5 on v4

--- a/solution.py
+++ b/solution.py
@@ -736,7 +736,7 @@
 
 def layer_kernel(
     ny, nz,
-    lens, tok, cot, mix_w, out_w, up_w, down_w, norms_in, freq_in, scale_ref, dct_in, spread_in,
+    lens, tok, cot, mix_w, out_w, up_w, down_w, gain_a, bias_a, gain_f, bias_f, freq_in, scale_ref, dct_in, spread_in,
     out_rows, grad_rows, gmix_out, gout_out, gup_out, gdown_out, gains_out,
     xs, gs, nf, na, act, gp, feed, gxf, gm,
     up, down, mix, outw, small, gains, meta, table, scale, norms, freq, scale_in, dct, spread,
@@ -767,7 +767,9 @@
             local.start(weight.at[:, pl.ds(n * width, width)], raw(first + n)) for n in range(count)
         ]
 
-    norms_load = local.start(norms_in, norms)
+    norms_load = [
+        local.start(src, norms.at[k]) for k, src in enumerate((gain_a, bias_a, gain_f, bias_f))
+    ]
     mix_load = raw_load(mix_w, 0)
     up_load = raw_load(up_w, len(mix_load))
     out_mine = local.start(out_w, outw.at[y, z // 2, z % 2, c])
@@ -788,12 +790,13 @@
     for s in range(micro):
         for k in range(lens.shape[1]):
             facts = jnp.where((row == 1 + s) & (lane == k), lens[s, k].astype(WIDE), facts)
-    norms_load.wait()
+    for copy in norms_load:
+        copy.wait()
     at_row = lax.broadcasted_iota(jnp.int32, (shard, 128), 0)
     at_lane = lax.broadcasted_iota(jnp.int32, (shard, 128), 1)
     for k in range(4):
         pick = jnp.where(at_lane == at_row + k * shard, 1.0, 0.0).astype(LOW)
-        facts = jnp.where(row == 0, facts + dot_nn(norms[k : k + 1, :], pick), facts)
+        facts = jnp.where(row == 0, facts + dot_nn(norms[k], pick), facts)
     small[y, x, z, c] = facts
 
     def up_stage(q):
@@ -1165,12 +1168,12 @@
 
     out_here = outw.at[:, 1 - c, :, c]
     out_swap = links.plan(out_here, out_here, partial(place.member_id, 1))
+    landed(mix_swaps[0:3])
     landed(small_swaps)
     small_gather.begin()
     out_mine.wait()
     chunks[0].begin()
     send_tokens()
-    landed(mix_swaps[0:3])
     chunks[1].begin()
     landed(mix_swaps[3:6])
     chunks[2].begin()
@@ -1179,109 +1182,81 @@
     small_gather.late()
     landed(mix_swaps[6:9])
     chunks[0].forward()
+    make_table()
+    chunks[1].forward()
     chunks[3].begin()
-    chunks[1].forward()
     landed(up_swaps)
-    make_table()
     small_gather.finish()
     make_gains()
     make_turns()
     chunks[0].late()
     chunks[2].forward()
+    chunks[1].late()
     landed([tok_sib])
     norm(1)
-    chunks[1].late()
     chunks[3].forward()
+    norm(0)
     chunks[4].begin()
+    chunks[1].finish()
     chunks[0].finish()
+    out_swap.start()
     chunks[5].begin()
-    out_swap.start()
     chunks[2].late()
     out_swap.wait_recv()
     landed([cot_sib])
-    chunks[1].finish()
-    norm(0)
+    chunks[3].late()
+    chunks[2].finish()
+    chunks[6].begin()
     for copy in down_mine:
         copy.wait()
-    chunks[3].late()
-    chunks[2].finish()
     chunks[3].finish()
-    chunks[6].begin()
     tok_fwd = links.plan(gp.at[2], gp.at[3], partial(place.member_id, 1))
+    cot_fwd = links.plan(gs.at[2], gs.at[3], partial(place.member_id, 1))
+    grad_here = outw.at[:, c, :, 1 - c]
+    grad_swap = links.plan(grad_here, grad_here, partial(place.member_id, 1))
+    first_up, second_up = up_sums
 
     def take_tokens():
         tok_far.wait_recv()
         tok_fwd.start()
 
-    loop(
-        0, 2, attend,
-        {
-            (0, 0): lambda: turn_chunk(4),
-            (0, 1): take_tokens,
-            (0, 2): lambda: turn_chunk(5),
-            (1, 0): lambda: turn_chunk(6),
-            (1, 2): lambda: turn_chunk(7),
-        },
-    )
-    norm(2)
-    landed([tok_fwd])
-    norm(3)
-    for copy in (tok_sib, tok_far, tok_fwd):
-        copy.wait_send()
-    for i in of_up[:2]:
-        chunks[i].finish()
-    loop(0, 4 * micro, hidden(0), {})
-    turn_chunk(8)
-    cot_fwd = links.plan(gs.at[2], gs.at[3], partial(place.member_id, 1))
-
     def take_cot():
         cot_far.wait_recv()
         cot_fwd.start()
 
-    for copy in mix_swaps + up_swaps:
-        copy.wait_send()
-
-    chunks[0].drain()
-    out_swap.wait_send()
-    pl.semaphore_signal(out_free, inc=1, device_id=place.member_id(1), device_id_type=MESH_ID)
-
-    loop(
-        2, 4, attend,
-        {
-            (2, 0): lambda: turn_chunk(9),
-            (2, 1): take_cot,
-            (2, 2): lambda: turn_chunk(10),
-            (3, 0): lambda: turn_chunk(11),
-            (3, 1): cot_fwd.wait_recv,
-            (3, 2): chunks[11].late,
-        },
-    )
-    for i in of_mix:
-        chunks[i].drain()
-    outer_mix(0, blocks // 2)
-    mix_sum.begin()
-    outer_mix(blocks // 2, blocks)
-    val_sum.begin()
-    part = dot_tn(gm[:, :, :, wide_mix:].reshape(rest, group), gs[...].reshape(rest, width))
-    outw[:, c] = part.astype(LOW).reshape(ny, 2, 2, shard, width)
-    pl.semaphore_wait(out_free, 1)
-    of_sibling = outw.at[:, c, :, 1 - c]
-    grad_swap = links.start(of_sibling, of_sibling, place.member_id(1))
-    for sem, r in ((sib_free, 1), (far_free, 2)):
-        pl.semaphore_signal(sem, inc=1, device_id=place.member_id(r), device_id_type=MESH_ID)
-    for i in of_up[2:]:
-        chunks[i].finish()
-    loop(0, 4 * micro, hidden(1), {})
-    landed([grad_swap])
-    out_sum.begin()
-    val_sum.hand_on()
-    outer_down(0, blocks // 2)
-    down_sum.begin()
-    mix_sum.turn(0)
-    for i in of_down:
-        chunks[i].finish()
-    for sem in (sib_free, far_free):
-        pl.semaphore_wait(sem, 1)
+    def free_out():
+        chunks[0].drain()
+        out_swap.wait_send()
+        pl.semaphore_signal(
+            out_free, inc=1, device_id=place.member_id(1), device_id_type=MESH_ID
+        )
+
+    def outer_out():
+        part = dot_tn(gm[:, :, :, wide_mix:].reshape(rest, group), gs[...].reshape(rest, width))
+        outw[:, c] = part.astype(LOW).reshape(ny, 2, 2, shard, width)
+        pl.semaphore_wait(out_free, 1)
+        grad_swap.start()
+
+    def free_rows():
+        for sem, r in ((sib_free, 1), (far_free, 2)):
+            pl.semaphore_signal(sem, inc=1, device_id=place.member_id(r), device_id_type=MESH_ID)
+
+    def await_rows():
+        for sem in (sib_free, far_free):
+            pl.semaphore_wait(sem, 1)
+
+    def free_act():
+        for one in [place.yid()] + [place.zid(step) for step in range(1, nz)]:
+            pl.semaphore_signal(act_free, inc=1, device_id=one, device_id_type=MESH_ID)
+
+    def sum_gains():
+        gsum[...] = jnp.zeros_like(gsum)
+        for k in range(4):
+            gsum[k : k + 1, :] = jnp.sum(gacc[8 * k : 8 * k + 8, :], axis=0, keepdims=True)
+
+    def drained(ones):
+        for one in ones:
+            one.drain()
 
     def rows_copy(sem, j, r, land):
         def copy(s, kind):
@@ -1352,47 +1327,6 @@
         pump(0)
         rows_out_of(j, s)
         rows_back(j, s)
-
-    loop(
-        0, 2 * micro, back_far,
-        {
-            (0, 0): lambda: out_sum.hand_on(),
-            (1, 0): lambda: mix_sum.turn(1),
-            (2, 0): lambda: (mix_sum.turn(2), outer_down(blocks // 2, blocks)),
-            (3, 0): lambda: mix_sum.turn(3),
-        },
-    )
-    for one in [place.yid()] + [place.zid(step) for step in range(1, nz)]:
-        pl.semaphore_signal(act_free, inc=1, device_id=one, device_id_type=MESH_ID)
-    loop(
-        0, 2 * micro, back_own,
-        {
-            (0, 0): lambda: down_sum.turn(0),
-            (1, 0): lambda: (val_sum.turn(), out_sum.turn()),
-            (2, 0): lambda: (down_sum.turn(1), mix_sum.hand_on()),
-        },
-    )
-    outer_up(0, blocks // 2)
-    pl.semaphore_wait(act_free, nz)
-    first_up, second_up = up_sums
-    first_up.begin()
-    outer_up(blocks // 2, blocks)
-    loop(
-        0, 2 * micro, rows_own,
-        {
-            (0, 0): lambda: down_sum.turn(2),
-            (1, 0): lambda: down_sum.turn(3),
-            (2, 0): lambda: first_up.turn(0),
-            (3, 0): lambda: (first_up.turn(1), down_sum.hand_on()),
-        },
-    )
-    links.drain()
-    gsum[...] = jnp.zeros_like(gsum)
-    for k in range(4):
-        gsum[k : k + 1, :] = jnp.sum(gacc[8 * k : 8 * k + 8, :], axis=0, keepdims=True)
-    gain_y = links.start(gsum, gy, place.yid())
-    second_up.begin()
-    own_again = local.start(tok, xs.at[0])
 
     def finish(s, carry):
         for kind in (0, 1):
@@ -1458,25 +1392,136 @@
 
         return emit
 
+    def finish_gains():
+        totals = g3[...] + gm_sum[0] + gm_sum[1] + gm_sum[2]
+        mine = ((y * 2 + x) * nz + z) * 2 + c
+        pick_row = lax.broadcasted_iota(jnp.int32, (width, shard), 0) - mine * shard
+        pick_col = lax.broadcasted_iota(jnp.int32, (width, shard), 1)
+        gains_out[...] = lax.dot_general(
+            totals, jnp.where(pick_row == pick_col, 1.0, 0.0), (((1,), (0,)), ((), ())),
+            precision=lax.Precision.HIGHEST, preferred_element_type=WIDE,
+        )
+
+    chunks[4].forward()
+    loop(
+        0, 2, attend,
+        {
+            (0, 0): lambda: (chunks[7].begin(), chunks[5].forward()),
+            (0, 2): lambda: (chunks[4].late(), take_tokens(), chunks[8].begin()),
+            (1, 0): lambda: (chunks[5].late(), chunks[9].begin(), chunks[6].forward()),
+            (1, 1): lambda: chunks[4].finish(),
+            (1, 2): lambda: (chunks[6].late(), chunks[10].begin()),
+        },
+    )
+    norm(2)
+    landed([tok_fwd])
+    norm(3)
+    for copy in (tok_sib, tok_far, tok_fwd):
+        copy.wait_send()
+    chunks[5].finish()
+    loop(
+        0, 4 * micro, hidden(0),
+        {
+            (5, 0): lambda: chunks[7].forward(),
+        },
+    )
+    chunks[8].forward()
+    drained([chunks[i] for i in of_mix])
+    chunks[11].begin()
+    for copy in mix_swaps + up_swaps:
+        copy.wait_send()
+    free_out()
+    loop(
+        2, 4, attend,
+        {
+            (2, 0): lambda: (chunks[9].forward(), take_cot(), chunks[10].forward()),
+            (2, 2): lambda: chunks[8].late(),
+            (3, 0): lambda: (chunks[10].late(), chunks[11].forward()),
+            (3, 1): lambda: (chunks[9].late(), cot_fwd.wait_recv(), chunks[7].late()),
+            (3, 2): lambda: chunks[11].late(),
+        },
+    )
+    outer_mix(0, blocks // 2)
+    mix_sum.begin()
+    outer_mix(blocks // 2, blocks)
+    val_sum.begin()
+    outer_out()
+    chunks[6].finish()
+    free_rows()
+    chunks[7].finish()
+    loop(
+        0, 4 * micro, hidden(1),
+        {
+            (3, 0): lambda: chunks[10].finish(),
+        },
+    )
+    landed([grad_swap])
+    val_sum.hand_on()
+    outer_down(0, blocks // 2)
+    out_sum.begin()
+    down_sum.begin()
+    chunks[11].finish()
+    mix_sum.turn(0)
+    chunks[9].finish()
+    chunks[8].finish()
+    await_rows()
+    loop(
+        0, 2 * micro, back_far,
+        {
+            (1, 0): lambda: mix_sum.turn(1),
+            (2, 0): lambda: (mix_sum.turn(2), outer_down(blocks // 2, blocks), mix_sum.turn(3)),
+            (3, 0): lambda: out_sum.hand_on(),
+        },
+    )
+    free_act()
+    down_sum.turn(0)
+    out_sum.turn()
+    loop(
+        0, 2 * micro, back_own,
+        {
+            (1, 0): lambda: val_sum.turn(),
+            (2, 0): lambda: (mix_sum.hand_on(), down_sum.turn(1)),
+        },
+    )
+    outer_up(0, blocks // 2)
+    pl.semaphore_wait(act_free, nz)
+    first_up.begin()
+    outer_up(blocks // 2, blocks)
+    down_sum.turn(2)
+    down_sum.hand_on()
+    loop(
+        0, 2 * micro, rows_own,
+        {
+            (2, 0): lambda: first_up.turn(0),
+            (3, 0): lambda: first_up.turn(1),
+        },
+    )
+    links.drain()
+    sum_gains()
+    gain_y = links.start(gsum, gy, place.yid())
+    second_up.begin()
+    landed([gain_y])
+    g2[...] = gsum[...] + gy[...]
+    gain_zs = [links.start(g2, gz.at[step - 1], place.zid(step)) for step in range(1, nz)]
     first_up.turn(2)
+    own_again = local.start(tok, xs.at[0])
     mix_sum.total(keep_sum(mix_send.at[two]))
     mix_send[2] = val_sum.total().astype(LOW)
     mix_shares = share(mix_send, of_mix_share, mix_recv)
     nf[1, 1, 0:shard, :] = out_sum.total().astype(LOW)
     written = [local.start(nf.at[1, 1, pl.ds(0, shard)], gout_out)]
     first_up.turn(3)
-    landed([gain_y])
-    g2[...] = gsum[...] + gy[...]
-    gain_zs = [links.start(g2, gz.at[step - 1], place.zid(step)) for step in range(1, nz)]
-    for one in chunks + [small_gather]:
-        one.drain()
+    down_sum.turn(3)
+    drained(chunks + [small_gather])
     second_up.turn(0)
     second_up.turn(1)
     first_up.hand_on()
-    for one in (mix_sum, val_sum, out_sum):
-        one.drain()
     second_up.turn(2)
     second_up.turn(3)
+    own_again.wait()
+    lax.fori_loop(0, micro, finish, 0)
+    written.append(local.start(feed.at[0], out_rows))
+    written.append(local.start(gxf.at[0], grad_rows))
     second_up.hand_on()
     down_sum.total(keep_sum(nf.at[1, 0, pl.ds(0, feed_shard)]))
     written.append(local.start(nf.at[1, 0, pl.ds(0, feed_shard)], gdown_out))
@@ -1485,34 +1530,23 @@
     landed(gain_zs)
     g3[...] = g2[...] + sum(gz[step - 1] for step in range(1, nz))
     gain_ms = [links.start(g3, gm_sum.at[r - 1], place.member_id(r)) for r in (1, 2, 3)]
-    own_again.wait()
-    lax.fori_loop(0, micro, finish, 0)
-    rows_out = local.start(feed.at[0], out_rows)
-    grads_out = local.start(gxf.at[0], grad_rows)
+    collect(mix_shares, mix_send, of_mix_share, mix_recv, put_mix)
+    written += put_out(1, gmix_out)
     second_up.total(keep_sum(up_send.at[1]))
     up_shares.append(share(up_send.at[1], of_up_share, up_recv.at[1]))
-    collect(mix_shares, mix_send, of_mix_share, mix_recv, put_mix)
-    written += put_out(1, gmix_out)
+    drained([down_sum, first_up])
     collect(up_shares[0], up_send.at[0], of_up_share, up_recv.at[0], partial(put_up, 0))
-    down_sum.drain()
-    first_up.drain()
     landed(gain_ms)
-    totals = g3[...] + gm_sum[0] + gm_sum[1] + gm_sum[2]
-    mine = ((y * 2 + x) * nz + z) * 2 + c
-    pick_row = lax.broadcasted_iota(jnp.int32, (width, shard), 0) - mine * shard
-    pick_col = lax.broadcasted_iota(jnp.int32, (width, shard), 1)
-    gains_out[...] = lax.dot_general(
-        totals, jnp.where(pick_row == pick_col, 1.0, 0.0), (((1,), (0,)), ((), ())),
-        precision=lax.Precision.HIGHEST, preferred_element_type=WIDE,
-    )
+    finish_gains()
+    drained([mix_sum, val_sum, out_sum])
     collect(up_shares[1], up_send.at[1], of_up_share, up_recv.at[1], partial(put_up, 1))
     written += put_out(0, gup_out)
-    for copy in written + [rows_out, grads_out]:
+    for copy in written:
         copy.wait()
-    for copy in (cot_sib, cot_far, cot_fwd):
+    for copy in (cot_sib, cot_far, cot_fwd, grad_swap):
         copy.wait_send()
     links.drain()
-    second_up.drain()
+    drained(chunks + up_sums + [small_gather, down_sum, mix_sum, val_sum, out_sum])
     for kind in (0, 1):
         for s in range(micro):
             sib_copy(s, kind).wait_send()
@@ -1564,6 +1598,7 @@
     copies = Locals(loaded)
     stores = Locals(stored)
     loads, written = [], []
+    row_loads = [copies.start(rows.at[s], rows_low.at[s]) for s in range(rows.shape[0])]
     for s, h in parts:
         at = pl.ds(h * half, half)
         loads.append(
@@ -1573,7 +1608,9 @@
             )
         )
     weight_loads = [copies.start(src, low) for src, low, _, _ in weights]
-    row_loads = [copies.start(rows.at[s], rows_low.at[s]) for s in range(rows.shape[0])]
+    for s, load in enumerate(row_loads):
+        load.wait()
+        written.append(stores.start(rows_low.at[s], rows_out.at[s]))
     for k, ref in enumerate((gain_one, bias_one, gain_two, bias_two)):
         ref[...] = gains[k : k + 1, :]
     for (s, h), pair in zip(parts, loads):
@@ -1586,9 +1623,6 @@
         load.wait()
         wide[...] = low[...].astype(WIDE)
         written.append(stores.start(wide, dst))
-    for s, load in enumerate(row_loads):
-        load.wait()
-        written.append(stores.start(rows_low.at[s], rows_out.at[s]))
     for copy in written:
         copy.wait()
 
@@ -1616,7 +1650,7 @@
     group = width // 4
     hidden = feed_shard * ny * nz
     half = hidden // 2
-    norms = jnp.stack([attn_gain, attn_bias, feed_gain, feed_bias])
+    norms = [one[None] for one in (attn_gain, attn_bias, feed_gain, feed_bias)]
 
     dma = pltpu.SemaphoreType.DMA
     whole = pltpu.VMEM((4, micro, span, width), LOW)
@@ -1638,7 +1672,7 @@
             SHAPE(down_weight.shape, LOW),
             SHAPE((8, shard), WIDE),
         ],
-        in_specs=[SMEM] + [ANY] * 11,
+        in_specs=[SMEM] + [ANY] * 14,
         out_specs=[ANY] * 6 + [VMEM],
         scratch_shapes=[whole] * 9
         + [
@@ -1651,7 +1685,7 @@
             low(4, micro, 64, span),
             low(group, group),
             wide(8, group),
-            low(4, shard),
+            low(4, 1, shard),
             wide(HEAD, HEAD),
             wide(1, HEAD),
             wide(HEAD, HEAD),
@@ -1695,7 +1729,7 @@
             collective_id=0, has_side_effects=True, vmem_limit_bytes=LIMIT
         ),
     )(
-        lengths[:, 0], tokens, cotangent, mix_weight, out_weight, up_weight, down_weight, norms,
+        lengths[:, 0], tokens, cotangent, mix_weight, out_weight, up_weight, down_weight, *norms,
         feature_freq, feature_scale[None], cosine_basis(), spread_rows(),
     )
     shapes = [w.shape for w in (mix_weight, out_weight, up_weight, down_weight)]

time: 166 us -> 163 us (0.982)
  Pallas kernels: 164 us -> 162 us
    pallas_call x1, Pallas kernels: 159 us -> 158 us  [per_device_group(): pl.pallas_call(partial(layer_kernel, ny, nz), out_shape=[SHAPE((micro, sp...]
where the time goes in v5:
time: 163 us
  Pallas kernels  162 us (99%)
    pallas_call x1, Pallas kernels, per_device_group(): pl.pallas_call(partial(layer_kernel, ny, nz), out_shape=[SHAPE((micro, sp...  158 us
    pallas_call x1, Pallas kernels, per_device_group(): pl.pallas_call(widen_kernel, out_shape=[SHAPE(out_rows.shape, LOW), SHAPE...  4.71 us

profile of v5, /device:TPU:0, one launch (start us, length us, event | category | flops | bytes accessed | tf_op | source)
XLA Modules:
  0.0 163.1 jit_solution(3484592267110678165)
XLA Ops:
  0.6 157.6 %layer.1 = (bf16[2,256,1024]{2,1,0:T(8,128)(2,1)}, bf16[2,256,1024]{2,1,0:T(8,128)(2,1)}, bf16[32,3072]{1,0:T(8,128)(2,1)}, bf16[32,1024]{1,0:T(8,128)(2,1)}, bf...) custom-call(s32[2,4]{1,0:T(2,128)} %bitcast.10, bf16[2,256,1024]{2,1,0:T(8,128)(2,1)} %tok.1, ...), custom_call_target="tpu_custom_call" | custom-call | flops 44999999488 | bytes 20000000 | tf_op jit(solution)/shard_map/layer/pallas_call | solution.py:1664
  158.2 4.7 %widen.1 = (bf16[2,256,1024]{2,1,0:T(8,128)(2,1)}, f32[2,256,1024]{2,1,0:T(8,128)}, f32[1,32]{1,0:T(1,128)}, f32[1,32]{1,0:T(1,128)}, f32[1,32]{1,0:T(1,128)}, /...) custom-call(bf16[2,256,1024]{2,1,0:T(8,128)(2,1)} %get-tuple-element., ...), custom_call_target="tpu_custom_call" | custom-call | tf_op jit(solution)/shard_map/widen/pallas_call | solution.py:1737

commit v6 on v5

--- a/solution.py
+++ b/solution.py
@@ -1027,15 +1027,15 @@
         phi_query = raised_query.astype(LOW)
         phi_key = raised_key.astype(LOW)
         scores, totals = [], []
-        numer = jnp.zeros((span, group), WIDE)
         total = jnp.zeros((span, group), WIDE)
         for h in range(heads):
             score = dot_nt(jnp.where(of_head[h], phi_query, none), phi_key)
             score = jnp.where(allowed, score, 0.0)
             totals.append(jnp.sum(score, axis=1, keepdims=True))
             scores.append(score.astype(LOW))
-            numer += dot_nn(scores[h], jnp.where(of_head[h], value, none))
             total = jnp.where(of_head[h], totals[h], total)
+        values = jnp.concatenate([jnp.where(one, value, none) for one in of_head], axis=0)
+        numer = dot_nn(jnp.concatenate(scores, axis=1), values)
         att = (numer / total).astype(LOW)
         gm[j, s, :, wide_mix:] = att
         return (att, cosine, sine, allowed, raised_query, raised_key, phi_query, phi_key, value,
@@ -1048,27 +1048,27 @@
         grad_att = dot_nt(gs[j, s], outw[:, c].reshape(group, width))
         grad_numer = (grad_att / total).astype(LOW)
         product = grad_att * numer
-        grad_query = jnp.zeros((span, group), WIDE)
-        grad_key = jnp.zeros((span, group), WIDE)
-        grad_value = jnp.zeros((span, group), WIDE)
+        grad_scores, numers = [], []
         for h in range(heads):
             grad_total = -jnp.sum(jnp.where(of_head[h], product, 0.0), axis=1, keepdims=True)
             grad_total = grad_total / (totals[h] * totals[h])
-            numer_h = jnp.where(of_head[h], grad_numer, none)
-            grad_score = dot_nt(numer_h, value) + grad_total
-            grad_score = jnp.where(allowed, grad_score, 0.0).astype(LOW)
-            grad_query += dot_nn(grad_score, jnp.where(of_head[h], phi_key, none))
-            grad_key += dot_tn(grad_score, jnp.where(of_head[h], phi_query, none))
-            grad_value += dot_tn(scores[h], numer_h)
+            numers.append(jnp.where(of_head[h], grad_numer, none))
+            grad_score = dot_nt(numers[h], value) + grad_total
+            grad_scores.append(jnp.where(allowed, grad_score, 0.0).astype(LOW))
+        keys = jnp.concatenate([jnp.where(one, phi_key, none) for one in of_head], axis=0)
+        queries = jnp.concatenate([jnp.where(one, phi_query, none) for one in of_head], axis=0)
+        grad_query = dot_nn(jnp.concatenate(grad_scores, axis=1), keys)
+        grad_key = dot_tn(jnp.concatenate(grad_scores, axis=0), queries)
+        grad_value = dot_tn(jnp.concatenate(scores, axis=0), jnp.concatenate(numers, axis=0))
         back_query = turn(
             dot_nt((grad_query * raised_query).astype(LOW), table[...]), cosine, -sine
         )
         back_key = turn(dot_nt((grad_key * raised_key).astype(LOW), table[...]), cosine, -sine)
         parts = (back_query.astype(LOW), back_key.astype(LOW), grad_value.astype(LOW))
-        grad_normed = jnp.zeros((span, width), WIDE)
         for t in range(3):
             gm[j, s, :, t * group : (t + 1) * group] = parts[t]
-            grad_normed += dot_nt(parts[t], mix[t].reshape(width, group))
+        weights = jnp.concatenate([mix[t].reshape(width, group) for t in range(3)], axis=1)
+        grad_normed = dot_nt(jnp.concatenate(parts, axis=1), weights)
         gacc[0:8, :] += fold_rows(grad_normed * xs[j, s].astype(WIDE))
         gacc[8:16, :] += fold_rows(grad_normed)
         gxf[j, s] = (grad_normed * gains[0:1, :]).astype(LOW)

time: 163 us -> 160 us (0.982)
  Pallas kernels: 162 us -> 159 us
    pallas_call x1, Pallas kernels: 158 us -> 154 us  [per_device_group(): pl.pallas_call(partial(layer_kernel, ny, nz), out_shape=[SHAPE((micro, sp...]
where the time goes in v6:
time: 160 us
  Pallas kernels  159 us (99%)
    pallas_call x1, Pallas kernels, per_device_group(): pl.pallas_call(partial(layer_kernel, ny, nz), out_shape=[SHAPE((micro, sp...  154 us
    pallas_call x1, Pallas kernels, per_device_group(): pl.pallas_call(widen_kernel, out_shape=[SHAPE(out_rows.shape, LOW), SHAPE...  4.71 us

profile of v6, /device:TPU:0, one launch (start us, length us, event | category | flops | bytes accessed | tf_op | source)
XLA Modules:
  0.0 159.8 jit_solution(11307254142028137249)
XLA Ops:
  0.6 154.3 %layer.1 = (bf16[2,256,1024]{2,1,0:T(8,128)(2,1)}, bf16[2,256,1024]{2,1,0:T(8,128)(2,1)}, bf16[32,3072]{1,0:T(8,128)(2,1)}, bf16[32,1024]{1,0:T(8,128)(2,1)}, bf...) custom-call(s32[2,4]{1,0:T(2,128)} %bitcast.10, bf16[2,256,1024]{2,1,0:T(8,128)(2,1)} %tok.1, ...), custom_call_target="tpu_custom_call" | custom-call | flops 44999999488 | bytes 20000000 | tf_op jit(solution)/shard_map/layer/pallas_call | solution.py:1664
  154.9 4.7 %widen.1 = (bf16[2,256,1024]{2,1,0:T(8,128)(2,1)}, f32[2,256,1024]{2,1,0:T(8,128)}, f32[1,32]{1,0:T(1,128)}, f32[1,32]{1,0:T(1,128)}, f32[1,32]{1,0:T(1,128)}, /...) custom-call(bf16[2,256,1024]{2,1,0:T(8,128)(2,1)} %get-tuple-element., ...), custom_call_target="tpu_custom_call" | custom-call | tf_op jit(solution)/shard_map/widen/pallas_call | solution.py:1737
